TPU v7x, 256 devices: a whole 4x4x8 slice. The times are simulated.
256 devices in a mesh: wide: 16 (over y, z_hi, core), node: 16 (over z_lo, x).
Axes of the slice: x: 4, y: 4, z: 8 (z_hi: 2, z_lo: 4; z = z_hi * 4 + z_lo), core: 2. Of those that a mesh axis runs over, the one named last changes fastest.
Arguments:
- grad_codes: int32 [16, 16, 128, 9216], P('wide', 'node'), may hold values from -8 to 7
- scales: float32 [16, 16, 128, 72], P('wide', 'node'), may hold values from 0.01 to 0.2
- feedback: bfloat16 [16, 16, 128, 9216], P('wide', 'node'), may hold values from -1.1953125 to 1.1953125
- master: float32 [16, 16, 4608], P('node', 'wide'), may hold values from -0.3 to 0.3
- moment: float32 [16, 16, 4608], P('node', 'wide'), may hold values from -0.006 to 0.006
- second: float32 [16, 16, 4608], P('node', 'wide'), may hold values from 4e-06 to 0.0001
Outputs:
- adam_dir: float32 [16, 16, 4608], P('node', 'wide')
- new_master: float32 [16, 16, 4608], P('node', 'wide')
- weights_bf16: bfloat16 [128, 9216], replicated
Inputs may be any that keep to these rules, and one draw needn't show every extreme that they name: `grad_codes`: int4 codes.
All inputs are finite; a program needn't handle non-finite values.
Results may differ from a plain program's by a relative error of at most 0.018.
Values may be sent and summed in bfloat16 or wider, within the bound.
No kernel may reach another device: no remote copies, remote signals or barrier semaphores. Data moves between devices by JAX's collectives and lax.ppermute only.
A program may use at most 64 MiB of HBM per device.

v0:
```python
import jax
import jax.numpy as jnp
from jax import lax
from jax.sharding import PartitionSpec as P

beta_one = 0.9
beta_two = 0.999
adam_count = 100.0
adam_epsilon = 1e-08
learn_rate = 0.02


def shards(grad_codes, scales, feedback, master, moment, second):
    node_count = lax.axis_size("node")
    wide_count = lax.axis_size("wide")
    grad_rows = grad_codes.shape[2]
    width = grad_codes.shape[3]
    slab_len = master.shape[2]
    blocks = scales.shape[3]
    dequant = (
        grad_codes[0, 0].astype(jnp.float32).reshape(grad_rows, blocks, width // blocks)
        * scales[0, 0][..., None]
    )
    compensated = (dequant.reshape(grad_rows, width) + feedback[0, 0].astype(jnp.float32)).astype(
        jnp.bfloat16
    )
    pieces = compensated.reshape(node_count, wide_count, slab_len)
    node_sum = jnp.sum(
        lax.all_to_all(pieces, "node", split_axis=0, concat_axis=0, tiled=True).astype(jnp.float32),
        axis=0,
    ).astype(jnp.bfloat16)
    arrived = lax.all_to_all(node_sum, "wide", split_axis=0, concat_axis=0, tiled=True)
    summed = jnp.sum(arrived.astype(jnp.float32), axis=0)[None, None, :]
    grad = summed / (wide_count * node_count)
    first = beta_one * moment + (1.0 - beta_one) * grad
    squared = beta_two * second + (1.0 - beta_two) * grad * grad
    first_hat = first / (1.0 - beta_one**adam_count)
    squared_hat = squared / (1.0 - beta_two**adam_count)
    adam_dir = first_hat / (jnp.sqrt(squared_hat) + adam_epsilon)
    new_master = master - learn_rate * adam_dir
    owned = new_master.astype(jnp.bfloat16)
    by_owner = lax.all_gather(owned, "wide", axis=1, tiled=True)
    everyone = lax.all_gather(by_owner, "node", axis=0, tiled=True)
    weights_bf16 = everyone.reshape(grad_rows, width)
    return (adam_dir, new_master, weights_bf16)


def solution(mesh):
    placed = (
        P("wide", "node", None, None),
        P("wide", "node", None, None),
        P("wide", "node", None, None),
        P("node", "wide", None),
        P("node", "wide", None),
        P("node", "wide", None),
    )
    return jax.shard_map(
        shards,
        mesh=mesh,
        in_specs=placed,
        out_specs=(P("node", "wide", None), P("node", "wide", None), P()),
        check_vma=False,
    )
```

profile of v0, /device:TPU:8, one launch (start us, length us, event | category | flops | bytes accessed | tf_op | source)
XLA Modules:
  0.0 240.5 jit_solution(11132803456556693946)
XLA Ops:
  7.2 0.0 all-gather.2.cloned.1.call-start
  7.2 0.9 copy.20
  8.1 3.3 %mul.81 = f32[128,72,128]{2,1,0:T(8,128)} broadcast(f32[128,72]{1,0:T(8,128)S(1)} %copy.20), dimensions={0,1} | broadcast | bytes 4755456 | tf_op jit(solution)/shard_map/mul | solution.py:21
  11.4 5.3 %mul.82 = f32[16,16,4608]{2,1,0:T(8,128)} reshape(f32[128,72,128]{2,1,0:T(8,128)} %mul.81) | data formatting | bytes 9437184 | tf_op jit(solution)/shard_map/mul | solution.py:21
  16.7 5.0 %convert_element_type.29 = f32[1,1,128,9216]{3,2,1,0:T(8,128)} convert(s32[1,1,128,9216]{3,2,1,0:T(8,128)} %param.6) | non-fusion elementwise | flops 1179648 | bytes 9437184 | tf_op jit(solution)/shard_map/convert_element_type | solution.py:21
  21.7 0.0 copy-start
  21.7 5.5 %convert_element_type.30 = f32[16,16,4608]{2,1,0:T(8,128)} reshape(f32[1,1,128,9216]{3,2,1,0:T(8,128)} %convert_element_type.29) | data formatting | bytes 9437184 | tf_op jit(solution)/shard_map/convert_element_type | solution.py:21
  27.1 0.0 copy-done
  27.1 2.9 %reshape.57 = f32[16,16,4608]{2,1,0:T(8,128)} reshape(bf16[1,1,128,9216]{3,2,1,0:T(8,128)(2,1)S(1)} %copy-done) | data formatting | bytes 7077888 | tf_op jit(solution)/shard_map/convert_element_type | solution.py:24
  30.0 6.1 %add_convert_fusion = bf16[16,16,4608]{2,1,0:T(8,128)(2,1)S(1)} fusion(f32[16,16,4608]{2,1,0:T(8,128)} %reshape.57, f32[16,16,4608]{2,1,0:T(8,128)} %convert_element_type.30, f32[16,16,4608]{2,1,0:T(8,128)} %mul.82), kind=kLoop, calls=%fused_computation | loop fusion | flops 3538944 | bytes 16515072 | tf_op jit(solution)/shard_map/convert_element_type | solution.py:24
  36.1 0.0 copy-start.1
  36.1 0.0 copy-start.3
  36.1 0.0 copy-start.4
  36.1 63.7 %all_to_all.14 = bf16[16,16,4608]{2,1,0:T(8,128)(2,1)S(1)} all-to-all(bf16[16,16,4608]{2,1,0:T(8,128)(2,1)S(1)} %add_convert_fusion), channel_id=1, replica_groups=mesh['wide'=16,'node'=16] {'node'}, dimensions={0} | all-to-all | bytes 4718592 | tf_op jit(solution)/shard_map/all_to_all | solution.py:29
  99.8 0.3 reduce_sum.21
  100.1 0.5 broadcast.42
  100.6 0.7 reduce.2
  101.4 17.4 %all_to_all.15 = bf16[16,2,2304]{2,1,0:T(2,128)(2,1)S(1)} all-to-all(bf16[16,2,2304]{2,1,0:T(2,128)(2,1)S(1)} %reshape.58), channel_id=1, replica_groups=mesh['wide'=16,'node'=16] {'wide'}, dimensions={0} | all-to-all | bytes 294912 | tf_op jit(solution)/shard_map/all_to_all | solution.py:32
  118.8 0.1 reshape.59
  118.9 0.3 convert_reduce_fusion
  119.2 0.0 copy-done.1
  119.3 0.0 copy-done.3
  119.3 0.0 copy-done.4
  119.3 0.1 fusion.5
  119.4 0.0 copy-start.2
  119.4 25.1 %all_gather.6 = bf16[1,16,4608]{2,0,1:T(2,128)(2,1)S(1)} all-gather(bf16[1,1,4608]{2,0,1:T(2,128)(2,1)S(1)} %get-tuple-element.9), channel_id=1, replica_groups=mesh['wide'=16,'node'=16] {'wide'}, dimensions={1}, use_global_device_ids=true | all-gather | bytes 156672 | tf_op jit(solution)/shard_map/all_gather | solution.py:42
  144.5 0.7 copy.26
  145.1 0.0 all-gather.2.cloned.1.call-update
  145.2 0.6 fusion.4
  145.8 83.6 %all-gather.2.cloned.1.call-done = bf16[16,16,4608]{2,1,0:T(8,128)(2,1)} async-done(((bf16[1,16,4608]{2,1,0:T(8,128)(2,1)}), bf16[16,16,4608]{2,1,0:T(8,128)(2,1)}) %all-gather.2.cloned.1.call-update) | async-done | bytes 2359312 | tf_op jit(solution)/shard_map/all_gather | solution.py:43
  229.4 4.2 %reshape.56 = bf16[128,9216]{1,0:T(8,128)(2,1)} reshape(bf16[16,16,4608]{2,1,0:T(8,128)(2,1)} %all-gather.2.cloned.1.call-done) | data formatting | bytes 4718592 | tf_op jit(solution)/shard_map/reshape | solution.py:44
  233.6 0.0 copy-done.2
  (2 shorter events, 0.0 us)
Async XLA Ops:
  7.2 222.2 %all-gather.2.cloned.1.call-start = ((), (), s32[]{:S(2)}) async-start(), calls=%async_computation.2 | async-start | bytes 2506752 | tf_op jit(solution)/shard_map/all_gather | solution.py:43
  21.7 5.5 %copy-start = (bf16[1,1,128,9216]{3,2,1,0:T(8,128)(2,1)S(1)}, bf16[1,1,128,9216]{3,2,1,0:T(8,128)(2,1)}, u32[]{:S(2)}) copy-start(bf16[1,1,128,9216]{3,2,1,0:T(8,128)(2,1)} %param.8) | copy-start | bytes 7077892
  36.1 83.2 %copy-start.1 = (f32[1,1,4608]{2,1,0:T(1,128)S(1)}, f32[1,1,4608]{2,1,0:T(1,128)}, u32[]{:S(2)}) copy-start(f32[1,1,4608]{2,1,0:T(1,128)} %param.9) | copy-start | bytes 55300
  36.1 83.2 %copy-start.3 = (f32[1,1,4608]{2,1,0:T(1,128)S(1)}, f32[1,1,4608]{2,1,0:T(1,128)}, u32[]{:S(2)}) copy-start(f32[1,1,4608]{2,1,0:T(1,128)} %param.11) | copy-start | bytes 55300
  36.1 83.2 %copy-start.4 = (f32[1,1,4608]{2,1,0:T(1,128)S(1)}, f32[1,1,4608]{2,1,0:T(1,128)}, u32[]{:S(2)}) copy-start(f32[1,1,4608]{2,1,0:T(1,128)} %param.10) | copy-start | bytes 55300
  119.4 114.2 %copy-start.2 = (f32[1,1,4608]{2,0,1:T(1,128)}, f32[1,1,4608]{2,0,1:T(1,128)S(1)}, u32[]{:S(2)}) copy-start(f32[1,1,4608]{2,0,1:T(1,128)S(1)} %get-tuple-element.10) | copy-start | bytes 55300
Sparse Core Ops, SparseCore 0:
  145.3 84.0 all-gather.1
where the time goes:
time: 241 us; the launch traced here: 240 us
  blocking collectives  106 us (44%)
  waiting for transfers between devices  83.6 us (35%)
  local copies, waits for them, and re-layouts  23.4 us (10%)
  between operations  14.1 us (6%)
  other arithmetic  13.1 us (5%)
    all_gather x1, waiting for transfers between devices, shards(): everyone = lax.all_gather(by_owner, 'node', axis=0, tiled=True)  83.6 us
    all_to_all x1, blocking collectives, shards(): lax.all_to_all(pieces, 'node', split_axis=0, concat_axis=0, tiled=True)  63.7 us
    all_gather x1, blocking collectives, shards(): by_owner = lax.all_gather(owned, 'wide', axis=1, tiled=True)  25.1 us
    all_to_all x1, blocking collectives, shards(): lax.all_to_all(node_sum, 'wide', split_axis=0, concat_axis=0, tiled=True)  17.4 us
    mul x3, local copies, waits for them, and re-layouts, shards(): grad_codes[0, 0].astype(jnp.float32)  9.46 us
    convert_element_type x1, other arithmetic, shards(): (dequant.reshape(grad_rows, width) + feedback[0, 0].astype(jnp.float32))....  6.05 us
    convert_element_type x1, local copies, waits for them, and re-layouts, shards(): grad_codes[0, 0].astype(jnp.float32)  5.45 us
    convert_element_type x1, other arithmetic, shards(): grad_codes[0, 0].astype(jnp.float32)  5 us
  transfers between devices with their start and end apart: 1, of which 1 were waited for; matrix products, arithmetic and copies ran while one was open for 0% of the time, Pallas kernels for 0%

commit v1 on v0

v1 whole, which is shorter than its diff:
```python
import functools

import jax
import jax.numpy as jnp
from jax import lax
from jax.experimental import pallas as pl
from jax.experimental.pallas import tpu as pltpu
from jax.sharding import Mesh
from jax.sharding import PartitionSpec as P

beta_one = 0.9
beta_two = 0.999
adam_count = 100.0
adam_epsilon = 1e-08
learn_rate = 0.02

AXES = ("y", "zh", "core", "zl", "x")
SIZES = (4, 2, 2, 4, 4)
ROWS = 128
WIDTH = 9216
HALF = WIDTH // 2
LANES = 128
CHUNKS = 4
CHUNK = HALF // CHUNKS
PER_CHUNK = CHUNK // LANES
SLAB_ROWS = HALF // LANES
F32 = jnp.float32
BF16 = jnp.bfloat16
VMEM = 48 * 1024 * 1024


def params():
    return pltpu.CompilerParams(vmem_limit_bytes=VMEM)


def owner_order(transposed):
    sent = lax.broadcasted_iota(jnp.int32, (ROWS, ROWS), 1 if transposed else 0)
    flat = lax.broadcasted_iota(jnp.int32, (ROWS, ROWS), 0 if transposed else 1)
    x, y, zl, zh = sent // 32, sent // 8 % 4, sent // 2 % 4, sent % 2
    return (zl * 32 + x * 8 + y * 2 + zh == flat).astype(F32).astype(BF16)


def compensate_kernel(half_ref, codes_ref, scales_ref, feedback_ref, out_ref, turned):
    first = (half_ref[0] * CHUNKS + pl.program_id(0)) * PER_CHUNK
    turned[0:PER_CHUNK, :] = scales_ref[pl.ds(first, PER_CHUNK), :]
    scale = turned[...].T
    for block in range(PER_CHUNK):
        columns = slice(block * LANES, (block + 1) * LANES)
        dequant = codes_ref[:, columns].astype(F32) * scale[:, block : block + 1]
        out_ref[:, columns] = (dequant + feedback_ref[:, columns].astype(F32)).astype(BF16)


def compensate(half, codes, scales, feedback):
    chunk = lambda i, half: (0, half[0] * CHUNKS + i)
    return pl.pallas_call(
        compensate_kernel,
        out_shape=jax.ShapeDtypeStruct((ROWS, HALF), BF16),
        grid_spec=pltpu.PrefetchScalarGridSpec(
            num_scalar_prefetch=1,
            grid=(CHUNKS,),
            in_specs=[
                pl.BlockSpec((ROWS, CHUNK), chunk),
                pl.BlockSpec((WIDTH // LANES, ROWS), lambda i, half: (0, 0)),
                pl.BlockSpec((ROWS, CHUNK), chunk),
            ],
            out_specs=pl.BlockSpec((ROWS, CHUNK), lambda i, half: (0, i)),
            scratch_shapes=[pltpu.VMEM((ROWS, LANES), F32)],
        ),
        compiler_params=params(),
        cost_estimate=pl.CostEstimate(flops=3 * ROWS * HALF, bytes_accessed=8 * ROWS * HALF, transcendentals=0),
        name="compensate",
    )(half, codes, scales, feedback)


def pair_sum_kernel(own_ref, other_ref, out_ref):
    order = owner_order(False)
    total = (own_ref[...].astype(F32) + other_ref[...].astype(F32)).astype(BF16)
    out_ref[...] = jnp.dot(order, total, preferred_element_type=F32).astype(BF16)


def pair_sum(own, other):
    block = pl.BlockSpec((ROWS, CHUNK), lambda i: (0, i))
    return pl.pallas_call(
        pair_sum_kernel,
        out_shape=jax.ShapeDtypeStruct((ROWS, HALF), BF16),
        grid=(CHUNKS,),
        in_specs=[block, block],
        out_specs=block,
        compiler_params=params(),
        name="pair_sum",
    )(own, other)


def plane_sum_kernel(in_ref, out_ref, spread):
    total = jnp.sum(in_ref[...].astype(F32), axis=0)
    for block in range(SLAB_ROWS):
        spread[:, block, :] = total[:, block * LANES : (block + 1) * LANES]
    out_ref[...] = spread[...].astype(BF16)


def plane_sum(arrived):
    return pl.pallas_call(
        plane_sum_kernel,
        out_shape=jax.ShapeDtypeStruct((8, SLAB_ROWS, LANES), BF16),
        scratch_shapes=[pltpu.VMEM((8, SLAB_ROWS, LANES), F32)],
        compiler_params=params(),
        name="plane_sum",
    )(arrived)


def adam_kernel(arrived_ref, master_ref, moment_ref, second_ref, dir_ref, new_ref, copies_ref):
    grad = jnp.sum(arrived_ref[...].astype(F32), axis=0) / 256.0
    first = beta_one * moment_ref[...] + (1.0 - beta_one) * grad
    squared = beta_two * second_ref[...] + (1.0 - beta_two) * grad * grad
    first_hat = first / (1.0 - beta_one**adam_count)
    squared_hat = squared / (1.0 - beta_two**adam_count)
    adam_dir = first_hat / (jnp.sqrt(squared_hat) + adam_epsilon)
    new_master = master_ref[...] - learn_rate * adam_dir
    dir_ref[...] = adam_dir
    new_ref[...] = new_master
    copies_ref[...] = jnp.broadcast_to(new_master.astype(BF16)[None], copies_ref.shape)


def adam(arrived, master, moment, second):
    slab = jax.ShapeDtypeStruct((SLAB_ROWS, LANES), F32)
    return pl.pallas_call(
        adam_kernel,
        out_shape=(slab, slab, jax.ShapeDtypeStruct((8, SLAB_ROWS, LANES), BF16)),
        compiler_params=params(),
        name="adam",
    )(arrived, master, moment, second)


def line_kernel(in_ref, out_ref, spread):
    spread[...] = in_ref[...].astype(F32)
    for block in range(SLAB_ROWS):
        columns = slice(block * LANES, (block + 1) * LANES)
        rows = spread[:, block, :].astype(BF16)
        out_ref[:, :, columns] = jnp.broadcast_to(rows[None], (16, 8, LANES))


def line_copies(arrived):
    return pl.pallas_call(
        line_kernel,
        out_shape=jax.ShapeDtypeStruct((16, 8, HALF), BF16),
        scratch_shapes=[pltpu.VMEM((8, SLAB_ROWS, LANES), F32)],
        compiler_params=params(),
        name="line_copies",
    )(arrived)


def restore_kernel(core_ref, own_ref, other_ref, out_ref):
    order = owner_order(True)
    mine = (pl.program_id(0) // CHUNKS) == core_ref[0]

    @pl.when(mine)
    def _():
        out_ref[...] = jnp.dot(order, own_ref[...], preferred_element_type=F32).astype(BF16)

    @pl.when(jnp.logical_not(mine))
    def _():
        out_ref[...] = jnp.dot(order, other_ref[...], preferred_element_type=F32).astype(BF16)


def restore(core, own, other):
    return pl.pallas_call(
        restore_kernel,
        out_shape=jax.ShapeDtypeStruct((ROWS, WIDTH), BF16),
        grid_spec=pltpu.PrefetchScalarGridSpec(
            num_scalar_prefetch=1,
            grid=(2 * CHUNKS,),
            in_specs=[
                pl.BlockSpec((ROWS, CHUNK), lambda i, core: (0, i % CHUNKS)),
                pl.BlockSpec((ROWS, CHUNK), lambda i, core: (0, i % CHUNKS)),
            ],
            out_specs=pl.BlockSpec((ROWS, CHUNK), lambda i, core: (0, i)),
        ),
        compiler_params=params(),
        name="restore",
    )(core, own, other)


def shards(grad_codes, scales, feedback, master, moment, second):
    core = lax.axis_index("core").astype(jnp.int32).reshape(1)
    codes, feed = grad_codes[0, 0], feedback[0, 0]
    turned = jnp.swapaxes(scales[0, 0], 0, 1)
    swap = [(0, 1), (1, 0)]
    given = compensate(1 - core, codes, turned, feed)
    taken = lax.ppermute(given, "core", swap)
    kept = compensate(core, codes, turned, feed)
    chip = pair_sum(kept, taken).reshape(16, 8, HALF)
    plane = plane_sum(lax.all_to_all(chip, ("x", "y"), 0, 0, tiled=True))
    line = lax.all_to_all(plane, ("zl", "zh"), 0, 0, tiled=True)
    slab = lambda a: a.reshape(SLAB_ROWS, LANES)
    adam_dir, new_master, copies = adam(line, slab(master), slab(moment), slab(second))
    owned = line_copies(lax.all_to_all(copies, ("zl", "zh"), 0, 0, tiled=True))
    mine = lax.all_to_all(owned, ("x", "y"), 0, 0, tiled=True).reshape(ROWS, HALF)
    theirs = lax.ppermute(mine, "core", swap)
    weights = restore(core, mine, theirs)
    return adam_dir.reshape(1, 1, HALF), new_master.reshape(1, 1, HALF), weights


def solution(mesh):
    fine = Mesh(mesh.devices.reshape(SIZES), AXES)
    wide, node = ("y", "zh", "core"), ("zl", "x")
    placed = (
        P(wide, node, None, None),
        P(wide, node, None, None),
        P(wide, node, None, None),
        P(node, wide, None),
        P(node, wide, None),
        P(node, wide, None),
    )
    return jax.shard_map(
        shards,
        mesh=fine,
        in_specs=placed,
        out_specs=(P(node, wide, None), P(node, wide, None), P()),
        check_vma=False,
    )
```

time: 241 us -> 92.5 us (0.38)
  the two profiles are of different devices: /device:TPU:8 before, /device:TPU:1 now
where the time goes in v1:
time: 92.5 us; the launch traced here: 92.1 us
  blocking collectives  49.1 us (53%)
  starting transfers between devices  16.8 us (18%)
  Pallas kernels  13.9 us (15%)
  waiting for transfers between devices  7.69 us (8%)
  local copies, waits for them, and re-layouts  3.69 us (4%)
    all_to_all x1, blocking collectives, shards(): plane = plane_sum(lax.all_to_all(chip, ('x', 'y'), 0, 0, tiled=True))  22.8 us
    all_to_all x1, blocking collectives, shards(): lax.all_to_all(owned, ('x', 'y'), 0, 0, tiled=True).reshape(ROWS, HALF)  17.3 us
    all_to_all x1, blocking collectives, shards(): owned = line_copies(lax.all_to_all(copies, ('zl', 'zh'), 0, 0, tiled=True))  9.05 us
    all_to_all x1, starting transfers between devices, shards(): line = lax.all_to_all(plane, ('zl', 'zh'), 0, 0, tiled=True)  8.18 us
    pallas_call x2, Pallas kernels, compensate(): pl.pallas_call(compensate_kernel, out_shape=jax.ShapeDtypeStruct((ROWS, H...  6.92 us
    all_to_all x1, waiting for transfers between devices, shards(): line = lax.all_to_all(plane, ('zl', 'zh'), 0, 0, tiled=True)  6.46 us
    ppermute x1, starting transfers between devices, shards(): theirs = lax.ppermute(mine, 'core', swap)  5.33 us
    pallas_call x1, Pallas kernels, restore(): pl.pallas_call(restore_kernel, out_shape=jax.ShapeDtypeStruct((ROWS, WIDT...  4.33 us
  transfers between devices with their start and end apart: 3, of which 2 were waited for; matrix products, arithmetic and copies ran while one was open for 2% of the time, Pallas kernels for 4%

profile of v1, /device:TPU:1, one launch (start us, length us, event | category | flops | bytes accessed | tf_op | source)
XLA Modules:
  0.0 92.1 jit_solution(8438249872680309687)
XLA Ops:
  0.6 0.0 copy-start
  0.6 1.7 %copy-done = bf16[1,1,128,9216]{3,2,1,0:T(8,128)(2,1)S(1)} copy-done((bf16[1,1,128,9216]{3,2,1,0:T(8,128)(2,1)S(1)}, bf16[1,1,128,9216]{3,2,1,0:T(8,128)(2,1)}, u32[]{:S(2)}) %copy-start) | copy-done | bytes 2359320
  2.3 0.0 copy-start.2
  2.3 0.8 copy-done.2
  3.1 0.0 copy-start.1
  3.1 0.0 copy-start.3
  3.1 3.5 %compensate.3 = bf16[128,4608]{1,0:T(8,128)(2,1)S(1)} custom-call(s32[1]{0:T(128)S(6)} %sub.3.half_ref, s32[128,9216]{1,0:T(8,128)} %bitcast.21, f32[72,128]{1,0:T(8,128)S(1)} %bitcast.16, bf16[128,9216]{1,0:T(8,128)(2,1)S(1)} %bitcast.11), custom_call_target="tpu_custom_call" | custom-call | flops 1769472 | bytes 4718592 | tf_op jit(solution)/shard_map/compensate/pallas_call | solution.py:55
  6.6 3.3 %collective-permute-start = (bf16[128,4608]{1,0:T(8,128)(2,1)S(1)}, bf16[128,4608]{1,0:T(8,128)(2,1)S(1)}, u32[]{:S(2)}, u32[]{:S(2)}) collective-permute-start(bf16[128,4608]{1,0:T(8,128)(2,1)S(1)} %compensate.3), channel_id=1, source_target_pairs={{0,16},{16,0},{1,17},{17,1},{2,18},{18,2},{3,19},{19,3},{4,20},{20... | collective-permute-start | bytes 3538952 | tf_op jit(solution)/shard_map/ppermute | solution.py:189
  9.9 0.0 copy-done.1
  9.9 0.0 copy-done.3
  10.0 3.4 %compensate.2.own_ref = bf16[128,4608]{1,0:T(8,128)(2,1)S(1)} custom-call(s32[1]{0:T(128)} %bitcast.half_ref.core_ref, s32[128,9216]{1,0:T(8,128)} %bitcast.22, f32[72,128]{1,0:T(8,128)S(1)} %bitcast.17, bf16[128,9216]{1,0:T(8,128)(2,1)S(1)} %bitcast.12), custom_call_target="tpu_custom_call" | custom-call | flops 1769472 | bytes 4718592 | tf_op jit(solution)/shard_map/compensate/pallas_call | solution.py:55
  13.3 0.0 collective-permute-done.other_ref
  13.4 1.4 %pair_sum.1 = bf16[128,4608]{1,0:T(8,128)(2,1)S(1)} custom-call(bf16[128,4608]{1,0:T(8,128)(2,1)S(1)} %compensate.2.own_ref, bf16[128,4608]{1,0:T(8,128)(2,1)S(1)} %collective-permute-done.other_ref), custom_call_target="tpu_custom_call" | custom-call | tf_op jit(solution)/shard_map/pair_sum/pallas_call | solution.py:83
  14.8 22.8 %all_to_all.20.in_ref = bf16[16,8,4608]{2,1,0:T(8,128)(2,1)S(1)} all-to-all(bf16[16,8,4608]{2,1,0:T(8,128)(2,1)S(1)} %bitcast.15), channel_id=1, replica_groups=mesh['y'=4,'zh'=2,'core'=2,'zl'=4,'x'=4] {'x','y'}, dimensions={0} | all-to-all | bytes 2359296 | tf_op jit(solution)/shard_map/all_to_all | solution.py:192
  37.6 0.0 copy-start.4
  37.6 0.0 copy-start.5
  37.6 0.0 copy-start.6
  37.6 0.9 %plane_sum.1 = bf16[8,36,128]{2,1,0:T(8,128)(2,1)} custom-call(bf16[16,8,4608]{2,1,0:T(8,128)(2,1)S(1)} %all_to_all.20.in_ref), custom_call_target="tpu_custom_call" | custom-call | tf_op jit(solution)/shard_map/plane_sum/pallas_call | solution.py:102
  38.5 8.2 %all-to-all-start.1 = ((bf16[8,36,128]{2,1,0:T(8,128)(2,1)}), bf16[8,36,128]{2,1,0:T(8,128)(2,1)S(1)}, u32[]{:S(2)}, u32[]{:S(2)}) async-start(bf16[8,36,128]{2,1,0:T(8,128)(2,1)} %plane_sum.1), calls=%async_computation.1 | async-start | bytes 163840 | tf_op jit(solution)/shard_map/all_to_all | solution.py:193
  46.7 0.0 copy-done.4
  46.7 0.0 copy-done.5
  46.8 0.0 copy-done.6
  46.9 6.5 %all-to-all-done.1.arrived_ref = bf16[8,36,128]{2,1,0:T(8,128)(2,1)S(1)} async-done(((bf16[8,36,128]{2,1,0:T(8,128)(2,1)}), bf16[8,36,128]{2,1,0:T(8,128)(2,1)S(1)}, u32[]{:S(2)}, u32[]{:S(2)}) %all-to-all-start.1) | async-done | bytes 73760 | tf_op jit(solution)/shard_map/all_to_all | solution.py:193
  53.4 9.0 %all_to_all.21.in_ref = bf16[8,36,128]{2,1,0:T(8,128)(2,1)S(1)} all-to-all(bf16[8,36,128]{2,1,0:T(8,128)(2,1)S(1)} %get-tuple-element.8), channel_id=1, replica_groups=mesh['y'=4,'zh'=2,'core'=2,'zl'=4,'x'=4] {'zl','zh'}, dimensions={0} | all-to-all | bytes 147456 | tf_op jit(solution)/shard_map/all_to_all | solution.py:196
  62.4 0.2 line_copies.1
  62.6 17.3 %all_to_all.22 = bf16[16,8,4608]{2,1,0:T(8,128)(2,1)S(1)} all-to-all(bf16[16,8,4608]{2,1,0:T(8,128)(2,1)S(1)} %line_copies.1), channel_id=1, replica_groups=mesh['y'=4,'zh'=2,'core'=2,'zl'=4,'x'=4] {'x','y'}, dimensions={0} | all-to-all | bytes 2359296 | tf_op jit(solution)/shard_map/all_to_all | solution.py:197
  79.9 5.3 %collective-permute-start.1 = (bf16[128,4608]{1,0:T(8,128)(2,1)S(1)}, bf16[128,4608]{1,0:T(8,128)(2,1)S(1)}, u32[]{:S(2)}, u32[]{:S(2)}) collective-permute-start(bf16[128,4608]{1,0:T(8,128)(2,1)S(1)} %bitcast.13), channel_id=1, source_target_pairs={{0,16},{16,0},{1,17},{17,1},{2,18},{18,2},{3,19},{19,3},{4,20},{20... | collective-permute-start | bytes 3538952 | tf_op jit(solution)/shard_map/ppermute | solution.py:198
  85.3 0.6 reshape.35
  85.9 0.6 reshape.36
  86.5 1.2 %collective-permute-done.1.other_ref = bf16[128,4608]{1,0:T(8,128)(2,1)S(1)} collective-permute-done((bf16[128,4608]{1,0:T(8,128)(2,1)S(1)}, bf16[128,4608]{1,0:T(8,128)(2,1)S(1)}, u32[]{:S(2)}, u32[]{:S(2)}) %collective-permute-start.1) | collective-permute-done | bytes 1179680 | tf_op jit(solution)/shard_map/ppermute | solution.py:198
  87.8 4.3 %restore.1 = bf16[128,9216]{1,0:T(8,128)(2,1)} custom-call(s32[1]{0:T(128)} %bitcast.half_ref.core_ref, bf16[128,4608]{1,0:T(8,128)(2,1)S(1)} %bitcast.14, bf16[128,4608]{1,0:T(8,128)(2,1)S(1)} %collective-permute-done.1.other_ref), custom_call_target="tpu_custom_call" | custom-call | tf_op jit(solution)/shard_map/restore/pallas_call | solution.py:166
  (4 shorter events, 0.2 us)
Async XLA Ops:
  0.6 1.7 %copy-start = (bf16[1,1,128,9216]{3,2,1,0:T(8,128)(2,1)S(1)}, bf16[1,1,128,9216]{3,2,1,0:T(8,128)(2,1)}, u32[]{:S(2)}) copy-start(bf16[1,1,128,9216]{3,2,1,0:T(8,128)(2,1)} %param.8) | copy-start | bytes 7077892
  2.3 0.8 copy-start.2
  3.1 6.9 %copy-start.1 = (bf16[1,1,128,9216]{3,2,1,0:T(8,128)(2,1)S(1)}, bf16[1,1,128,9216]{3,2,1,0:T(8,128)(2,1)}, u32[]{:S(2)}) copy-start(bf16[1,1,128,9216]{3,2,1,0:T(8,128)(2,1)} %param.8) | copy-start | bytes 7077892
  3.1 6.9 %copy-start.3 = (f32[1,1,128,72]{2,3,1,0:T(8,128)S(1)}, f32[1,1,128,72]{2,3,1,0:T(8,128)}, u32[]{:S(2)}) copy-start(f32[1,1,128,72]{2,3,1,0:T(8,128)} %param.7) | copy-start | bytes 110596
  6.6 6.7 %collective-permute-start = (bf16[128,4608]{1,0:T(8,128)(2,1)S(1)}, bf16[128,4608]{1,0:T(8,128)(2,1)S(1)}, u32[]{:S(2)}, u32[]{:S(2)}) collective-permute-start(bf16[128,4608]{1,0:T(8,128)(2,1)S(1)} %compensate.3), channel_id=1, source_target_pairs={{0,16},{16,0},{1,17},{17,1},{2,18},{18,2},{3,19},{19,3},{4,20},{20... | collective-permute-start | bytes 3538952 | tf_op jit(solution)/shard_map/ppermute | solution.py:189
  37.6 9.1 %copy-start.4 = (f32[1,1,4608]{2,1,0:T(1,128)S(1)}, f32[1,1,4608]{2,1,0:T(1,128)}, u32[]{:S(2)}) copy-start(f32[1,1,4608]{2,1,0:T(1,128)} %param.9) | copy-start | bytes 55300
  37.6 9.2 %copy-start.5 = (f32[1,1,4608]{2,1,0:T(1,128)S(1)}, f32[1,1,4608]{2,1,0:T(1,128)}, u32[]{:S(2)}) copy-start(f32[1,1,4608]{2,1,0:T(1,128)} %param.10) | copy-start | bytes 55300
  37.6 9.3 %copy-start.6 = (f32[1,1,4608]{2,1,0:T(1,128)S(1)}, f32[1,1,4608]{2,1,0:T(1,128)}, u32[]{:S(2)}) copy-start(f32[1,1,4608]{2,1,0:T(1,128)} %param.11) | copy-start | bytes 55300
  38.5 14.8 %all-to-all-start.1 = ((bf16[8,36,128]{2,1,0:T(8,128)(2,1)}), bf16[8,36,128]{2,1,0:T(8,128)(2,1)S(1)}, u32[]{:S(2)}, u32[]{:S(2)}) async-start(bf16[8,36,128]{2,1,0:T(8,128)(2,1)} %plane_sum.1), calls=%async_computation.1 | async-start | bytes 163840 | tf_op jit(solution)/shard_map/all_to_all | solution.py:193
  79.9 7.8 %collective-permute-start.1 = (bf16[128,4608]{1,0:T(8,128)(2,1)S(1)}, bf16[128,4608]{1,0:T(8,128)(2,1)S(1)}, u32[]{:S(2)}, u32[]{:S(2)}) collective-permute-start(bf16[128,4608]{1,0:T(8,128)(2,1)S(1)} %bitcast.13), channel_id=1, source_target_pairs={{0,16},{16,0},{1,17},{17,1},{2,18},{18,2},{3,19},{19,3},{4,20},{20... | collective-permute-start | bytes 3538952 | tf_op jit(solution)/shard_map/ppermute | solution.py:198

commit v2 on v1

v2 whole, which is shorter than its diff:
```python
import functools

import jax
import jax.numpy as jnp
from jax import lax
from jax.experimental import pallas as pl
from jax.experimental.pallas import tpu as pltpu
from jax.sharding import Mesh
from jax.sharding import PartitionSpec as P

beta_one = 0.9
beta_two = 0.999
adam_count = 100.0
adam_epsilon = 1e-08
learn_rate = 0.02

AXES = ("y", "zh", "core", "zl", "x")
SIZES = (4, 2, 2, 4, 4)
ROWS = 128
WIDTH = 9216
HALF = WIDTH // 2
LANES = 128
CHUNKS = 4
CHUNK = HALF // CHUNKS
PER_CHUNK = CHUNK // LANES
SLAB_ROWS = HALF // LANES
F32 = jnp.float32
BF16 = jnp.bfloat16
VMEM_LIMIT = 32 * 1024 * 1024
WHOLE = pl.BlockSpec(memory_space=pltpu.VMEM)
SCALAR = pl.BlockSpec(memory_space=pltpu.SMEM)
FAR = pl.BlockSpec(memory_space=pltpu.HBM)


def params():
    return pltpu.CompilerParams(vmem_limit_bytes=VMEM_LIMIT)


def in_hbm(array):
    return pltpu.with_memory_space_constraint(array, pltpu.HBM)


def shifted(stage, step):
    pairs = []
    for y in range(4):
        for zh in range(2):
            for core in range(2):
                for zl in range(4):
                    for x in range(4):
                        flat = lambda y, x: (((y * 2 + zh) * 2 + core) * 4 + zl) * 4 + x
                        along_x = core == stage
                        to = flat(y, (x + step) % 4) if along_x else flat((y + step) % 4, x)
                        pairs.append((flat(y, x), to))
    return pairs


SWAP = [(i, i ^ 16) for i in range(256)]


def send(array, stage, step):
    return lax.ppermute(array, AXES, shifted(stage, step))


def swap_cores(array):
    return lax.ppermute(array, AXES, SWAP)


def order(place, half, transposed):
    x0, y0 = place % 4, place // 64
    sent = lax.broadcasted_iota(jnp.int32, (ROWS, ROWS), 1 if transposed else 0)
    flat = lax.broadcasted_iota(jnp.int32, (ROWS, ROWS), 0 if transposed else 1)
    a0, a_step = jnp.where(half == 0, x0, y0), jnp.where(half == 0, 8, 2)
    b0, b_step = jnp.where(half == 0, y0, x0), jnp.where(half == 0, 2, 8)
    a, b = (sent // 32 + a0) % 4, (sent // 8 % 4 + b0) % 4
    return (sent // 2 % 4 * 32 + a * a_step + b * b_step + sent % 2 == flat).astype(F32).astype(BF16)


def compensate_kernel(other, place_ref, codes_hbm, scales_hbm, feedback_hbm, out_ref, codes, scales, feedback, turned, sems):
    core = place_ref[0] // 16 % 2
    half = 1 - core if other else core
    copies = [pltpu.make_async_copy(scales_hbm, scales, sems.at[2 * CHUNKS])]
    for i in range(CHUNKS):
        columns = pl.ds(pl.multiple_of(half * HALF + i * CHUNK, LANES), CHUNK)
        copies.append(pltpu.make_async_copy(codes_hbm.at[:, columns], codes.at[i], sems.at[2 * i]))
        copies.append(pltpu.make_async_copy(feedback_hbm.at[:, columns], feedback.at[i], sems.at[2 * i + 1]))
    for copy in copies:
        copy.start()
    moved = order(place_ref[0], half, False)
    copies[0].wait()
    turned[0:SLAB_ROWS, :] = scales[pl.ds(half * SLAB_ROWS, SLAB_ROWS), :]
    scale = turned[...].T
    for i in range(CHUNKS):
        copies[1 + 2 * i].wait()
        copies[2 + 2 * i].wait()
        for block in range(PER_CHUNK):
            columns = slice(block * LANES, (block + 1) * LANES)
            at = i * PER_CHUNK + block
            dequant = codes[i, :, columns].astype(F32) * scale[:, at : at + 1]
            compensated = (dequant + feedback[i, :, columns].astype(F32)).astype(BF16)
            out_ref[:, at * LANES : (at + 1) * LANES] = jnp.dot(moved, compensated, preferred_element_type=F32).astype(BF16)


def compensate(other, place, codes, scales, feedback):
    return pl.pallas_call(
        functools.partial(compensate_kernel, other),
        out_shape=jax.ShapeDtypeStruct((ROWS, HALF), BF16),
        in_specs=[SCALAR, FAR, FAR, FAR],
        out_specs=WHOLE,
        scratch_shapes=[
            pltpu.VMEM((CHUNKS, ROWS, CHUNK), jnp.int32),
            pltpu.VMEM((WIDTH // LANES, ROWS), F32),
            pltpu.VMEM((CHUNKS, ROWS, CHUNK), BF16),
            pltpu.VMEM((ROWS, LANES), F32),
            pltpu.SemaphoreType.DMA((2 * CHUNKS + 1,)),
        ],
        compiler_params=params(),
        cost_estimate=pl.CostEstimate(flops=2 * ROWS * ROWS * HALF, bytes_accessed=8 * ROWS * HALF, transcendentals=0),
        name="compensate",
    )(place, in_hbm(codes), in_hbm(scales), in_hbm(feedback))


def pair_sum_kernel(own_ref, other_ref, *out_refs):
    for piece, out_ref in enumerate(out_refs):
        rows = slice(piece * 32, (piece + 1) * 32)
        out_ref[...] = (own_ref[rows, :].astype(F32) + other_ref[rows, :].astype(F32)).astype(BF16)


def pair_sum(own, other):
    return pl.pallas_call(
        pair_sum_kernel,
        out_shape=[jax.ShapeDtypeStruct((32, HALF), BF16)] * 4,
        in_specs=[WHOLE] * 2,
        out_specs=[WHOLE] * 4,
        compiler_params=params(),
        name="pair_sum",
    )(own, other)


def total_of(refs, rows):
    first, *others = [ref[rows, :].astype(F32) for ref in refs]
    return functools.reduce(lambda a, b: a + b, others, first)


def first_sum_kernel(a_ref, b_ref, c_ref, d_ref, *out_refs):
    for piece, out_ref in enumerate(out_refs):
        out_ref[...] = total_of((a_ref, b_ref, c_ref, d_ref), slice(piece * 8, (piece + 1) * 8)).astype(BF16)


def first_sum(parts):
    return pl.pallas_call(
        first_sum_kernel,
        out_shape=[jax.ShapeDtypeStruct((8, HALF), BF16)] * 4,
        in_specs=[WHOLE] * 4,
        out_specs=[WHOLE] * 4,
        compiler_params=params(),
        name="first_sum",
    )(*parts)


def second_sum_kernel(a_ref, b_ref, c_ref, d_ref, out_ref, spread):
    total = total_of((a_ref, b_ref, c_ref, d_ref), slice(None))
    for block in range(SLAB_ROWS):
        spread[:, block, :] = total[:, block * LANES : (block + 1) * LANES]
    out_ref[...] = spread[...].astype(BF16)


def second_sum(parts):
    return pl.pallas_call(
        second_sum_kernel,
        out_shape=jax.ShapeDtypeStruct((8, SLAB_ROWS, LANES), BF16),
        in_specs=[WHOLE] * 4,
        out_specs=WHOLE,
        scratch_shapes=[pltpu.VMEM((8, SLAB_ROWS, LANES), F32)],
        compiler_params=params(),
        name="second_sum",
    )(*parts)


def adam_kernel(arrived_ref, master_ref, moment_ref, second_ref, dir_ref, new_ref, copies_ref):
    grad = jnp.sum(arrived_ref[...].astype(F32), axis=0) / 256.0
    first = beta_one * moment_ref[...] + (1.0 - beta_one) * grad
    squared = beta_two * second_ref[...] + (1.0 - beta_two) * grad * grad
    first_hat = first / (1.0 - beta_one**adam_count)
    squared_hat = squared / (1.0 - beta_two**adam_count)
    adam_dir = first_hat / (jnp.sqrt(squared_hat) + adam_epsilon)
    new_master = master_ref[...] - learn_rate * adam_dir
    dir_ref[...] = adam_dir
    new_ref[...] = new_master
    copies_ref[...] = jnp.broadcast_to(new_master.astype(BF16)[None], copies_ref.shape)


def adam(arrived, master, moment, second):
    slab = jax.ShapeDtypeStruct((SLAB_ROWS, LANES), F32)
    return pl.pallas_call(
        adam_kernel,
        out_shape=(slab, slab, jax.ShapeDtypeStruct((8, SLAB_ROWS, LANES), BF16)),
        in_specs=[WHOLE] * 4,
        out_specs=[WHOLE] * 3,
        compiler_params=params(),
        name="adam",
    )(arrived, master, moment, second)


def line_kernel(in_ref, out_ref, spread):
    spread[...] = in_ref[...].astype(F32)
    for block in range(SLAB_ROWS):
        out_ref[:, block * LANES : (block + 1) * LANES] = spread[:, block, :].astype(BF16)


def line_rows(arrived):
    return pl.pallas_call(
        line_kernel,
        out_shape=jax.ShapeDtypeStruct((8, HALF), BF16),
        in_specs=[WHOLE],
        out_specs=WHOLE,
        scratch_shapes=[pltpu.VMEM((8, SLAB_ROWS, LANES), F32)],
        compiler_params=params(),
        name="line_rows",
    )(arrived)


def join_kernel(a_ref, b_ref, c_ref, d_ref, out_ref):
    for piece, ref in enumerate((a_ref, b_ref, c_ref, d_ref)):
        out_ref[piece * 8 : (piece + 1) * 8, :] = ref[...]


def join(parts):
    return pl.pallas_call(
        join_kernel,
        out_shape=jax.ShapeDtypeStruct((32, HALF), BF16),
        in_specs=[WHOLE] * 4,
        out_specs=WHOLE,
        compiler_params=params(),
        name="join",
    )(*parts)


def restore_kernel(other, place_ref, a_ref, b_ref, c_ref, d_ref, *refs):
    out_hbm, staged, sems = refs[-3:]
    core = place_ref[0] // 16 % 2
    half = 1 - core if other else core
    moved = order(place_ref[0], half, True)
    copies = []
    for i in range(CHUNKS):
        columns = slice(i * CHUNK, (i + 1) * CHUNK)
        rows = jnp.concatenate([ref[:, columns] for ref in (a_ref, b_ref, c_ref, d_ref)], axis=0)
        staged[i] = jnp.dot(moved, rows, preferred_element_type=F32).astype(BF16)
        to = pl.ds(pl.multiple_of(half * HALF + i * CHUNK, LANES), CHUNK)
        copies.append(pltpu.make_async_copy(staged.at[i], out_hbm.at[:, to], sems.at[i]))
        copies[-1].start()
    for copy in copies:
        copy.wait()


def restore(other, place, parts, held=()):
    return pl.pallas_call(
        functools.partial(restore_kernel, other),
        out_shape=jax.ShapeDtypeStruct((ROWS, WIDTH), BF16),
        in_specs=[SCALAR] + [WHOLE] * 4 + [FAR] * len(held),
        out_specs=FAR,
        scratch_shapes=[pltpu.VMEM((CHUNKS, ROWS, CHUNK), BF16), pltpu.SemaphoreType.DMA((CHUNKS,))],
        input_output_aliases={5: 0} if held else {},
        compiler_params=params(),
        name="restore",
    )(place, *parts, *held)


def shards(grad_codes, scales, feedback, master, moment, second):
    place = lax.axis_index(AXES).astype(jnp.int32).reshape(1)
    codes, feed = grad_codes[0, 0], feedback[0, 0]
    turned = jnp.swapaxes(scales[0, 0], 0, 1)
    given = compensate(True, place, codes, turned, feed)
    taken = swap_cores(given)
    kept = compensate(False, place, codes, turned, feed)
    first = pair_sum(kept, taken)
    second_parts = first_sum([first[0]] + [send(first[step], 0, step) for step in (1, 2, 3)])
    plane = second_sum([second_parts[0]] + [send(second_parts[step], 1, step) for step in (1, 2, 3)])
    line = lax.all_to_all(plane, ("zl", "zh"), 0, 0, tiled=True)
    slab = lambda a: a.reshape(SLAB_ROWS, LANES)
    adam_dir, new_master, copies = adam(line, slab(master), slab(moment), slab(second))
    owned = line_rows(lax.all_to_all(copies, ("zl", "zh"), 0, 0, tiled=True))
    joined = join([owned] + [send(owned, 1, 4 - place_of) for place_of in (1, 2, 3)])
    mine = [joined] + [send(joined, 0, 4 - place_of) for place_of in (1, 2, 3)]
    theirs = [swap_cores(part) for part in mine]
    half = restore(False, place, mine)
    weights = restore(True, place, theirs, (half,))
    return adam_dir.reshape(1, 1, HALF), new_master.reshape(1, 1, HALF), weights


def solution(mesh):
    fine = Mesh(mesh.devices.reshape(SIZES), AXES)
    wide, node = ("y", "zh", "core"), ("zl", "x")
    placed = (
        P(wide, node, None, None),
        P(wide, node, None, None),
        P(wide, node, None, None),
        P(node, wide, None),
        P(node, wide, None),
        P(node, wide, None),
    )
    return jax.shard_map(
        shards,
        mesh=fine,
        in_specs=placed,
        out_specs=(P(node, wide, None), P(node, wide, None), P()),
        check_vma=False,
    )
```

time: 92.5 us -> 84 us (0.908)
  blocking collectives: 49.1 us -> 9.05 us
  starting transfers between devices: 16.8 us -> 42.4 us
  waiting for transfers between devices: 7.69 us -> 19.6 us
  Pallas kernels: 13.9 us -> 10.1 us
  local copies, waits for them, and re-layouts: 3.69 us -> 1.27 us
    all_to_all x3 -> x1, blocking collectives: 49.1 us -> 9.05 us  [shards(): owned = line_rows(lax.all_to_all(copies, ('zl', 'zh'), 0, 0, tiled=True))]
    ppermute x2 -> x17, starting transfers between devices: 8.66 us -> 34.5 us  [the longest x5 19.3 us: swap_cores(): return lax.ppermute(array, AXES, SWAP)]
    ppermute x2 -> x17, waiting for transfers between devices: 1.23 us -> 13.1 us  [the longest x12 13.1 us: send(): return lax.ppermute(array, AXES, shifted(stage, step))]
    pallas_call x6 -> x9, Pallas kernels: 13.8 us -> 10 us  [the longest x2 6.06 us: compensate(): pl.pallas_call(functools.partial(compensate_kernel, other), out_shape=jax...]
    unnamed x14 -> x6, local copies, waits for them, and re-layouts: 2.44 us -> 0.02 us
  transfers between devices with their start and end apart: 3 -> 18, of which waited for: 2 -> 8; matrix products, arithmetic and copies ran while one was open for 2% -> 2% of each run, Pallas kernels for 4% -> 5%
where the time goes in v2:
time: 84 us; the launch traced here: 83.4 us
  starting transfers between devices  42.4 us (50%)
  waiting for transfers between devices  19.6 us (23%)
  Pallas kernels  10.1 us (12%)
  blocking collectives  9.05 us (11%)
  local copies, waits for them, and re-layouts  1.27 us (2%)
  between operations  0.98 us (1%)
    ppermute x5, starting transfers between devices, swap_cores(): return lax.ppermute(array, AXES, SWAP)  19.3 us
    ppermute x12, starting transfers between devices, send(): return lax.ppermute(array, AXES, shifted(stage, step))  15.3 us
    ppermute x12, waiting for transfers between devices, send(): return lax.ppermute(array, AXES, shifted(stage, step))  13.1 us
    all_to_all x1, blocking collectives, shards(): owned = line_rows(lax.all_to_all(copies, ('zl', 'zh'), 0, 0, tiled=True))  9.05 us
    all_to_all x1, starting transfers between devices, shards(): line = lax.all_to_all(plane, ('zl', 'zh'), 0, 0, tiled=True)  7.86 us
    all_to_all x1, waiting for transfers between devices, shards(): line = lax.all_to_all(plane, ('zl', 'zh'), 0, 0, tiled=True)  6.46 us
    pallas_call x2, Pallas kernels, compensate(): pl.pallas_call(functools.partial(compensate_kernel, other), out_shape=jax...  6.06 us
    pallas_call x2, Pallas kernels, restore(): pl.pallas_call(functools.partial(restore_kernel, other), out_shape=jax.Sh...  2.57 us
  transfers between devices with their start and end apart: 18, of which 8 were waited for; matrix products, arithmetic and copies ran while one was open for 2% of the time, Pallas kernels for 5%

profile of v2, /device:TPU:1, one launch (start us, length us, event | category | flops | bytes accessed | tf_op | source)
XLA Modules:
  0.0 83.4 jit_solution(5654031863171338948)
XLA Ops:
  0.6 3.0 %compensate.3 = bf16[128,4608]{1,0:T(8,128)(2,1)S(1)} custom-call(s32[1]{0:T(128)} %bitcast.place_ref, s32[128,9216]{1,0:T(8,128)} %bitcast.12, f32[72,128]{1,0:T(8,128)} %bitcast.16, bf16[128,9216]{1,0:T(8,128)(2,1)} %bitcast.14), custom_call_target="tpu_custom_call" | custom-call | flops 150994944 | bytes 4718592 | tf_op jit(solution)/shard_map/compensate/pallas_call | solution.py:104
  3.7 3.3 %collective-permute-start = (bf16[128,4608]{1,0:T(8,128)(2,1)S(1)}, bf16[128,4608]{1,0:T(8,128)(2,1)S(1)}, u32[]{:S(2)}, u32[]{:S(2)}) collective-permute-start(bf16[128,4608]{1,0:T(8,128)(2,1)S(1)} %compensate.3), channel_id=1, source_target_pairs={{0,16},{1,17},{2,18},{3,19},{4,20},{5,21},{6,22},{7,23},{8,24},{9,... | collective-permute-start | bytes 3538952 | tf_op jit(solution)/shard_map/ppermute | solution.py:65
  7.0 3.0 %compensate.2.own_ref = bf16[128,4608]{1,0:T(8,128)(2,1)S(1)} custom-call(s32[1]{0:T(128)} %bitcast.place_ref, s32[128,9216]{1,0:T(8,128)} %bitcast.13, f32[72,128]{1,0:T(8,128)} %bitcast.17, bf16[128,9216]{1,0:T(8,128)(2,1)} %bitcast.15), custom_call_target="tpu_custom_call" | custom-call | flops 150994944 | bytes 4718592 | tf_op jit(solution)/shard_map/compensate/pallas_call | solution.py:104
  10.0 0.0 copy-start
  10.1 0.0 copy-start.1
  10.1 0.0 copy-start.2
  10.1 0.0 collective-permute-done.other_ref
  10.1 0.3 pair_sum.1
  10.4 0.1 collective-permute-start.1
  10.5 2.2 %collective-permute-start.2 = (bf16[32,4608]{1,0:T(8,128)(2,1)S(1)}, bf16[32,4608]{1,0:T(8,128)(2,1)S(1)}, u32[]{:S(2)}, u32[]{:S(2)}) collective-permute-start(bf16[32,4608]{1,0:T(8,128)(2,1)S(1)} %get-tuple-element.16), channel_id=1, source_target_pairs={{0,2},{1,3},{2,0},{3,1},{4,6},{5,7},{6,4},{7,5},{8,10},{9,11},{10,... | collective-permute-start | bytes 884744 | tf_op jit(solution)/shard_map/ppermute | solution.py:61
  12.6 1.1 %collective-permute-start.3 = (bf16[32,4608]{1,0:T(8,128)(2,1)S(1)}, bf16[32,4608]{1,0:T(8,128)(2,1)S(1)}, u32[]{:S(2)}, u32[]{:S(2)}) collective-permute-start(bf16[32,4608]{1,0:T(8,128)(2,1)S(1)} %get-tuple-element.17), channel_id=1, source_target_pairs={{0,3},{1,0},{2,1},{3,2},{4,7},{5,4},{6,5},{7,6},{8,11},{9,8},{10,9... | collective-permute-start | bytes 884744 | tf_op jit(solution)/shard_map/ppermute | solution.py:61
  13.7 7.0 %collective-permute-done.1.b_ref = bf16[32,4608]{1,0:T(8,128)(2,1)S(1)} collective-permute-done((bf16[32,4608]{1,0:T(8,128)(2,1)S(1)}, bf16[32,4608]{1,0:T(8,128)(2,1)S(1)}, u32[]{:S(2)}, u32[]{:S(2)}) %collective-permute-start.1) | collective-permute-done | bytes 294944 | tf_op jit(solution)/shard_map/ppermute | solution.py:61
  20.7 0.0 collective-permute-done.2.c_ref
  20.7 0.6 collective-permute-done.3.d_ref
  21.3 0.1 first_sum.1
  21.5 0.1 collective-permute-start.4
  21.6 2.2 %collective-permute-start.5 = (bf16[8,4608]{1,0:T(8,128)(2,1)S(1)}, bf16[8,4608]{1,0:T(8,128)(2,1)S(1)}, u32[]{:S(2)}, u32[]{:S(2)}) collective-permute-start(bf16[8,4608]{1,0:T(8,128)(2,1)S(1)} %get-tuple-element.20), channel_id=1, source_target_pairs={{0,128},{1,129},{2,130},{3,131},{4,132},{5,133},{6,134},{7,135},{8... | collective-permute-start | bytes 221192 | tf_op jit(solution)/shard_map/ppermute | solution.py:61
  23.8 1.2 %collective-permute-start.6 = (bf16[8,4608]{1,0:T(8,128)(2,1)S(1)}, bf16[8,4608]{1,0:T(8,128)(2,1)S(1)}, u32[]{:S(2)}, u32[]{:S(2)}) collective-permute-start(bf16[8,4608]{1,0:T(8,128)(2,1)S(1)} %get-tuple-element.21), channel_id=1, source_target_pairs={{0,192},{1,193},{2,194},{3,195},{4,196},{5,197},{6,198},{7,199},{8... | collective-permute-start | bytes 221192 | tf_op jit(solution)/shard_map/ppermute | solution.py:61
  24.9 1.8 %collective-permute-done.4.b_ref = bf16[8,4608]{1,0:T(8,128)(2,1)S(1)} collective-permute-done((bf16[8,4608]{1,0:T(8,128)(2,1)S(1)}, bf16[8,4608]{1,0:T(8,128)(2,1)S(1)}, u32[]{:S(2)}, u32[]{:S(2)}) %collective-permute-start.4) | collective-permute-done | bytes 73760 | tf_op jit(solution)/shard_map/ppermute | solution.py:61
  26.7 0.0 collective-permute-done.5.c_ref
  26.7 0.9 %collective-permute-done.6.d_ref = bf16[8,4608]{1,0:T(8,128)(2,1)S(1)} collective-permute-done((bf16[8,4608]{1,0:T(8,128)(2,1)S(1)}, bf16[8,4608]{1,0:T(8,128)(2,1)S(1)}, u32[]{:S(2)}, u32[]{:S(2)}) %collective-permute-start.6) | collective-permute-done | bytes 73760 | tf_op jit(solution)/shard_map/ppermute | solution.py:61
  27.6 0.8 second_sum.1
  28.4 7.9 %all-to-all-start = ((bf16[8,36,128]{2,1,0:T(8,128)(2,1)}), bf16[8,36,128]{2,1,0:T(8,128)(2,1)S(1)}, u32[]{:S(2)}, u32[]{:S(2)}) async-start(bf16[8,36,128]{2,1,0:T(8,128)(2,1)} %second_sum.1), calls=%async_computation | async-start | bytes 163840 | tf_op jit(solution)/shard_map/all_to_all | solution.py:278
  36.4 6.5 %all-to-all-done.arrived_ref = bf16[8,36,128]{2,1,0:T(8,128)(2,1)S(1)} async-done(((bf16[8,36,128]{2,1,0:T(8,128)(2,1)}), bf16[8,36,128]{2,1,0:T(8,128)(2,1)S(1)}, u32[]{:S(2)}, u32[]{:S(2)}) %all-to-all-start) | async-done | bytes 73760 | tf_op jit(solution)/shard_map/all_to_all | solution.py:278
  43.0 9.0 %all_to_all.10.in_ref = bf16[8,36,128]{2,1,0:T(8,128)(2,1)S(1)} all-to-all(bf16[8,36,128]{2,1,0:T(8,128)(2,1)S(1)} %get-tuple-element.24), channel_id=1, replica_groups=mesh['y'=4,'zh'=2,'core'=2,'zl'=4,'x'=4] {'zl','zh'}, dimensions={0} | all-to-all | bytes 147456 | tf_op jit(solution)/shard_map/all_to_all | solution.py:281
  52.0 0.2 line_rows.1.a_ref
  52.2 0.6 collective-permute-start.9
  52.7 2.7 %collective-permute-start.8 = (bf16[8,4608]{1,0:T(8,128)(2,1)S(1)}, bf16[8,4608]{1,0:T(8,128)(2,1)S(1)}, u32[]{:S(2)}, u32[]{:S(2)}) collective-permute-start(bf16[8,4608]{1,0:T(8,128)(2,1)S(1)} %line_rows.1.a_ref), channel_id=1, source_target_pairs={{0,128},{1,129},{2,130},{3,131},{4,132},{5,133},{6,134},{7,135},{8... | collective-permute-start | bytes 221192 | tf_op jit(solution)/shard_map/ppermute | solution.py:61
  55.5 0.4 collective-permute-start.7
  55.9 0.9 %collective-permute-done.9.d_ref = bf16[8,4608]{1,0:T(8,128)(2,1)S(1)} collective-permute-done((bf16[8,4608]{1,0:T(8,128)(2,1)S(1)}, bf16[8,4608]{1,0:T(8,128)(2,1)S(1)}, u32[]{:S(2)}, u32[]{:S(2)}) %collective-permute-start.9) | collective-permute-done | bytes 73760 | tf_op jit(solution)/shard_map/ppermute | solution.py:61
  56.8 1.2 %collective-permute-done.8.c_ref = bf16[8,4608]{1,0:T(8,128)(2,1)S(1)} collective-permute-done((bf16[8,4608]{1,0:T(8,128)(2,1)S(1)}, bf16[8,4608]{1,0:T(8,128)(2,1)S(1)}, u32[]{:S(2)}, u32[]{:S(2)}) %collective-permute-start.8) | collective-permute-done | bytes 73760 | tf_op jit(solution)/shard_map/ppermute | solution.py:61
  58.0 0.7 collective-permute-done.7.b_ref
  58.7 1.4 %collective-permute-start.15 = (bf16[32,4608]{1,0:T(8,128)(2,1)S(1)}, bf16[32,4608]{1,0:T(8,128)(2,1)S(1)}, u32[]{:S(2)}, u32[]{:S(2)}) collective-permute-start(bf16[32,4608]{1,0:T(8,128)(2,1)S(1)} %join.1.a_ref), channel_id=1, source_target_pairs={{0,1},{1,2},{2,3},{3,0},{4,5},{5,6},{6,7},{7,4},{8,9},{9,10},{10,1... | collective-permute-start | bytes 884744 | tf_op jit(solution)/shard_map/ppermute | solution.py:61
  60.1 2.1 %collective-permute-start.13 = (bf16[32,4608]{1,0:T(8,128)(2,1)S(1)}, bf16[32,4608]{1,0:T(8,128)(2,1)S(1)}, u32[]{:S(2)}, u32[]{:S(2)}) collective-permute-start(bf16[32,4608]{1,0:T(8,128)(2,1)S(1)} %join.1.a_ref), channel_id=1, source_target_pairs={{0,2},{1,3},{2,0},{3,1},{4,6},{5,7},{6,4},{7,5},{8,10},{9,11},{10,... | collective-permute-start | bytes 884744 | tf_op jit(solution)/shard_map/ppermute | solution.py:61
  62.1 1.3 %collective-permute-start.11 = (bf16[32,4608]{1,0:T(8,128)(2,1)S(1)}, bf16[32,4608]{1,0:T(8,128)(2,1)S(1)}, u32[]{:S(2)}, u32[]{:S(2)}) collective-permute-start(bf16[32,4608]{1,0:T(8,128)(2,1)S(1)} %join.1.a_ref), channel_id=1, source_target_pairs={{0,3},{1,0},{2,1},{3,2},{4,7},{5,4},{6,5},{7,6},{8,11},{9,8},{10,9... | collective-permute-start | bytes 884744 | tf_op jit(solution)/shard_map/ppermute | solution.py:61
  63.5 9.0 %collective-permute-start.10 = (bf16[32,4608]{1,0:T(8,128)(2,1)S(1)}, bf16[32,4608]{1,0:T(8,128)(2,1)S(1)}, u32[]{:S(2)}, u32[]{:S(2)}) collective-permute-start(bf16[32,4608]{1,0:T(8,128)(2,1)S(1)} %join.1.a_ref), channel_id=1, source_target_pairs={{0,16},{1,17},{2,18},{3,19},{4,20},{5,21},{6,22},{7,23},{8,24},{9,... | collective-permute-start | bytes 884744 | tf_op jit(solution)/shard_map/ppermute | solution.py:65
  72.5 0.0 collective-permute-done.15.d_ref
  72.5 2.7 %collective-permute-start.16 = (bf16[32,4608]{1,0:T(8,128)(2,1)S(1)}, bf16[32,4608]{1,0:T(8,128)(2,1)S(1)}, u32[]{:S(2)}, u32[]{:S(2)}) collective-permute-start(bf16[32,4608]{1,0:T(8,128)(2,1)S(1)} %collective-permute-done.15.d_ref), channel_id=1, source_target_pairs={{0,16},{1,17},{2,18},{3,19},{4,20},{5,21},{6,22},{7,23},{8,24},{9,... | collective-permute-start | bytes 884744 | tf_op jit(solution)/shard_map/ppermute | solution.py:65
  75.3 0.0 collective-permute-done.13.c_ref
  75.3 4.2 %collective-permute-start.14 = (bf16[32,4608]{1,0:T(8,128)(2,1)S(1)}, bf16[32,4608]{1,0:T(8,128)(2,1)S(1)}, u32[]{:S(2)}, u32[]{:S(2)}) collective-permute-start(bf16[32,4608]{1,0:T(8,128)(2,1)S(1)} %collective-permute-done.13.c_ref), channel_id=1, source_target_pairs={{0,16},{1,17},{2,18},{3,19},{4,20},{5,21},{6,22},{7,23},{8,24},{9,... | collective-permute-start | bytes 884744 | tf_op jit(solution)/shard_map/ppermute | solution.py:65
  79.4 0.0 collective-permute-done.11.b_ref
  79.4 0.0 collective-permute-start.12
  79.4 0.6 reshape.28
  80.0 0.6 reshape.29
  80.7 1.3 %restore.2.refs_0_ = bf16[128,9216]{1,0:T(8,128)(2,1)} custom-call(s32[1]{0:T(128)} %bitcast.place_ref, bf16[32,4608]{1,0:T(8,128)(2,1)S(1)} %join.1.a_ref, bf16[32,4608]{1,0:T(8,128)(2,1)S(1)} %collective-permute-done.11.b_ref, bf16[32,4608]{1,0:T(8,128)(2,1)S(1)} %collective-permute-done.13.c_ref, bf16[32,4608]{1,0:T(8,128)(2,1)S(1)} %collective-permute-done.15.d_ref), custom_call_target="tpu_custom_call" | custom-call | tf_op jit(solution)/shard_map/restore/pallas_call | solution.py:256
  82.0 0.0 collective-permute-done.16.d_ref
  82.0 0.0 collective-permute-done.14.c_ref
  82.0 1.3 %restore.3 = bf16[128,9216]{1,0:T(8,128)(2,1)} custom-call(s32[1]{0:T(128)} %bitcast.place_ref, bf16[32,4608]{1,0:T(8,128)(2,1)S(1)} %collective-permute-done.10.a_ref, bf16[32,4608]{1,0:T(8,128)(2,1)S(1)} %collective-permute-done.12.b_ref, bf16[32,4608]{1,0:T(8,128)(2,1)S(1)} %collective-permute-done.14.c_ref, ...), custom_call_target="tpu_custom_call", output_to_operand_aliasing={{}: (5, {})} | custom-call | tf_op jit(solution)/shard_map/restore/pallas_call | solution.py:256
  (10 shorter events, 0.2 us)
Async XLA Ops:
  3.7 6.4 %collective-permute-start = (bf16[128,4608]{1,0:T(8,128)(2,1)S(1)}, bf16[128,4608]{1,0:T(8,128)(2,1)S(1)}, u32[]{:S(2)}, u32[]{:S(2)}) collective-permute-start(bf16[128,4608]{1,0:T(8,128)(2,1)S(1)} %compensate.3), channel_id=1, source_target_pairs={{0,16},{1,17},{2,18},{3,19},{4,20},{5,21},{6,22},{7,23},{8,24},{9,... | collective-permute-start | bytes 3538952 | tf_op jit(solution)/shard_map/ppermute | solution.py:65
  10.0 26.2 %copy-start = (f32[1,1,4608]{2,1,0:T(1,128)S(1)}, f32[1,1,4608]{2,1,0:T(1,128)}, u32[]{:S(2)}) copy-start(f32[1,1,4608]{2,1,0:T(1,128)} %param.9) | copy-start | bytes 55300
  10.1 26.3 %copy-start.1 = (f32[1,1,4608]{2,1,0:T(1,128)S(1)}, f32[1,1,4608]{2,1,0:T(1,128)}, u32[]{:S(2)}) copy-start(f32[1,1,4608]{2,1,0:T(1,128)} %param.10) | copy-start | bytes 55300
  10.1 26.3 %copy-start.2 = (f32[1,1,4608]{2,1,0:T(1,128)S(1)}, f32[1,1,4608]{2,1,0:T(1,128)}, u32[]{:S(2)}) copy-start(f32[1,1,4608]{2,1,0:T(1,128)} %param.11) | copy-start | bytes 55300
  10.4 10.3 %collective-permute-start.1 = (bf16[32,4608]{1,0:T(8,128)(2,1)S(1)}, bf16[32,4608]{1,0:T(8,128)(2,1)S(1)}, u32[]{:S(2)}, u32[]{:S(2)}) collective-permute-start(bf16[32,4608]{1,0:T(8,128)(2,1)S(1)} %get-tuple-element.15), channel_id=1, source_target_pairs={{0,1},{1,2},{2,3},{3,0},{4,5},{5,6},{6,7},{7,4},{8,9},{9,10},{10,1... | collective-permute-start | bytes 884744 | tf_op jit(solution)/shard_map/ppermute | solution.py:61
  10.5 10.2 %collective-permute-start.2 = (bf16[32,4608]{1,0:T(8,128)(2,1)S(1)}, bf16[32,4608]{1,0:T(8,128)(2,1)S(1)}, u32[]{:S(2)}, u32[]{:S(2)}) collective-permute-start(bf16[32,4608]{1,0:T(8,128)(2,1)S(1)} %get-tuple-element.16), channel_id=1, source_target_pairs={{0,2},{1,3},{2,0},{3,1},{4,6},{5,7},{6,4},{7,5},{8,10},{9,11},{10,... | collective-permute-start | bytes 884744 | tf_op jit(solution)/shard_map/ppermute | solution.py:61
  12.6 8.7 %collective-permute-start.3 = (bf16[32,4608]{1,0:T(8,128)(2,1)S(1)}, bf16[32,4608]{1,0:T(8,128)(2,1)S(1)}, u32[]{:S(2)}, u32[]{:S(2)}) collective-permute-start(bf16[32,4608]{1,0:T(8,128)(2,1)S(1)} %get-tuple-element.17), channel_id=1, source_target_pairs={{0,3},{1,0},{2,1},{3,2},{4,7},{5,4},{6,5},{7,6},{8,11},{9,8},{10,9... | collective-permute-start | bytes 884744 | tf_op jit(solution)/shard_map/ppermute | solution.py:61
  21.5 5.3 %collective-permute-start.4 = (bf16[8,4608]{1,0:T(8,128)(2,1)S(1)}, bf16[8,4608]{1,0:T(8,128)(2,1)S(1)}, u32[]{:S(2)}, u32[]{:S(2)}) collective-permute-start(bf16[8,4608]{1,0:T(8,128)(2,1)S(1)} %get-tuple-element.19), channel_id=1, source_target_pairs={{0,64},{1,65},{2,66},{3,67},{4,68},{5,69},{6,70},{7,71},{8,72},{9,... | collective-permute-start | bytes 221192 | tf_op jit(solution)/shard_map/ppermute | solution.py:61
  21.6 5.2 %collective-permute-start.5 = (bf16[8,4608]{1,0:T(8,128)(2,1)S(1)}, bf16[8,4608]{1,0:T(8,128)(2,1)S(1)}, u32[]{:S(2)}, u32[]{:S(2)}) collective-permute-start(bf16[8,4608]{1,0:T(8,128)(2,1)S(1)} %get-tuple-element.20), channel_id=1, source_target_pairs={{0,128},{1,129},{2,130},{3,131},{4,132},{5,133},{6,134},{7,135},{8... | collective-permute-start | bytes 221192 | tf_op jit(solution)/shard_map/ppermute | solution.py:61
  23.8 3.8 %collective-permute-start.6 = (bf16[8,4608]{1,0:T(8,128)(2,1)S(1)}, bf16[8,4608]{1,0:T(8,128)(2,1)S(1)}, u32[]{:S(2)}, u32[]{:S(2)}) collective-permute-start(bf16[8,4608]{1,0:T(8,128)(2,1)S(1)} %get-tuple-element.21), channel_id=1, source_target_pairs={{0,192},{1,193},{2,194},{3,195},{4,196},{5,197},{6,198},{7,199},{8... | collective-permute-start | bytes 221192 | tf_op jit(solution)/shard_map/ppermute | solution.py:61
  28.4 14.5 %all-to-all-start = ((bf16[8,36,128]{2,1,0:T(8,128)(2,1)}), bf16[8,36,128]{2,1,0:T(8,128)(2,1)S(1)}, u32[]{:S(2)}, u32[]{:S(2)}) async-start(bf16[8,36,128]{2,1,0:T(8,128)(2,1)} %second_sum.1), calls=%async_computation | async-start | bytes 163840 | tf_op jit(solution)/shard_map/all_to_all | solution.py:278
  52.2 4.6 %collective-permute-start.9 = (bf16[8,4608]{1,0:T(8,128)(2,1)S(1)}, bf16[8,4608]{1,0:T(8,128)(2,1)S(1)}, u32[]{:S(2)}, u32[]{:S(2)}) collective-permute-start(bf16[8,4608]{1,0:T(8,128)(2,1)S(1)} %line_rows.1.a_ref), channel_id=1, source_target_pairs={{0,64},{1,65},{2,66},{3,67},{4,68},{5,69},{6,70},{7,71},{8,72},{9,... | collective-permute-start | bytes 221192 | tf_op jit(solution)/shard_map/ppermute | solution.py:61
  52.7 5.2 %collective-permute-start.8 = (bf16[8,4608]{1,0:T(8,128)(2,1)S(1)}, bf16[8,4608]{1,0:T(8,128)(2,1)S(1)}, u32[]{:S(2)}, u32[]{:S(2)}) collective-permute-start(bf16[8,4608]{1,0:T(8,128)(2,1)S(1)} %line_rows.1.a_ref), channel_id=1, source_target_pairs={{0,128},{1,129},{2,130},{3,131},{4,132},{5,133},{6,134},{7,135},{8... | collective-permute-start | bytes 221192 | tf_op jit(solution)/shard_map/ppermute | solution.py:61
  55.5 3.2 %collective-permute-start.7 = (bf16[8,4608]{1,0:T(8,128)(2,1)S(1)}, bf16[8,4608]{1,0:T(8,128)(2,1)S(1)}, u32[]{:S(2)}, u32[]{:S(2)}) collective-permute-start(bf16[8,4608]{1,0:T(8,128)(2,1)S(1)} %line_rows.1.a_ref), channel_id=1, source_target_pairs={{0,192},{1,193},{2,194},{3,195},{4,196},{5,197},{6,198},{7,199},{8... | collective-permute-start | bytes 221192 | tf_op jit(solution)/shard_map/ppermute | solution.py:61
  58.7 13.8 %collective-permute-start.15 = (bf16[32,4608]{1,0:T(8,128)(2,1)S(1)}, bf16[32,4608]{1,0:T(8,128)(2,1)S(1)}, u32[]{:S(2)}, u32[]{:S(2)}) collective-permute-start(bf16[32,4608]{1,0:T(8,128)(2,1)S(1)} %join.1.a_ref), channel_id=1, source_target_pairs={{0,1},{1,2},{2,3},{3,0},{4,5},{5,6},{6,7},{7,4},{8,9},{9,10},{10,1... | collective-permute-start | bytes 884744 | tf_op jit(solution)/shard_map/ppermute | solution.py:61
  60.1 15.2 %collective-permute-start.13 = (bf16[32,4608]{1,0:T(8,128)(2,1)S(1)}, bf16[32,4608]{1,0:T(8,128)(2,1)S(1)}, u32[]{:S(2)}, u32[]{:S(2)}) collective-permute-start(bf16[32,4608]{1,0:T(8,128)(2,1)S(1)} %join.1.a_ref), channel_id=1, source_target_pairs={{0,2},{1,3},{2,0},{3,1},{4,6},{5,7},{6,4},{7,5},{8,10},{9,11},{10,... | collective-permute-start | bytes 884744 | tf_op jit(solution)/shard_map/ppermute | solution.py:61
  62.1 17.3 %collective-permute-start.11 = (bf16[32,4608]{1,0:T(8,128)(2,1)S(1)}, bf16[32,4608]{1,0:T(8,128)(2,1)S(1)}, u32[]{:S(2)}, u32[]{:S(2)}) collective-permute-start(bf16[32,4608]{1,0:T(8,128)(2,1)S(1)} %join.1.a_ref), channel_id=1, source_target_pairs={{0,3},{1,0},{2,1},{3,2},{4,7},{5,4},{6,5},{7,6},{8,11},{9,8},{10,9... | collective-permute-start | bytes 884744 | tf_op jit(solution)/shard_map/ppermute | solution.py:61
  63.5 18.5 %collective-permute-start.10 = (bf16[32,4608]{1,0:T(8,128)(2,1)S(1)}, bf16[32,4608]{1,0:T(8,128)(2,1)S(1)}, u32[]{:S(2)}, u32[]{:S(2)}) collective-permute-start(bf16[32,4608]{1,0:T(8,128)(2,1)S(1)} %join.1.a_ref), channel_id=1, source_target_pairs={{0,16},{1,17},{2,18},{3,19},{4,20},{5,21},{6,22},{7,23},{8,24},{9,... | collective-permute-start | bytes 884744 | tf_op jit(solution)/shard_map/ppermute | solution.py:65
  72.5 9.5 %collective-permute-start.16 = (bf16[32,4608]{1,0:T(8,128)(2,1)S(1)}, bf16[32,4608]{1,0:T(8,128)(2,1)S(1)}, u32[]{:S(2)}, u32[]{:S(2)}) collective-permute-start(bf16[32,4608]{1,0:T(8,128)(2,1)S(1)} %collective-permute-done.15.d_ref), channel_id=1, source_target_pairs={{0,16},{1,17},{2,18},{3,19},{4,20},{5,21},{6,22},{7,23},{8,24},{9,... | collective-permute-start | bytes 884744 | tf_op jit(solution)/shard_map/ppermute | solution.py:65
  75.3 6.7 %collective-permute-start.14 = (bf16[32,4608]{1,0:T(8,128)(2,1)S(1)}, bf16[32,4608]{1,0:T(8,128)(2,1)S(1)}, u32[]{:S(2)}, u32[]{:S(2)}) collective-permute-start(bf16[32,4608]{1,0:T(8,128)(2,1)S(1)} %collective-permute-done.13.c_ref), channel_id=1, source_target_pairs={{0,16},{1,17},{2,18},{3,19},{4,20},{5,21},{6,22},{7,23},{8,24},{9,... | collective-permute-start | bytes 884744 | tf_op jit(solution)/shard_map/ppermute | solution.py:65
  79.4 2.6 %collective-permute-start.12 = (bf16[32,4608]{1,0:T(8,128)(2,1)S(1)}, bf16[32,4608]{1,0:T(8,128)(2,1)S(1)}, u32[]{:S(2)}, u32[]{:S(2)}) collective-permute-start(bf16[32,4608]{1,0:T(8,128)(2,1)S(1)} %collective-permute-done.11.b_ref), channel_id=1, source_target_pairs={{0,16},{1,17},{2,18},{3,19},{4,20},{5,21},{6,22},{7,23},{8,24},{9,... | collective-permute-start | bytes 884744 | tf_op jit(solution)/shard_map/ppermute | solution.py:65

commit v3 on v2

--- a/solution.py
+++ b/solution.py
@@ -20,7 +20,7 @@
 WIDTH = 9216
 HALF = WIDTH // 2
 LANES = 128
-CHUNKS = 4
+CHUNKS = 6
 CHUNK = HALF // CHUNKS
 PER_CHUNK = CHUNK // LANES
 SLAB_ROWS = HALF // LANES
@@ -40,29 +40,35 @@
     return pltpu.with_memory_space_constraint(array, pltpu.HBM)
 
 
-def shifted(stage, step):
+def shifted(step):
+    flat = lambda y, zh, core, zl, x: (((y * 2 + zh) * 2 + core) * 4 + zl) * 4 + x
     pairs = []
-    for y in range(4):
-        for zh in range(2):
-            for core in range(2):
-                for zl in range(4):
-                    for x in range(4):
-                        flat = lambda y, x: (((y * 2 + zh) * 2 + core) * 4 + zl) * 4 + x
-                        along_x = core == stage
-                        to = flat(y, (x + step) % 4) if along_x else flat((y + step) % 4, x)
-                        pairs.append((flat(y, x), to))
+    for i in range(256):
+        x, zl, core, zh, y = i % 4, i // 4 % 4, i // 16 % 2, i // 32 % 2, i // 64
+        to = flat((y + step) % 4, zh, core, zl, x) if core else flat(y, zh, core, zl, (x + step) % 4)
+        pairs.append((i, to))
     return pairs
 
 
 SWAP = [(i, i ^ 16) for i in range(256)]
 
 
-def send(array, stage, step):
-    return lax.ppermute(array, AXES, shifted(stage, step))
+def send(array, step):
+    return lax.ppermute(array, AXES, shifted(step))
 
 
 def swap_cores(array):
     return lax.ppermute(array, AXES, SWAP)
+
+
+def owner_groups():
+    flat = lambda y, zh, core, zl, x: (((y * 2 + zh) * 2 + core) * 4 + zl) * 4 + x
+    groups = [[flat(y, zh, 0, zl, x) for y in range(4) for zl in range(4) for zh in range(2)] for x in range(4)]
+    return groups + [[flat(y, zh, 1, zl, x) for x in range(4) for zl in range(4) for zh in range(2)] for y in range(4)]
+
+
+def exchange(array):
+    return lax.all_to_all(array, AXES, 0, 0, axis_index_groups=owner_groups(), tiled=True)
 
 
 def order(place, half, transposed):
@@ -70,12 +76,11 @@
     sent = lax.broadcasted_iota(jnp.int32, (ROWS, ROWS), 1 if transposed else 0)
     flat = lax.broadcasted_iota(jnp.int32, (ROWS, ROWS), 0 if transposed else 1)
     a0, a_step = jnp.where(half == 0, x0, y0), jnp.where(half == 0, 8, 2)
-    b0, b_step = jnp.where(half == 0, y0, x0), jnp.where(half == 0, 2, 8)
-    a, b = (sent // 32 + a0) % 4, (sent // 8 % 4 + b0) % 4
-    return (sent // 2 % 4 * 32 + a * a_step + b * b_step + sent % 2 == flat).astype(F32).astype(BF16)
-
-
-def compensate_kernel(other, place_ref, codes_hbm, scales_hbm, feedback_hbm, out_ref, codes, scales, feedback, turned, sems):
+    a, b = (sent // 32 + a0) % 4, sent // 8 % 4
+    return (sent // 2 % 4 * 32 + a * a_step + b * (10 - a_step) + sent % 2 == flat).astype(F32).astype(BF16)
+
+
+def compensate_kernel(other, place_ref, codes_hbm, scales_hbm, feedback_hbm, out_ref, codes, scales, feedback, turned, summed, sems):
     core = place_ref[0] // 16 % 2
     half = 1 - core if other else core
     copies = [pltpu.make_async_copy(scales_hbm, scales, sems.at[2 * CHUNKS])]
@@ -96,8 +101,8 @@
             columns = slice(block * LANES, (block + 1) * LANES)
             at = i * PER_CHUNK + block
             dequant = codes[i, :, columns].astype(F32) * scale[:, at : at + 1]
-            compensated = (dequant + feedback[i, :, columns].astype(F32)).astype(BF16)
-            out_ref[:, at * LANES : (at + 1) * LANES] = jnp.dot(moved, compensated, preferred_element_type=F32).astype(BF16)
+            summed[:, columns] = (dequant + feedback[i, :, columns].astype(F32)).astype(BF16)
+        out_ref[:, i * CHUNK : (i + 1) * CHUNK] = jnp.dot(moved, summed[...], preferred_element_type=F32).astype(BF16)
 
 
 def compensate(other, place, codes, scales, feedback):
@@ -111,6 +116,7 @@
             pltpu.VMEM((WIDTH // LANES, ROWS), F32),
             pltpu.VMEM((CHUNKS, ROWS, CHUNK), BF16),
             pltpu.VMEM((ROWS, LANES), F32),
+            pltpu.VMEM((ROWS, CHUNK), BF16),
             pltpu.SemaphoreType.DMA((2 * CHUNKS + 1,)),
         ],
         compiler_params=params(),
@@ -141,38 +147,23 @@
     return functools.reduce(lambda a, b: a + b, others, first)
 
 
-def first_sum_kernel(a_ref, b_ref, c_ref, d_ref, *out_refs):
-    for piece, out_ref in enumerate(out_refs):
-        out_ref[...] = total_of((a_ref, b_ref, c_ref, d_ref), slice(piece * 8, (piece + 1) * 8)).astype(BF16)
-
-
-def first_sum(parts):
-    return pl.pallas_call(
-        first_sum_kernel,
-        out_shape=[jax.ShapeDtypeStruct((8, HALF), BF16)] * 4,
-        in_specs=[WHOLE] * 4,
-        out_specs=[WHOLE] * 4,
-        compiler_params=params(),
-        name="first_sum",
-    )(*parts)
-
-
-def second_sum_kernel(a_ref, b_ref, c_ref, d_ref, out_ref, spread):
+def first_sum_kernel(a_ref, b_ref, c_ref, d_ref, out_ref, columns):
     total = total_of((a_ref, b_ref, c_ref, d_ref), slice(None))
     for block in range(SLAB_ROWS):
-        spread[:, block, :] = total[:, block * LANES : (block + 1) * LANES]
-    out_ref[...] = spread[...].astype(BF16)
-
-
-def second_sum(parts):
-    return pl.pallas_call(
-        second_sum_kernel,
-        out_shape=jax.ShapeDtypeStruct((8, SLAB_ROWS, LANES), BF16),
+        columns[block * 32 : (block + 1) * 32, :] = total[:, block * LANES : (block + 1) * LANES]
+    for row in range(32):
+        out_ref[row] = columns[pl.ds(row, SLAB_ROWS, stride=32), :].astype(BF16)
+
+
+def first_sum(parts):
+    return pl.pallas_call(
+        first_sum_kernel,
+        out_shape=jax.ShapeDtypeStruct((32, SLAB_ROWS, LANES), BF16),
         in_specs=[WHOLE] * 4,
         out_specs=WHOLE,
-        scratch_shapes=[pltpu.VMEM((8, SLAB_ROWS, LANES), F32)],
-        compiler_params=params(),
-        name="second_sum",
+        scratch_shapes=[pltpu.VMEM((SLAB_ROWS * 32, LANES), F32)],
+        compiler_params=params(),
+        name="first_sum",
     )(*parts)
 
 
@@ -193,7 +184,7 @@
     slab = jax.ShapeDtypeStruct((SLAB_ROWS, LANES), F32)
     return pl.pallas_call(
         adam_kernel,
-        out_shape=(slab, slab, jax.ShapeDtypeStruct((8, SLAB_ROWS, LANES), BF16)),
+        out_shape=(slab, slab, jax.ShapeDtypeStruct((32, SLAB_ROWS, LANES), BF16)),
         in_specs=[WHOLE] * 4,
         out_specs=[WHOLE] * 3,
         compiler_params=params(),
@@ -210,29 +201,13 @@
 def line_rows(arrived):
     return pl.pallas_call(
         line_kernel,
-        out_shape=jax.ShapeDtypeStruct((8, HALF), BF16),
+        out_shape=jax.ShapeDtypeStruct((32, HALF), BF16),
         in_specs=[WHOLE],
         out_specs=WHOLE,
-        scratch_shapes=[pltpu.VMEM((8, SLAB_ROWS, LANES), F32)],
+        scratch_shapes=[pltpu.VMEM((32, SLAB_ROWS, LANES), F32)],
         compiler_params=params(),
         name="line_rows",
     )(arrived)
-
-
-def join_kernel(a_ref, b_ref, c_ref, d_ref, out_ref):
-    for piece, ref in enumerate((a_ref, b_ref, c_ref, d_ref)):
-        out_ref[piece * 8 : (piece + 1) * 8, :] = ref[...]
-
-
-def join(parts):
-    return pl.pallas_call(
-        join_kernel,
-        out_shape=jax.ShapeDtypeStruct((32, HALF), BF16),
-        in_specs=[WHOLE] * 4,
-        out_specs=WHOLE,
-        compiler_params=params(),
-        name="join",
-    )(*parts)
 
 
 def restore_kernel(other, place_ref, a_ref, b_ref, c_ref, d_ref, *refs):
@@ -273,18 +248,17 @@
     taken = swap_cores(given)
     kept = compensate(False, place, codes, turned, feed)
     first = pair_sum(kept, taken)
-    second_parts = first_sum([first[0]] + [send(first[step], 0, step) for step in (1, 2, 3)])
-    plane = second_sum([second_parts[0]] + [send(second_parts[step], 1, step) for step in (1, 2, 3)])
-    line = lax.all_to_all(plane, ("zl", "zh"), 0, 0, tiled=True)
+    plane = first_sum([first[0]] + [send(first[step], step) for step in (1, 2, 3)])
     slab = lambda a: a.reshape(SLAB_ROWS, LANES)
-    adam_dir, new_master, copies = adam(line, slab(master), slab(moment), slab(second))
-    owned = line_rows(lax.all_to_all(copies, ("zl", "zh"), 0, 0, tiled=True))
-    joined = join([owned] + [send(owned, 1, 4 - place_of) for place_of in (1, 2, 3)])
-    mine = [joined] + [send(joined, 0, 4 - place_of) for place_of in (1, 2, 3)]
+    adam_dir, new_master, copies = adam(exchange(plane), slab(master), slab(moment), slab(second))
+    joined = line_rows(exchange(copies))
+    mine = [joined] + [send(joined, 4 - place_of) for place_of in (1, 2, 3)]
+    adam_dir, new_master = adam_dir.reshape(1, 1, HALF), new_master.reshape(1, 1, HALF)
+    mine[2], adam_dir, new_master = lax.optimization_barrier((mine[2], adam_dir, new_master))
     theirs = [swap_cores(part) for part in mine]
     half = restore(False, place, mine)
     weights = restore(True, place, theirs, (half,))
-    return adam_dir.reshape(1, 1, HALF), new_master.reshape(1, 1, HALF), weights
+    return adam_dir, new_master, weights
 
 
 def solution(mesh):

time: 84 us -> 82.4 us (0.981)
  starting transfers between devices: 42.4 us -> 31 us
  blocking collectives: 9.05 us -> 18.2 us
  Pallas kernels: 10.1 us -> 12.4 us
  waiting for transfers between devices: 19.6 us -> 18.3 us
    all_to_all x1, blocking collectives: 9.05 us -> 18.2 us  [exchange(): lax.all_to_all(array, AXES, 0, 0, axis_index_groups=owner_groups(), tiled...]
    ppermute x5, starting transfers between devices: 19.3 us -> 12.6 us  [swap_cores(): return lax.ppermute(array, AXES, SWAP)]
    ppermute x12 -> x6, starting transfers between devices: 15.3 us -> 8.76 us  [send(): return lax.ppermute(array, AXES, shifted(step))]
    ppermute x12 -> x6, waiting for transfers between devices: 13.1 us -> 7.62 us  [send(): return lax.ppermute(array, AXES, shifted(step))]
    all_to_all x1, waiting for transfers between devices: 6.46 us -> 10.5 us  [exchange(): lax.all_to_all(array, AXES, 0, 0, axis_index_groups=owner_groups(), tiled...]
    all_to_all x1, starting transfers between devices: 7.86 us -> 9.63 us  [exchange(): lax.all_to_all(array, AXES, 0, 0, axis_index_groups=owner_groups(), tiled...]
    pallas_call x2, Pallas kernels: 6.06 us -> 7.54 us  [compensate(): pl.pallas_call(functools.partial(compensate_kernel, other), out_shape=jax...]
    pallas_call x4 -> x2, Pallas kernels: 1.11 us -> 1.97 us  [the longest x1 1.33 us: first_sum(): pl.pallas_call(first_sum_kernel, out_shape=jax.ShapeDtypeStruct((32, SLAB...]
  transfers between devices with their start and end apart: 18 -> 12, of which waited for: 8 -> 4; matrix products, arithmetic and copies ran while one was open for 2% -> 2% of each run, Pallas kernels for 5% -> 6%
where the time goes in v3:
time: 82.4 us; the launch traced here: 82.2 us
  starting transfers between devices  31 us (38%)
  waiting for transfers between devices  18.3 us (22%)
  blocking collectives  18.2 us (22%)
  Pallas kernels  12.4 us (15%)
  local copies, waits for them, and re-layouts  1.27 us (2%)
    all_to_all x1, blocking collectives, exchange(): lax.all_to_all(array, AXES, 0, 0, axis_index_groups=owner_groups(), tiled...  18.2 us
    ppermute x5, starting transfers between devices, swap_cores(): return lax.ppermute(array, AXES, SWAP)  12.6 us
    all_to_all x1, waiting for transfers between devices, exchange(): lax.all_to_all(array, AXES, 0, 0, axis_index_groups=owner_groups(), tiled...  10.5 us
    all_to_all x1, starting transfers between devices, exchange(): lax.all_to_all(array, AXES, 0, 0, axis_index_groups=owner_groups(), tiled...  9.63 us
    ppermute x6, starting transfers between devices, send(): return lax.ppermute(array, AXES, shifted(step))  8.76 us
    ppermute x6, waiting for transfers between devices, send(): return lax.ppermute(array, AXES, shifted(step))  7.62 us
    pallas_call x2, Pallas kernels, compensate(): pl.pallas_call(functools.partial(compensate_kernel, other), out_shape=jax...  7.54 us
    pallas_call x2, Pallas kernels, restore(): pl.pallas_call(functools.partial(restore_kernel, other), out_shape=jax.Sh...  2.55 us
  transfers between devices with their start and end apart: 12, of which 4 were waited for; matrix products, arithmetic and copies ran while one was open for 2% of the time, Pallas kernels for 6%

profile of v3, /device:TPU:1, one launch (start us, length us, event | category | flops | bytes accessed | tf_op | source)
XLA Modules:
  0.0 82.2 jit_solution(13981254595674209445)
XLA Ops:
  0.6 3.8 %compensate.3 = bf16[128,4608]{1,0:T(8,128)(2,1)S(1)} custom-call(s32[1]{0:T(128)} %bitcast.place_ref, s32[128,9216]{1,0:T(8,128)} %bitcast.12, f32[72,128]{1,0:T(8,128)} %bitcast.16, bf16[128,9216]{1,0:T(8,128)(2,1)} %bitcast.14), custom_call_target="tpu_custom_call" | custom-call | flops 150994944 | bytes 4718592 | tf_op jit(solution)/shard_map/compensate/pallas_call | solution.py:109
  4.4 3.3 %collective-permute-start = (bf16[128,4608]{1,0:T(8,128)(2,1)S(1)}, bf16[128,4608]{1,0:T(8,128)(2,1)S(1)}, u32[]{:S(2)}, u32[]{:S(2)}) collective-permute-start(bf16[128,4608]{1,0:T(8,128)(2,1)S(1)} %compensate.3), channel_id=1, source_target_pairs={{0,16},{1,17},{2,18},{3,19},{4,20},{5,21},{6,22},{7,23},{8,24},{9,... | collective-permute-start | bytes 3538952 | tf_op jit(solution)/shard_map/ppermute | solution.py:61
  7.7 3.8 %compensate.2.own_ref = bf16[128,4608]{1,0:T(8,128)(2,1)S(1)} custom-call(s32[1]{0:T(128)} %bitcast.place_ref, s32[128,9216]{1,0:T(8,128)} %bitcast.13, f32[72,128]{1,0:T(8,128)} %bitcast.17, bf16[128,9216]{1,0:T(8,128)(2,1)} %bitcast.15), custom_call_target="tpu_custom_call" | custom-call | flops 150994944 | bytes 4718592 | tf_op jit(solution)/shard_map/compensate/pallas_call | solution.py:109
  11.5 0.0 copy-start
  11.5 0.0 copy-start.1
  11.5 0.0 copy-start.2
  11.6 0.0 collective-permute-done.other_ref
  11.6 0.3 pair_sum.1
  11.8 0.1 collective-permute-start.1
  11.9 2.2 %collective-permute-start.2 = (bf16[32,4608]{1,0:T(8,128)(2,1)S(1)}, bf16[32,4608]{1,0:T(8,128)(2,1)S(1)}, u32[]{:S(2)}, u32[]{:S(2)}) collective-permute-start(bf16[32,4608]{1,0:T(8,128)(2,1)S(1)} %get-tuple-element.15), channel_id=1, source_target_pairs={{0,2},{1,3},{2,0},{3,1},{4,6},{5,7},{6,4},{7,5},{8,10},{9,11},{10,... | collective-permute-start | bytes 884744 | tf_op jit(solution)/shard_map/ppermute | solution.py:57
  14.1 1.1 %collective-permute-start.3 = (bf16[32,4608]{1,0:T(8,128)(2,1)S(1)}, bf16[32,4608]{1,0:T(8,128)(2,1)S(1)}, u32[]{:S(2)}, u32[]{:S(2)}) collective-permute-start(bf16[32,4608]{1,0:T(8,128)(2,1)S(1)} %get-tuple-element.16), channel_id=1, source_target_pairs={{0,3},{1,0},{2,1},{3,2},{4,7},{5,4},{6,5},{7,6},{8,11},{9,8},{10,9... | collective-permute-start | bytes 884744 | tf_op jit(solution)/shard_map/ppermute | solution.py:57
  15.2 7.0 %collective-permute-done.1.b_ref = bf16[32,4608]{1,0:T(8,128)(2,1)S(1)} collective-permute-done((bf16[32,4608]{1,0:T(8,128)(2,1)S(1)}, bf16[32,4608]{1,0:T(8,128)(2,1)S(1)}, u32[]{:S(2)}, u32[]{:S(2)}) %collective-permute-start.1) | collective-permute-done | bytes 294944 | tf_op jit(solution)/shard_map/ppermute | solution.py:57
  22.2 0.0 collective-permute-done.2.c_ref
  22.2 0.6 collective-permute-done.3.d_ref
  22.8 1.3 %first_sum.1 = bf16[32,36,128]{2,1,0:T(8,128)(2,1)} custom-call(bf16[32,4608]{1,0:T(8,128)(2,1)S(1)} %get-tuple-element.13.a_ref, bf16[32,4608]{1,0:T(8,128)(2,1)S(1)} %collective-permute-done.1.b_ref, bf16[32,4608]{1,0:T(8,128)(2,1)S(1)} %collective-permute-done.2.c_ref, bf16[32,4608]{1,0:T(8,128)(2,1)S(1)} %collective-permute-done.3.d_ref), custom_call_target="tpu_custom_call" | custom-call | tf_op jit(solution)/shard_map/first_sum/pallas_call | solution.py:159
  24.1 9.6 %all-to-all-start = ((bf16[32,36,128]{2,1,0:T(8,128)(2,1)}), bf16[32,36,128]{2,1,0:T(8,128)(2,1)S(1)}, u32[]{:S(2)}, u32[]{:S(2)}) async-start(bf16[32,36,128]{2,1,0:T(8,128)(2,1)} %first_sum.1), calls=%async_computation | async-start | bytes 655360 | tf_op jit(solution)/shard_map/all_to_all | solution.py:71
  33.8 0.0 copy-done
  33.8 0.0 copy-done.1
  33.9 0.0 copy-done.2
  33.9 10.5 %all-to-all-done.arrived_ref = bf16[32,36,128]{2,1,0:T(8,128)(2,1)S(1)} async-done(((bf16[32,36,128]{2,1,0:T(8,128)(2,1)}), bf16[32,36,128]{2,1,0:T(8,128)(2,1)S(1)}, u32[]{:S(2)}, u32[]{:S(2)}) %all-to-all-start) | async-done | bytes 294944 | tf_op jit(solution)/shard_map/all_to_all | solution.py:71
  44.4 0.1 adam.1
  44.5 18.2 %all_to_all.10.in_ref = bf16[32,36,128]{2,1,0:T(8,128)(2,1)S(1)} all-to-all(bf16[32,36,128]{2,1,0:T(8,128)(2,1)S(1)} %get-tuple-element.17), channel_id=1, replica_groups={{0,32,4,36,8,40,12,44,64,96,68,100,72,104,76,108,128,160,132,164,136,16..., dimensions={0} | all-to-all | bytes 589824 | tf_op jit(solution)/shard_map/all_to_all | solution.py:71
  62.8 0.6 line_rows.1.a_ref
  63.4 2.8 %collective-permute-start.4 = (bf16[32,4608]{1,0:T(8,128)(2,1)S(1)}, bf16[32,4608]{1,0:T(8,128)(2,1)S(1)}, u32[]{:S(2)}, u32[]{:S(2)}) collective-permute-start(bf16[32,4608]{1,0:T(8,128)(2,1)S(1)} %line_rows.1.a_ref), channel_id=1, source_target_pairs={{0,2},{1,3},{2,0},{3,1},{4,6},{5,7},{6,4},{7,5},{8,10},{9,11},{10,... | collective-permute-start | bytes 884744 | tf_op jit(solution)/shard_map/ppermute | solution.py:57
  66.2 0.0 collective-permute-start.9
  66.2 2.7 %collective-permute-start.6 = (bf16[32,4608]{1,0:T(8,128)(2,1)S(1)}, bf16[32,4608]{1,0:T(8,128)(2,1)S(1)}, u32[]{:S(2)}, u32[]{:S(2)}) collective-permute-start(bf16[32,4608]{1,0:T(8,128)(2,1)S(1)} %line_rows.1.a_ref), channel_id=1, source_target_pairs={{0,3},{1,0},{2,1},{3,2},{4,7},{5,4},{6,5},{7,6},{8,11},{9,8},{10,9... | collective-permute-start | bytes 884744 | tf_op jit(solution)/shard_map/ppermute | solution.py:57
  68.8 0.6 reshape.28
  69.5 0.6 reshape.29
  70.1 4.8 %collective-permute-start.5 = (bf16[32,4608]{1,0:T(8,128)(2,1)S(1)}, bf16[32,4608]{1,0:T(8,128)(2,1)S(1)}, u32[]{:S(2)}, u32[]{:S(2)}) collective-permute-start(bf16[32,4608]{1,0:T(8,128)(2,1)S(1)} %line_rows.1.a_ref), channel_id=1, source_target_pairs={{0,16},{1,17},{2,18},{3,19},{4,20},{5,21},{6,22},{7,23},{8,24},{9,... | collective-permute-start | bytes 884744 | tf_op jit(solution)/shard_map/ppermute | solution.py:61
  74.9 0.0 collective-permute-done.4.c_ref
  74.9 0.0 collective-permute-done.9.d_ref
  75.0 3.9 %collective-permute-start.10 = (bf16[32,4608]{1,0:T(8,128)(2,1)S(1)}, bf16[32,4608]{1,0:T(8,128)(2,1)S(1)}, u32[]{:S(2)}, u32[]{:S(2)}) collective-permute-start(bf16[32,4608]{1,0:T(8,128)(2,1)S(1)} %collective-permute-done.9.d_ref), channel_id=1, source_target_pairs={{0,16},{1,17},{2,18},{3,19},{4,20},{5,21},{6,22},{7,23},{8,24},{9,... | collective-permute-start | bytes 884744 | tf_op jit(solution)/shard_map/ppermute | solution.py:61
  78.9 0.0 collective-permute-done.6.b_ref
  78.9 0.0 collective-permute-start.7
  78.9 0.5 collective-permute-start.8
  79.4 1.3 %restore.2.refs_0_ = bf16[128,9216]{1,0:T(8,128)(2,1)} custom-call(s32[1]{0:T(128)} %bitcast.place_ref, bf16[32,4608]{1,0:T(8,128)(2,1)S(1)} %line_rows.1.a_ref, bf16[32,4608]{1,0:T(8,128)(2,1)S(1)} %collective-permute-done.6.b_ref, bf16[32,4608]{1,0:T(8,128)(2,1)S(1)} %collective-permute-done.4.c_ref, bf16[32,4608]{1,0:T(8,128)(2,1)S(1)} %collective-permute-done.9.d_ref), custom_call_target="tpu_custom_call" | custom-call | tf_op jit(solution)/shard_map/restore/pallas_call | solution.py:231
  80.7 0.0 collective-permute-done.5.a_ref
  80.7 0.0 collective-permute-done.10.d_ref
  80.7 0.0 collective-permute-done.7.b_ref
  80.7 0.2 collective-permute-done.8.c_ref
  80.9 1.3 %restore.3 = bf16[128,9216]{1,0:T(8,128)(2,1)} custom-call(s32[1]{0:T(128)} %bitcast.place_ref, bf16[32,4608]{1,0:T(8,128)(2,1)S(1)} %collective-permute-done.5.a_ref, bf16[32,4608]{1,0:T(8,128)(2,1)S(1)} %collective-permute-done.7.b_ref, bf16[32,4608]{1,0:T(8,128)(2,1)S(1)} %collective-permute-done.8.c_ref, ...), custom_call_target="tpu_custom_call", output_to_operand_aliasing={{}: (5, {})} | custom-call | tf_op jit(solution)/shard_map/restore/pallas_call | solution.py:231
  (3 shorter events, 0.1 us)
Async XLA Ops:
  4.4 7.1 %collective-permute-start = (bf16[128,4608]{1,0:T(8,128)(2,1)S(1)}, bf16[128,4608]{1,0:T(8,128)(2,1)S(1)}, u32[]{:S(2)}, u32[]{:S(2)}) collective-permute-start(bf16[128,4608]{1,0:T(8,128)(2,1)S(1)} %compensate.3), channel_id=1, source_target_pairs={{0,16},{1,17},{2,18},{3,19},{4,20},{5,21},{6,22},{7,23},{8,24},{9,... | collective-permute-start | bytes 3538952 | tf_op jit(solution)/shard_map/ppermute | solution.py:61
  11.5 22.2 %copy-start = (f32[1,1,4608]{2,1,0:T(1,128)S(1)}, f32[1,1,4608]{2,1,0:T(1,128)}, u32[]{:S(2)}) copy-start(f32[1,1,4608]{2,1,0:T(1,128)} %param.9) | copy-start | bytes 55300
  11.5 22.3 %copy-start.1 = (f32[1,1,4608]{2,1,0:T(1,128)S(1)}, f32[1,1,4608]{2,1,0:T(1,128)}, u32[]{:S(2)}) copy-start(f32[1,1,4608]{2,1,0:T(1,128)} %param.10) | copy-start | bytes 55300
  11.5 22.3 %copy-start.2 = (f32[1,1,4608]{2,1,0:T(1,128)S(1)}, f32[1,1,4608]{2,1,0:T(1,128)}, u32[]{:S(2)}) copy-start(f32[1,1,4608]{2,1,0:T(1,128)} %param.11) | copy-start | bytes 55300
  11.8 10.3 %collective-permute-start.1 = (bf16[32,4608]{1,0:T(8,128)(2,1)S(1)}, bf16[32,4608]{1,0:T(8,128)(2,1)S(1)}, u32[]{:S(2)}, u32[]{:S(2)}) collective-permute-start(bf16[32,4608]{1,0:T(8,128)(2,1)S(1)} %get-tuple-element.14), channel_id=1, source_target_pairs={{0,1},{1,2},{2,3},{3,0},{4,5},{5,6},{6,7},{7,4},{8,9},{9,10},{10,1... | collective-permute-start | bytes 884744 | tf_op jit(solution)/shard_map/ppermute | solution.py:57
  11.9 10.2 %collective-permute-start.2 = (bf16[32,4608]{1,0:T(8,128)(2,1)S(1)}, bf16[32,4608]{1,0:T(8,128)(2,1)S(1)}, u32[]{:S(2)}, u32[]{:S(2)}) collective-permute-start(bf16[32,4608]{1,0:T(8,128)(2,1)S(1)} %get-tuple-element.15), channel_id=1, source_target_pairs={{0,2},{1,3},{2,0},{3,1},{4,6},{5,7},{6,4},{7,5},{8,10},{9,11},{10,... | collective-permute-start | bytes 884744 | tf_op jit(solution)/shard_map/ppermute | solution.py:57
  14.1 8.7 %collective-permute-start.3 = (bf16[32,4608]{1,0:T(8,128)(2,1)S(1)}, bf16[32,4608]{1,0:T(8,128)(2,1)S(1)}, u32[]{:S(2)}, u32[]{:S(2)}) collective-permute-start(bf16[32,4608]{1,0:T(8,128)(2,1)S(1)} %get-tuple-element.16), channel_id=1, source_target_pairs={{0,3},{1,0},{2,1},{3,2},{4,7},{5,4},{6,5},{7,6},{8,11},{9,8},{10,9... | collective-permute-start | bytes 884744 | tf_op jit(solution)/shard_map/ppermute | solution.py:57
  24.1 20.3 %all-to-all-start = ((bf16[32,36,128]{2,1,0:T(8,128)(2,1)}), bf16[32,36,128]{2,1,0:T(8,128)(2,1)S(1)}, u32[]{:S(2)}, u32[]{:S(2)}) async-start(bf16[32,36,128]{2,1,0:T(8,128)(2,1)} %first_sum.1), calls=%async_computation | async-start | bytes 655360 | tf_op jit(solution)/shard_map/all_to_all | solution.py:71
  63.4 11.5 %collective-permute-start.4 = (bf16[32,4608]{1,0:T(8,128)(2,1)S(1)}, bf16[32,4608]{1,0:T(8,128)(2,1)S(1)}, u32[]{:S(2)}, u32[]{:S(2)}) collective-permute-start(bf16[32,4608]{1,0:T(8,128)(2,1)S(1)} %line_rows.1.a_ref), channel_id=1, source_target_pairs={{0,2},{1,3},{2,0},{3,1},{4,6},{5,7},{6,4},{7,5},{8,10},{9,11},{10,... | collective-permute-start | bytes 884744 | tf_op jit(solution)/shard_map/ppermute | solution.py:57
  66.2 8.8 %collective-permute-start.9 = (bf16[32,4608]{1,0:T(8,128)(2,1)S(1)}, bf16[32,4608]{1,0:T(8,128)(2,1)S(1)}, u32[]{:S(2)}, u32[]{:S(2)}) collective-permute-start(bf16[32,4608]{1,0:T(8,128)(2,1)S(1)} %line_rows.1.a_ref), channel_id=1, source_target_pairs={{0,1},{1,2},{2,3},{3,0},{4,5},{5,6},{6,7},{7,4},{8,9},{9,10},{10,1... | collective-permute-start | bytes 884744 | tf_op jit(solution)/shard_map/ppermute | solution.py:57
  66.2 12.7 %collective-permute-start.6 = (bf16[32,4608]{1,0:T(8,128)(2,1)S(1)}, bf16[32,4608]{1,0:T(8,128)(2,1)S(1)}, u32[]{:S(2)}, u32[]{:S(2)}) collective-permute-start(bf16[32,4608]{1,0:T(8,128)(2,1)S(1)} %line_rows.1.a_ref), channel_id=1, source_target_pairs={{0,3},{1,0},{2,1},{3,2},{4,7},{5,4},{6,5},{7,6},{8,11},{9,8},{10,9... | collective-permute-start | bytes 884744 | tf_op jit(solution)/shard_map/ppermute | solution.py:57
  70.1 10.6 %collective-permute-start.5 = (bf16[32,4608]{1,0:T(8,128)(2,1)S(1)}, bf16[32,4608]{1,0:T(8,128)(2,1)S(1)}, u32[]{:S(2)}, u32[]{:S(2)}) collective-permute-start(bf16[32,4608]{1,0:T(8,128)(2,1)S(1)} %line_rows.1.a_ref), channel_id=1, source_target_pairs={{0,16},{1,17},{2,18},{3,19},{4,20},{5,21},{6,22},{7,23},{8,24},{9,... | collective-permute-start | bytes 884744 | tf_op jit(solution)/shard_map/ppermute | solution.py:61
  75.0 5.7 %collective-permute-start.10 = (bf16[32,4608]{1,0:T(8,128)(2,1)S(1)}, bf16[32,4608]{1,0:T(8,128)(2,1)S(1)}, u32[]{:S(2)}, u32[]{:S(2)}) collective-permute-start(bf16[32,4608]{1,0:T(8,128)(2,1)S(1)} %collective-permute-done.9.d_ref), channel_id=1, source_target_pairs={{0,16},{1,17},{2,18},{3,19},{4,20},{5,21},{6,22},{7,23},{8,24},{9,... | collective-permute-start | bytes 884744 | tf_op jit(solution)/shard_map/ppermute | solution.py:61
  78.9 1.8 %collective-permute-start.7 = (bf16[32,4608]{1,0:T(8,128)(2,1)S(1)}, bf16[32,4608]{1,0:T(8,128)(2,1)S(1)}, u32[]{:S(2)}, u32[]{:S(2)}) collective-permute-start(bf16[32,4608]{1,0:T(8,128)(2,1)S(1)} %collective-permute-done.6.b_ref), channel_id=1, source_target_pairs={{0,16},{1,17},{2,18},{3,19},{4,20},{5,21},{6,22},{7,23},{8,24},{9,... | collective-permute-start | bytes 884744 | tf_op jit(solution)/shard_map/ppermute | solution.py:61
  78.9 2.0 %collective-permute-start.8 = (bf16[32,4608]{1,0:T(8,128)(2,1)S(1)}, bf16[32,4608]{1,0:T(8,128)(2,1)S(1)}, u32[]{:S(2)}, u32[]{:S(2)}) collective-permute-start(bf16[32,4608]{1,0:T(8,128)(2,1)S(1)} %collective-permute-done.4.c_ref), channel_id=1, source_target_pairs={{0,16},{1,17},{2,18},{3,19},{4,20},{5,21},{6,22},{7,23},{8,24},{9,... | collective-permute-start | bytes 884744 | tf_op jit(solution)/shard_map/ppermute | solution.py:61

commit v4 on v3

v4 whole, which is shorter than its diff:
```python
import functools

import jax
import jax.numpy as jnp
from jax import lax
from jax.experimental import pallas as pl
from jax.experimental.pallas import tpu as pltpu
from jax.sharding import Mesh
from jax.sharding import PartitionSpec as P

beta_one = 0.9
beta_two = 0.999
adam_count = 100.0
adam_epsilon = 1e-08
learn_rate = 0.02

AXES = ("y", "zh", "core", "zl", "x")
SIZES = (4, 2, 2, 4, 4)
ROWS = 128
WIDTH = 9216
HALF = WIDTH // 2
LANES = 128
CHUNKS = 3
CHUNK = HALF // CHUNKS
PER_CHUNK = CHUNK // LANES
SLAB_ROWS = HALF // LANES
SLAB = (2, HALF // 2)
F32 = jnp.float32
BF16 = jnp.bfloat16
VMEM_LIMIT = 32 * 1024 * 1024
WHOLE = pl.BlockSpec(memory_space=pltpu.VMEM)
SCALAR = pl.BlockSpec(memory_space=pltpu.SMEM)
FAR = pl.BlockSpec(memory_space=pltpu.HBM)


def params():
    return pltpu.CompilerParams(vmem_limit_bytes=VMEM_LIMIT)


def in_hbm(array):
    return pltpu.with_memory_space_constraint(array, pltpu.HBM)


def device(x, y, z, core):
    return (((y * 2 + z // 4) * 2 + core) * 4 + z % 4) * 4 + x


def paired(core, pair, which):
    return (2 * pair + core + which) % 8


def large_groups():
    groups = [[device(x, y, paired(0, p, k), 0) for x in range(4) for k in range(2)] for y in range(4) for p in range(4)]
    return groups + [[device(x, y, paired(1, p, k), 1) for y in range(4) for k in range(2)] for x in range(4) for p in range(4)]


def small_groups():
    groups = [[device(x, y, paired(0, p, k), 0) for y in range(4) for p in range(4)] for x in range(4) for k in range(2)]
    return groups + [[device(x, y, paired(1, p, k), 1) for x in range(4) for p in range(4)] for y in range(4) for k in range(2)]


SWAP = [(i, i ^ 16) for i in range(256)]


def swap_cores(array):
    return lax.ppermute(array, AXES, SWAP)


def exchange(array, groups):
    return lax.all_to_all(array, AXES, 0, 0, axis_index_groups=groups, tiled=True)


def order(half, transposed):
    sent = lax.broadcasted_iota(jnp.int32, (ROWS, ROWS), 1 if transposed else 0)
    flat = lax.broadcasted_iota(jnp.int32, (ROWS, ROWS), 0 if transposed else 1)
    a, k, b, p = sent // 32, sent // 16 % 2, sent // 4 % 4, sent % 4
    z = (2 * p + k + half) % 8
    a_step = jnp.where(half == 0, 8, 2)
    return (z % 4 * 32 + a * a_step + b * (10 - a_step) + z // 4 == flat).astype(F32).astype(BF16)


def compensate_kernel(other, core_ref, codes_hbm, scales_hbm, feedback_hbm, out_ref, codes, scales, feedback, turned, summed, sems):
    core = core_ref[0]
    half = 1 - core if other else core
    copies = [pltpu.make_async_copy(scales_hbm, scales, sems.at[2 * CHUNKS])]
    for i in range(CHUNKS):
        columns = pl.ds(pl.multiple_of(half * HALF + i * CHUNK, LANES), CHUNK)
        copies.append(pltpu.make_async_copy(codes_hbm.at[:, columns], codes.at[i], sems.at[2 * i]))
        copies.append(pltpu.make_async_copy(feedback_hbm.at[:, columns], feedback.at[i], sems.at[2 * i + 1]))
    for copy in copies:
        copy.start()
    moved = order(half, False)
    copies[0].wait()
    turned[0:SLAB_ROWS, :] = scales[pl.ds(half * SLAB_ROWS, SLAB_ROWS), :]
    scale = turned[...].T
    for i in range(CHUNKS):
        copies[1 + 2 * i].wait()
        copies[2 + 2 * i].wait()
        for block in range(PER_CHUNK):
            columns = slice(block * LANES, (block + 1) * LANES)
            at = i * PER_CHUNK + block
            dequant = codes[i, :, columns].astype(F32) * scale[:, at : at + 1]
            summed[i, :, columns] = (dequant + feedback[i, :, columns].astype(F32)).astype(BF16)
    for i in range(CHUNKS):
        out_ref[:, i * CHUNK : (i + 1) * CHUNK] = jnp.dot(moved, summed[i], preferred_element_type=F32).astype(BF16)


def compensate(other, core, codes, scales, feedback):
    return pl.pallas_call(
        functools.partial(compensate_kernel, other),
        out_shape=jax.ShapeDtypeStruct((ROWS, HALF), BF16),
        in_specs=[SCALAR, FAR, FAR, FAR],
        out_specs=WHOLE,
        scratch_shapes=[
            pltpu.VMEM((CHUNKS, ROWS, CHUNK), jnp.int32),
            pltpu.VMEM((WIDTH // LANES, ROWS), F32),
            pltpu.VMEM((CHUNKS, ROWS, CHUNK), BF16),
            pltpu.VMEM((ROWS, LANES), F32),
            pltpu.VMEM((CHUNKS, ROWS, CHUNK), BF16),
            pltpu.SemaphoreType.DMA((2 * CHUNKS + 1,)),
        ],
        compiler_params=params(),
        cost_estimate=pl.CostEstimate(flops=2 * ROWS * ROWS * HALF, bytes_accessed=8 * ROWS * HALF, transcendentals=0),
        name="compensate",
    )(core, in_hbm(codes), in_hbm(scales), in_hbm(feedback))


def pair_sum_kernel(own_ref, other_ref, out_ref):
    for piece in range(8):
        rows = slice(piece * 16, (piece + 1) * 16)
        out_ref[piece] = (own_ref[rows, :].astype(F32) + other_ref[rows, :].astype(F32)).astype(BF16)


def pair_sum(own, other):
    return pl.pallas_call(
        pair_sum_kernel,
        out_shape=jax.ShapeDtypeStruct((8, 16, HALF), BF16),
        in_specs=[WHOLE] * 2,
        out_specs=WHOLE,
        compiler_params=params(),
        name="pair_sum",
    )(own, other)


def group_sum_kernel(in_ref, out_ref):
    for block in range(SLAB_ROWS):
        columns = slice(block * LANES, (block + 1) * LANES)
        out_ref[:, columns] = jnp.sum(in_ref[:, :, columns].astype(F32), axis=0).astype(BF16)


def group_sum(arrived):
    return pl.pallas_call(
        group_sum_kernel,
        out_shape=jax.ShapeDtypeStruct((16, HALF), BF16),
        in_specs=[WHOLE],
        out_specs=WHOLE,
        compiler_params=params(),
        name="group_sum",
    )(arrived)


def adam_kernel(arrived_ref, master_ref, moment_ref, second_ref, dir_ref, new_ref, copies_ref):
    total = jnp.sum(arrived_ref[...].astype(F32), axis=0)
    grad = jnp.concatenate([total[0:1], total[1:2]], axis=1) / 256.0
    first = beta_one * moment_ref[...] + (1.0 - beta_one) * grad
    squared = beta_two * second_ref[...] + (1.0 - beta_two) * grad * grad
    first_hat = first / (1.0 - beta_one**adam_count)
    squared_hat = squared / (1.0 - beta_two**adam_count)
    adam_dir = first_hat / (jnp.sqrt(squared_hat) + adam_epsilon)
    new_master = master_ref[...] - learn_rate * adam_dir
    dir_ref[...] = adam_dir
    new_ref[...] = new_master
    rows = jnp.concatenate([new_master[:, : SLAB[1]], new_master[:, SLAB[1] :]], axis=0)
    copies_ref[...] = jnp.broadcast_to(rows.astype(BF16)[None], copies_ref.shape)


def adam(arrived, master, moment, second):
    slab = jax.ShapeDtypeStruct((1, HALF), F32)
    return pl.pallas_call(
        adam_kernel,
        out_shape=(slab, slab, jax.ShapeDtypeStruct((16, *SLAB), BF16)),
        in_specs=[WHOLE] * 4,
        out_specs=[WHOLE] * 3,
        compiler_params=params(),
        name="adam",
    )(arrived, master, moment, second)


def copies_kernel(in_ref, out_ref):
    out_ref[...] = jnp.broadcast_to(in_ref[...][None], out_ref.shape)


def copies_of(rows):
    return pl.pallas_call(
        copies_kernel,
        out_shape=jax.ShapeDtypeStruct((8, 16, HALF), BF16),
        in_specs=[WHOLE],
        out_specs=WHOLE,
        compiler_params=params(),
        name="copies_of",
    )(rows)


def place_half(half, rows_ref, weights_hbm, staged, sems):
    moved = order(half, True)
    copies = []
    for i in range(CHUNKS):
        rows = rows_ref[:, i * CHUNK : (i + 1) * CHUNK]
        staged[i] = jnp.dot(moved, rows, preferred_element_type=F32).astype(BF16)
        to = pl.ds(pl.multiple_of(half * HALF + i * CHUNK, LANES), CHUNK)
        copies.append(pltpu.make_async_copy(staged.at[i], weights_hbm.at[:, to], sems.at[i]))
        copies[-1].start()
    return copies


def restore_own_kernel(core_ref, rows_ref, dir_ref, new_ref, weights_hbm, dir_hbm, new_hbm, staged, sems):
    copies = [
        pltpu.make_async_copy(dir_ref, dir_hbm, sems.at[CHUNKS]),
        pltpu.make_async_copy(new_ref, new_hbm, sems.at[CHUNKS + 1]),
    ]
    for copy in copies:
        copy.start()
    for copy in copies + place_half(core_ref[0], rows_ref, weights_hbm, staged, sems):
        copy.wait()


def restore_own(core, rows, adam_dir, new_master):
    slab = jax.ShapeDtypeStruct((1, HALF), F32)
    return pl.pallas_call(
        restore_own_kernel,
        out_shape=(jax.ShapeDtypeStruct((ROWS, WIDTH), BF16), slab, slab),
        in_specs=[SCALAR] + [WHOLE] * 3,
        out_specs=[FAR] * 3,
        scratch_shapes=[pltpu.VMEM((CHUNKS, ROWS, CHUNK), BF16), pltpu.SemaphoreType.DMA((CHUNKS + 2,))],
        compiler_params=params(),
        name="restore_own",
    )(core, rows, adam_dir, new_master)


def restore_other_kernel(core_ref, rows_ref, held_hbm, weights_hbm, staged, sems):
    for copy in place_half(1 - core_ref[0], rows_ref, weights_hbm, staged, sems):
        copy.wait()


def restore_other(core, rows, weights):
    return pl.pallas_call(
        restore_other_kernel,
        out_shape=jax.ShapeDtypeStruct((ROWS, WIDTH), BF16),
        in_specs=[SCALAR, WHOLE, FAR],
        out_specs=FAR,
        scratch_shapes=[pltpu.VMEM((CHUNKS, ROWS, CHUNK), BF16), pltpu.SemaphoreType.DMA((CHUNKS,))],
        input_output_aliases={2: 0},
        compiler_params=params(),
        name="restore_other",
    )(core, rows, weights)


def shards(grad_codes, scales, feedback, master, moment, second):
    core = lax.axis_index("core").astype(jnp.int32).reshape(1)
    codes, feed = grad_codes[0, 0], feedback[0, 0]
    turned = jnp.swapaxes(scales[0, 0], 0, 1)
    given = compensate(True, core, codes, turned, feed)
    taken = swap_cores(given)
    kept = compensate(False, core, codes, turned, feed)
    partial = group_sum(exchange(pair_sum(kept, taken), large_groups()))
    arrived = exchange(partial.reshape(16, *SLAB), small_groups())
    adam_dir, new_master, copies = adam(arrived, master[0], moment[0], second[0])
    rows = exchange(copies, small_groups()).reshape(16, HALF)
    mine = exchange(copies_of(rows), large_groups()).reshape(ROWS, HALF)
    theirs = swap_cores(mine)
    weights, adam_dir, new_master = restore_own(core, mine, adam_dir, new_master)
    weights = restore_other(core, theirs, weights)
    return adam_dir[None], new_master[None], weights


def solution(mesh):
    fine = Mesh(mesh.devices.reshape(SIZES), AXES)
    wide, node = ("y", "zh", "core"), ("zl", "x")
    placed = (
        P(wide, node, None, None),
        P(wide, node, None, None),
        P(wide, node, None, None),
        P(node, wide, None),
        P(node, wide, None),
        P(node, wide, None),
    )
    return jax.shard_map(
        shards,
        mesh=fine,
        in_specs=placed,
        out_specs=(P(node, wide, None), P(node, wide, None), P()),
        check_vma=False,
    )
```

time: 82.4 us -> 80.4 us (0.976)
  blocking collectives: 18.2 us -> 63.3 us
  starting transfers between devices: 31 us -> 6.38 us
  waiting for transfers between devices: 18.3 us -> 1.16 us
  Pallas kernels: 12.4 us -> 8.53 us
  local copies, waits for them, and re-layouts: 1.27 us -> 0.07 us
    all_to_all x1 -> x4, blocking collectives: 18.2 us -> 63.3 us  [exchange(): lax.all_to_all(array, AXES, 0, 0, axis_index_groups=groups, tiled=True)]
    all_to_all x1 -> x0, waiting for transfers between devices: 10.5 us -> none  [exchange(): lax.all_to_all(array, AXES, 0, 0, axis_index_groups=owner_groups(), tiled...]
    all_to_all x1 -> x0, starting transfers between devices: 9.63 us -> none  [exchange(): lax.all_to_all(array, AXES, 0, 0, axis_index_groups=owner_groups(), tiled...]
    ppermute x6 -> x0, starting transfers between devices: 8.76 us -> none  [send(): return lax.ppermute(array, AXES, shifted(step))]
    ppermute x6 -> x0, waiting for transfers between devices: 7.62 us -> none  [send(): return lax.ppermute(array, AXES, shifted(step))]
    ppermute x5 -> x2, starting transfers between devices: 12.6 us -> 6.38 us  [swap_cores(): return lax.ppermute(array, AXES, SWAP)]
    pallas_call x2, Pallas kernels: 7.54 us -> 5.2 us  [compensate(): pl.pallas_call(functools.partial(compensate_kernel, other), out_shape=jax...]
    pallas_call x5, Pallas kernels: 4.79 us -> 3.11 us  [the longest x1 1.31 us: restore_own(): pl.pallas_call(restore_own_kernel, out_shape=(jax.ShapeDtypeStruct((ROWS,...]
  transfers between devices with their start and end apart: 12 -> 2, of which waited for: 4 -> 1; matrix products, arithmetic and copies ran while one was open for 2% -> 0% of each run, Pallas kernels for 6% -> 5%
where the time goes in v4:
time: 80.4 us; the launch traced here: 80.1 us
  blocking collectives  63.3 us (79%)
  Pallas kernels  8.53 us (11%)
  starting transfers between devices  6.38 us (8%)
  waiting for transfers between devices  1.16 us (1%)
    all_to_all x4, blocking collectives, exchange(): lax.all_to_all(array, AXES, 0, 0, axis_index_groups=groups, tiled=True)  63.3 us
    ppermute x2, starting transfers between devices, swap_cores(): return lax.ppermute(array, AXES, SWAP)  6.38 us
    pallas_call x2, Pallas kernels, compensate(): pl.pallas_call(functools.partial(compensate_kernel, other), out_shape=jax...  5.2 us
  transfers between devices with their start and end apart: 2, of which 1 were waited for; matrix products, arithmetic and copies ran while one was open for 0% of the time, Pallas kernels for 5%

profile of v4, /device:TPU:1, one launch (start us, length us, event | category | flops | bytes accessed | tf_op | source)
XLA Modules:
  0.0 80.1 jit_solution(11380184213494545917)
XLA Ops:
  0.6 2.6 %compensate.3 = bf16[128,4608]{1,0:T(8,128)(2,1)S(1)} custom-call(s32[1]{0:T(128)} %bitcast.core_ref, s32[128,9216]{1,0:T(8,128)} %bitcast.20, f32[72,128]{1,0:T(8,128)} %bitcast.25, bf16[128,9216]{1,0:T(8,128)(2,1)} %bitcast.22), custom_call_target="tpu_custom_call" | custom-call | flops 150994944 | bytes 4718592 | tf_op jit(solution)/shard_map/compensate/pallas_call | solution.py:109
  3.2 3.3 %collective-permute-start = (bf16[128,4608]{1,0:T(8,128)(2,1)S(1)}, bf16[128,4608]{1,0:T(8,128)(2,1)S(1)}, u32[]{:S(2)}, u32[]{:S(2)}) collective-permute-start(bf16[128,4608]{1,0:T(8,128)(2,1)S(1)} %compensate.3), channel_id=1, source_target_pairs={{0,16},{1,17},{2,18},{3,19},{4,20},{5,21},{6,22},{7,23},{8,24},{9,... | collective-permute-start | bytes 3538952 | tf_op jit(solution)/shard_map/ppermute | solution.py:66
  6.6 2.6 %compensate.2.own_ref = bf16[128,4608]{1,0:T(8,128)(2,1)S(1)} custom-call(s32[1]{0:T(128)} %bitcast.core_ref, s32[128,9216]{1,0:T(8,128)} %bitcast.21, f32[72,128]{1,0:T(8,128)} %bitcast.26, bf16[128,9216]{1,0:T(8,128)(2,1)} %bitcast.23), custom_call_target="tpu_custom_call" | custom-call | flops 150994944 | bytes 4718592 | tf_op jit(solution)/shard_map/compensate/pallas_call | solution.py:109
  9.2 0.0 collective-permute-done.other_ref
  9.2 0.3 pair_sum.1
  9.5 18.0 %all_to_all.20.in_ref = bf16[8,16,4608]{2,1,0:T(8,128)(2,1)S(1)} all-to-all(bf16[8,16,4608]{2,1,0:T(8,128)(2,1)S(1)} %pair_sum.1), channel_id=1, replica_groups={{0,4,1,5,2,6,3,7},{8,12,9,13,10,14,11,15},{32,36,33,37,34,38,35,39},{40..., dimensions={0} | all-to-all | bytes 2359296 | tf_op jit(solution)/shard_map/all_to_all | solution.py:70
  27.5 0.0 copy-start
  27.5 0.0 copy-start.1
  27.5 0.0 copy-start.2
  27.5 0.2 group_sum.1
  27.7 16.7 %all_to_all.21.arrived_ref = bf16[16,2,2304]{2,1,0:T(2,128)(2,1)S(1)} all-to-all(bf16[16,2,2304]{2,1,0:T(2,128)(2,1)S(1)} %reshape.19), channel_id=1, replica_groups={{0,8,32,40,64,72,96,104,128,136,160,168,192,200,224,232},{4,12,36,44,68..., dimensions={0} | all-to-all | bytes 294912 | tf_op jit(solution)/shard_map/all_to_all | solution.py:70
  44.3 0.0 copy-done
  44.3 0.0 copy-done.1
  44.3 0.0 copy-done.2
  44.3 0.2 adam.1
  44.6 14.4 %all_to_all.22 = bf16[16,2,2304]{2,1,0:T(2,128)(2,1)S(1)} all-to-all(bf16[16,2,2304]{2,1,0:T(2,128)(2,1)S(1)} %get-tuple-element.9), channel_id=1, replica_groups={{0,8,32,40,64,72,96,104,128,136,160,168,192,200,224,232},{4,12,36,44,68..., dimensions={0} | all-to-all | bytes 294912 | tf_op jit(solution)/shard_map/all_to_all | solution.py:70
  59.0 0.1 copies_of.1
  59.1 14.2 %all_to_all.23 = bf16[8,16,4608]{2,1,0:T(8,128)(2,1)S(1)} all-to-all(bf16[8,16,4608]{2,1,0:T(8,128)(2,1)S(1)} %copies_of.1), channel_id=1, replica_groups={{0,4,1,5,2,6,3,7},{8,12,9,13,10,14,11,15},{32,36,33,37,34,38,35,39},{40..., dimensions={0} | all-to-all | bytes 2359296 | tf_op jit(solution)/shard_map/all_to_all | solution.py:70
  73.3 3.1 %collective-permute-start.1 = (bf16[128,4608]{1,0:T(8,128)(2,1)S(1)}, bf16[128,4608]{1,0:T(8,128)(2,1)S(1)}, u32[]{:S(2)}, u32[]{:S(2)}) collective-permute-start(bf16[128,4608]{1,0:T(8,128)(2,1)S(1)} %bitcast.14), channel_id=1, source_target_pairs={{0,16},{1,17},{2,18},{3,19},{4,20},{5,21},{6,22},{7,23},{8,24},{9,... | collective-permute-start | bytes 3538952 | tf_op jit(solution)/shard_map/ppermute | solution.py:66
  76.3 1.3 %restore_own.1 = (bf16[128,9216]{1,0:T(8,128)(2,1)}, f32[1,4608]{1,0:T(1,128)}, f32[1,4608]{1,0:T(1,128)}) custom-call(s32[1]{0:T(128)} %bitcast.core_ref, bf16[128,4608]{1,0:T(8,128)(2,1)S(1)} %bitcast.15, f32[1,4608]{1,0:T(1,128)S(1)} %get-tuple-element.10.dir_ref, f32[1,4608]{1,0:T(1,128)S(1)} %get-tuple-element.11.new_ref), custom_call_target="tpu_custom_call" | custom-call | tf_op jit(solution)/shard_map/restore_own/pallas_call | solution.py:229
  77.7 1.2 %collective-permute-done.1.rows_ref = bf16[128,4608]{1,0:T(8,128)(2,1)S(1)} collective-permute-done((bf16[128,4608]{1,0:T(8,128)(2,1)S(1)}, bf16[128,4608]{1,0:T(8,128)(2,1)S(1)}, u32[]{:S(2)}, u32[]{:S(2)}) %collective-permute-start.1) | collective-permute-done | bytes 1179680 | tf_op jit(solution)/shard_map/ppermute | solution.py:66
  78.8 1.3 %restore_other.1 = bf16[128,9216]{1,0:T(8,128)(2,1)} custom-call(s32[1]{0:T(128)} %bitcast.core_ref, bf16[128,4608]{1,0:T(8,128)(2,1)S(1)} %collective-permute-done.1.rows_ref, bf16[128,9216]{1,0:T(8,128)(2,1)} %get-tuple-element.14.held_hbm), custom_call_target="tpu_custom_call", output_to_operand_aliasing={{}: (2, {})} | custom-call | tf_op jit(solution)/shard_map/restore_other/pallas_call | solution.py:246
  (2 shorter events, 0.1 us)
Async XLA Ops:
  3.2 5.9 %collective-permute-start = (bf16[128,4608]{1,0:T(8,128)(2,1)S(1)}, bf16[128,4608]{1,0:T(8,128)(2,1)S(1)}, u32[]{:S(2)}, u32[]{:S(2)}) collective-permute-start(bf16[128,4608]{1,0:T(8,128)(2,1)S(1)} %compensate.3), channel_id=1, source_target_pairs={{0,16},{1,17},{2,18},{3,19},{4,20},{5,21},{6,22},{7,23},{8,24},{9,... | collective-permute-start | bytes 3538952 | tf_op jit(solution)/shard_map/ppermute | solution.py:66
  27.5 16.9 %copy-start = (f32[1,1,4608]{2,1,0:T(1,128)S(1)}, f32[1,1,4608]{2,1,0:T(1,128)}, u32[]{:S(2)}) copy-start(f32[1,1,4608]{2,1,0:T(1,128)} %param.9) | copy-start | bytes 55300
  27.5 16.9 %copy-start.1 = (f32[1,1,4608]{2,1,0:T(1,128)S(1)}, f32[1,1,4608]{2,1,0:T(1,128)}, u32[]{:S(2)}) copy-start(f32[1,1,4608]{2,1,0:T(1,128)} %param.10) | copy-start | bytes 55300
  27.5 16.9 %copy-start.2 = (f32[1,1,4608]{2,1,0:T(1,128)S(1)}, f32[1,1,4608]{2,1,0:T(1,128)}, u32[]{:S(2)}) copy-start(f32[1,1,4608]{2,1,0:T(1,128)} %param.11) | copy-start | bytes 55300
  73.3 5.5 %collective-permute-start.1 = (bf16[128,4608]{1,0:T(8,128)(2,1)S(1)}, bf16[128,4608]{1,0:T(8,128)(2,1)S(1)}, u32[]{:S(2)}, u32[]{:S(2)}) collective-permute-start(bf16[128,4608]{1,0:T(8,128)(2,1)S(1)} %bitcast.14), channel_id=1, source_target_pairs={{0,16},{1,17},{2,18},{3,19},{4,20},{5,21},{6,22},{7,23},{8,24},{9,... | collective-permute-start | bytes 3538952 | tf_op jit(solution)/shard_map/ppermute | solution.py:66

commit v5 on v4

--- a/solution.py
+++ b/solution.py
@@ -59,6 +59,21 @@
     return groups + [[device(x, y, paired(1, p, k), 1) for x in range(4) for p in range(4)] for y in range(4) for k in range(2)]
 
 
+def owner_groups():
+    lines = [(zl + 4 * zh) for zl in range(4) for zh in range(2)]
+    groups = [[device(x, y, z, 0) for y in range(4) for z in lines] for x in range(4)]
+    return groups + [[device(x, y, z, 1) for x in range(4) for z in lines] for y in range(4)]
+
+
+def shifted(step):
+    pairs = []
+    for i in range(256):
+        x, zl, core, zh, y = i % 4, i // 4 % 4, i // 16 % 2, i // 32 % 2, i // 64
+        z = zl + 4 * zh
+        pairs.append((i, device(x, (y + step) % 4, z, 1) if core else device((x + step) % 4, y, z, 0)))
+    return pairs
+
+
 SWAP = [(i, i ^ 16) for i in range(256)]
 
 
@@ -66,21 +81,33 @@
     return lax.ppermute(array, AXES, SWAP)
 
 
+def send(array, step):
+    return lax.ppermute(array, AXES, shifted(step))
+
+
 def exchange(array, groups):
     return lax.all_to_all(array, AXES, 0, 0, axis_index_groups=groups, tiled=True)
 
 
-def order(half, transposed):
-    sent = lax.broadcasted_iota(jnp.int32, (ROWS, ROWS), 1 if transposed else 0)
-    flat = lax.broadcasted_iota(jnp.int32, (ROWS, ROWS), 0 if transposed else 1)
+def sent_order(place, half):
+    sent = lax.broadcasted_iota(jnp.int32, (ROWS, ROWS), 0)
+    flat = lax.broadcasted_iota(jnp.int32, (ROWS, ROWS), 1)
+    own, a_step = jnp.where(half == 0, place % 4, place // 64), jnp.where(half == 0, 8, 2)
+    a, b = (sent // 32 + own) % 4, sent // 8 % 4
+    return (sent // 2 % 4 * 32 + a * a_step + b * (10 - a_step) + sent % 2 == flat).astype(F32).astype(BF16)
+
+
+def gathered_order(half):
+    sent = lax.broadcasted_iota(jnp.int32, (ROWS, ROWS), 1)
+    flat = lax.broadcasted_iota(jnp.int32, (ROWS, ROWS), 0)
     a, k, b, p = sent // 32, sent // 16 % 2, sent // 4 % 4, sent % 4
     z = (2 * p + k + half) % 8
     a_step = jnp.where(half == 0, 8, 2)
     return (z % 4 * 32 + a * a_step + b * (10 - a_step) + z // 4 == flat).astype(F32).astype(BF16)
 
 
-def compensate_kernel(other, core_ref, codes_hbm, scales_hbm, feedback_hbm, out_ref, codes, scales, feedback, turned, summed, sems):
-    core = core_ref[0]
+def compensate_kernel(other, place_ref, codes_hbm, scales_hbm, feedback_hbm, out_ref, codes, scales, feedback, turned, spread, summed, sems):
+    core = place_ref[0] // 16 % 2
     half = 1 - core if other else core
     copies = [pltpu.make_async_copy(scales_hbm, scales, sems.at[2 * CHUNKS])]
     for i in range(CHUNKS):
@@ -89,23 +116,24 @@
         copies.append(pltpu.make_async_copy(feedback_hbm.at[:, columns], feedback.at[i], sems.at[2 * i + 1]))
     for copy in copies:
         copy.start()
-    moved = order(half, False)
+    moved = sent_order(place_ref[0], half)
     copies[0].wait()
     turned[0:SLAB_ROWS, :] = scales[pl.ds(half * SLAB_ROWS, SLAB_ROWS), :]
     scale = turned[...].T
+    for at in range(SLAB_ROWS):
+        spread[:, at * LANES : (at + 1) * LANES] = jnp.broadcast_to(scale[:, at : at + 1], (ROWS, LANES))
     for i in range(CHUNKS):
         copies[1 + 2 * i].wait()
         copies[2 + 2 * i].wait()
-        for block in range(PER_CHUNK):
-            columns = slice(block * LANES, (block + 1) * LANES)
-            at = i * PER_CHUNK + block
-            dequant = codes[i, :, columns].astype(F32) * scale[:, at : at + 1]
-            summed[i, :, columns] = (dequant + feedback[i, :, columns].astype(F32)).astype(BF16)
+        columns = slice(i * CHUNK, (i + 1) * CHUNK)
+        dequant = codes[i].astype(F32) * spread[:, columns]
+        summed[:, columns] = (dequant + feedback[i].astype(F32)).astype(BF16)
     for i in range(CHUNKS):
-        out_ref[:, i * CHUNK : (i + 1) * CHUNK] = jnp.dot(moved, summed[i], preferred_element_type=F32).astype(BF16)
-
-
-def compensate(other, core, codes, scales, feedback):
+        columns = slice(i * CHUNK, (i + 1) * CHUNK)
+        out_ref[:, columns] = jnp.dot(moved, summed[:, columns], preferred_element_type=F32).astype(BF16)
+
+
+def compensate(other, place, codes, scales, feedback):
     return pl.pallas_call(
         functools.partial(compensate_kernel, other),
         out_shape=jax.ShapeDtypeStruct((ROWS, HALF), BF16),
@@ -116,47 +144,47 @@
             pltpu.VMEM((WIDTH // LANES, ROWS), F32),
             pltpu.VMEM((CHUNKS, ROWS, CHUNK), BF16),
             pltpu.VMEM((ROWS, LANES), F32),
-            pltpu.VMEM((CHUNKS, ROWS, CHUNK), BF16),
+            pltpu.VMEM((ROWS, HALF), F32),
+            pltpu.VMEM((ROWS, HALF), BF16),
             pltpu.SemaphoreType.DMA((2 * CHUNKS + 1,)),
         ],
         compiler_params=params(),
         cost_estimate=pl.CostEstimate(flops=2 * ROWS * ROWS * HALF, bytes_accessed=8 * ROWS * HALF, transcendentals=0),
         name="compensate",
-    )(core, in_hbm(codes), in_hbm(scales), in_hbm(feedback))
-
-
-def pair_sum_kernel(own_ref, other_ref, out_ref):
-    for piece in range(8):
-        rows = slice(piece * 16, (piece + 1) * 16)
-        out_ref[piece] = (own_ref[rows, :].astype(F32) + other_ref[rows, :].astype(F32)).astype(BF16)
+    )(place, in_hbm(codes), in_hbm(scales), in_hbm(feedback))
+
+
+def pair_sum_kernel(own_ref, other_ref, *out_refs):
+    for piece, out_ref in enumerate(out_refs):
+        rows = slice(piece * 32, (piece + 1) * 32)
+        out_ref[...] = (own_ref[rows, :].astype(F32) + other_ref[rows, :].astype(F32)).astype(BF16)
 
 
 def pair_sum(own, other):
     return pl.pallas_call(
         pair_sum_kernel,
-        out_shape=jax.ShapeDtypeStruct((8, 16, HALF), BF16),
+        out_shape=[jax.ShapeDtypeStruct((32, HALF), BF16)] * 4,
         in_specs=[WHOLE] * 2,
-        out_specs=WHOLE,
+        out_specs=[WHOLE] * 4,
         compiler_params=params(),
         name="pair_sum",
     )(own, other)
 
 
-def group_sum_kernel(in_ref, out_ref):
-    for block in range(SLAB_ROWS):
-        columns = slice(block * LANES, (block + 1) * LANES)
-        out_ref[:, columns] = jnp.sum(in_ref[:, :, columns].astype(F32), axis=0).astype(BF16)
-
-
-def group_sum(arrived):
-    return pl.pallas_call(
-        group_sum_kernel,
-        out_shape=jax.ShapeDtypeStruct((16, HALF), BF16),
-        in_specs=[WHOLE],
+def line_sum_kernel(own_ref, a_ref, b_ref, c_ref, out_ref):
+    total = own_ref[...].astype(F32) + a_ref[...].astype(F32) + b_ref[...].astype(F32) + c_ref[...].astype(F32)
+    out_ref[...] = total.astype(BF16)
+
+
+def line_sum(own, arrived):
+    return pl.pallas_call(
+        line_sum_kernel,
+        out_shape=jax.ShapeDtypeStruct((32, HALF), BF16),
+        in_specs=[WHOLE] * 4,
         out_specs=WHOLE,
         compiler_params=params(),
-        name="group_sum",
-    )(arrived)
+        name="line_sum",
+    )(own, *arrived)
 
 
 def adam_kernel(arrived_ref, master_ref, moment_ref, second_ref, dir_ref, new_ref, copies_ref):
@@ -202,7 +230,7 @@
 
 
 def place_half(half, rows_ref, weights_hbm, staged, sems):
-    moved = order(half, True)
+    moved = gathered_order(half)
     copies = []
     for i in range(CHUNKS):
         rows = rows_ref[:, i * CHUNK : (i + 1) * CHUNK]
@@ -257,13 +285,15 @@
 
 def shards(grad_codes, scales, feedback, master, moment, second):
     core = lax.axis_index("core").astype(jnp.int32).reshape(1)
+    place = lax.axis_index(AXES).astype(jnp.int32).reshape(1)
     codes, feed = grad_codes[0, 0], feedback[0, 0]
     turned = jnp.swapaxes(scales[0, 0], 0, 1)
-    given = compensate(True, core, codes, turned, feed)
+    given = compensate(True, place, codes, turned, feed)
     taken = swap_cores(given)
-    kept = compensate(False, core, codes, turned, feed)
-    partial = group_sum(exchange(pair_sum(kept, taken), large_groups()))
-    arrived = exchange(partial.reshape(16, *SLAB), small_groups())
+    kept = compensate(False, place, codes, turned, feed)
+    own, *others = pair_sum(kept, taken)
+    partial = line_sum(own, [send(others[step - 1], step) for step in (2, 1, 3)])
+    arrived = exchange(partial.reshape(32, *SLAB), owner_groups())
     adam_dir, new_master, copies = adam(arrived, master[0], moment[0], second[0])
     rows = exchange(copies, small_groups()).reshape(16, HALF)
     mine = exchange(copies_of(rows), large_groups()).reshape(ROWS, HALF)

time: 80.4 us -> 79.9 us (level)
  blocking collectives: 63.3 us -> 50.7 us
  waiting for transfers between devices: 1.16 us -> 7.84 us
  starting transfers between devices: 6.38 us -> 11.7 us
    all_to_all x4 -> x3, blocking collectives: 63.3 us -> 50.7 us  [exchange(): lax.all_to_all(array, AXES, 0, 0, axis_index_groups=groups, tiled=True)]
    ppermute x0 -> x3, waiting for transfers between devices: none -> 6.68 us  [send(): return lax.ppermute(array, AXES, shifted(step))]
    ppermute x0 -> x3, starting transfers between devices: none -> 3.94 us  [send(): return lax.ppermute(array, AXES, shifted(step))]
    ppermute x2, starting transfers between devices: 6.38 us -> 7.73 us  [swap_cores(): return lax.ppermute(array, AXES, SWAP)]
  transfers between devices with their start and end apart: 2 -> 5, of which waited for: 1 -> 3; matrix products, arithmetic and copies ran while one was open for 0% -> 0% of each run, Pallas kernels for 5% -> 5%
where the time goes in v5:
time: 79.9 us; the launch traced here: 79.7 us
  blocking collectives  50.7 us (63%)
  starting transfers between devices  11.7 us (15%)
  Pallas kernels  8.61 us (11%)
  waiting for transfers between devices  7.84 us (10%)
    all_to_all x3, blocking collectives, exchange(): lax.all_to_all(array, AXES, 0, 0, axis_index_groups=groups, tiled=True)  50.7 us
    ppermute x2, starting transfers between devices, swap_cores(): return lax.ppermute(array, AXES, SWAP)  7.73 us
    ppermute x3, waiting for transfers between devices, send(): return lax.ppermute(array, AXES, shifted(step))  6.68 us
    pallas_call x2, Pallas kernels, compensate(): pl.pallas_call(functools.partial(compensate_kernel, other), out_shape=jax...  5.15 us
    ppermute x3, starting transfers between devices, send(): return lax.ppermute(array, AXES, shifted(step))  3.94 us
  transfers between devices with their start and end apart: 5, of which 3 were waited for; matrix products, arithmetic and copies ran while one was open for 0% of the time, Pallas kernels for 5%

profile of v5, /device:TPU:1, one launch (start us, length us, event | category | flops | bytes accessed | tf_op | source)
XLA Modules:
  0.0 79.7 jit_solution(14176900042764371234)
XLA Ops:
  0.6 2.6 %compensate.3 = bf16[128,4608]{1,0:T(8,128)(2,1)S(1)} custom-call(s32[1]{0:T(128)} %bitcast.1.place_ref, s32[128,9216]{1,0:T(8,128)} %bitcast.21, f32[72,128]{1,0:T(8,128)} %bitcast.26, bf16[128,9216]{1,0:T(8,128)(2,1)} %bitcast.23), custom_call_target="tpu_custom_call" | custom-call | flops 150994944 | bytes 4718592 | tf_op jit(solution)/shard_map/compensate/pallas_call | solution.py:137
  3.2 3.3 %collective-permute-start = (bf16[128,4608]{1,0:T(8,128)(2,1)S(1)}, bf16[128,4608]{1,0:T(8,128)(2,1)S(1)}, u32[]{:S(2)}, u32[]{:S(2)}) collective-permute-start(bf16[128,4608]{1,0:T(8,128)(2,1)S(1)} %compensate.3), channel_id=1, source_target_pairs={{0,16},{1,17},{2,18},{3,19},{4,20},{5,21},{6,22},{7,23},{8,24},{9,... | collective-permute-start | bytes 3538952 | tf_op jit(solution)/shard_map/ppermute | solution.py:81
  6.6 2.6 %compensate.2.own_ref = bf16[128,4608]{1,0:T(8,128)(2,1)S(1)} custom-call(s32[1]{0:T(128)} %bitcast.1.place_ref, s32[128,9216]{1,0:T(8,128)} %bitcast.22, f32[72,128]{1,0:T(8,128)} %bitcast.27, bf16[128,9216]{1,0:T(8,128)(2,1)} %bitcast.24), custom_call_target="tpu_custom_call" | custom-call | flops 150994944 | bytes 4718592 | tf_op jit(solution)/shard_map/compensate/pallas_call | solution.py:137
  9.1 0.0 collective-permute-done.other_ref
  9.1 0.3 pair_sum.1
  9.4 1.3 %collective-permute-start.1 = (bf16[32,4608]{1,0:T(8,128)(2,1)S(1)}, bf16[32,4608]{1,0:T(8,128)(2,1)S(1)}, u32[]{:S(2)}, u32[]{:S(2)}) collective-permute-start(bf16[32,4608]{1,0:T(8,128)(2,1)S(1)} %get-tuple-element.14), channel_id=1, source_target_pairs={{0,2},{1,3},{2,0},{3,1},{4,6},{5,7},{6,4},{7,5},{8,10},{9,11},{10,... | collective-permute-start | bytes 884744 | tf_op jit(solution)/shard_map/ppermute | solution.py:85
  10.7 0.4 collective-permute-start.2
  11.1 2.3 %collective-permute-start.3 = (bf16[32,4608]{1,0:T(8,128)(2,1)S(1)}, bf16[32,4608]{1,0:T(8,128)(2,1)S(1)}, u32[]{:S(2)}, u32[]{:S(2)}) collective-permute-start(bf16[32,4608]{1,0:T(8,128)(2,1)S(1)} %get-tuple-element.16), channel_id=1, source_target_pairs={{0,3},{1,0},{2,1},{3,2},{4,7},{5,4},{6,5},{7,6},{8,11},{9,8},{10,9... | collective-permute-start | bytes 884744 | tf_op jit(solution)/shard_map/ppermute | solution.py:85
  13.4 3.6 %collective-permute-done.1.a_ref = bf16[32,4608]{1,0:T(8,128)(2,1)S(1)} collective-permute-done((bf16[32,4608]{1,0:T(8,128)(2,1)S(1)}, bf16[32,4608]{1,0:T(8,128)(2,1)S(1)}, u32[]{:S(2)}, u32[]{:S(2)}) %collective-permute-start.1) | collective-permute-done | bytes 294944 | tf_op jit(solution)/shard_map/ppermute | solution.py:85
  16.9 3.1 %collective-permute-done.2.b_ref = bf16[32,4608]{1,0:T(8,128)(2,1)S(1)} collective-permute-done((bf16[32,4608]{1,0:T(8,128)(2,1)S(1)}, bf16[32,4608]{1,0:T(8,128)(2,1)S(1)}, u32[]{:S(2)}, u32[]{:S(2)}) %collective-permute-start.2) | collective-permute-done | bytes 294944 | tf_op jit(solution)/shard_map/ppermute | solution.py:85
  20.0 0.0 collective-permute-done.3.c_ref
  20.0 0.0 copy-start
  20.0 0.0 copy-start.1
  20.1 0.0 copy-start.2
  20.1 0.1 line_sum.1
  20.2 0.1 reshape.23
  20.3 19.7 %all_to_all.15.arrived_ref = bf16[32,2,2304]{2,1,0:T(2,128)(2,1)S(1)} all-to-all(bf16[32,2,2304]{2,1,0:T(2,128)(2,1)S(1)} %reshape.23), channel_id=1, replica_groups={{0,32,4,36,8,40,12,44,64,96,68,100,72,104,76,108,128,160,132,164,136,16..., dimensions={0} | all-to-all | bytes 589824 | tf_op jit(solution)/shard_map/all_to_all | solution.py:89
  40.0 0.0 copy-done
  40.0 0.0 copy-done.1
  40.0 0.0 copy-done.2
  40.0 0.4 adam.1
  40.3 14.2 %all_to_all.16 = bf16[16,2,2304]{2,1,0:T(2,128)(2,1)S(1)} all-to-all(bf16[16,2,2304]{2,1,0:T(2,128)(2,1)S(1)} %get-tuple-element.17), channel_id=1, replica_groups={{0,8,32,40,64,72,96,104,128,136,160,168,192,200,224,232},{4,12,36,44,68..., dimensions={0} | all-to-all | bytes 294912 | tf_op jit(solution)/shard_map/all_to_all | solution.py:89
  54.6 0.1 copies_of.1
  54.7 16.9 %all_to_all.17 = bf16[8,16,4608]{2,1,0:T(8,128)(2,1)S(1)} all-to-all(bf16[8,16,4608]{2,1,0:T(8,128)(2,1)S(1)} %copies_of.1), channel_id=1, replica_groups={{0,4,1,5,2,6,3,7},{8,12,9,13,10,14,11,15},{32,36,33,37,34,38,35,39},{40..., dimensions={0} | all-to-all | bytes 2359296 | tf_op jit(solution)/shard_map/all_to_all | solution.py:89
  71.5 4.4 %collective-permute-start.4 = (bf16[128,4608]{1,0:T(8,128)(2,1)S(1)}, bf16[128,4608]{1,0:T(8,128)(2,1)S(1)}, u32[]{:S(2)}, u32[]{:S(2)}) collective-permute-start(bf16[128,4608]{1,0:T(8,128)(2,1)S(1)} %bitcast.15), channel_id=1, source_target_pairs={{0,16},{1,17},{2,18},{3,19},{4,20},{5,21},{6,22},{7,23},{8,24},{9,... | collective-permute-start | bytes 3538952 | tf_op jit(solution)/shard_map/ppermute | solution.py:81
  75.9 1.3 %restore_own.1 = (bf16[128,9216]{1,0:T(8,128)(2,1)}, f32[1,4608]{1,0:T(1,128)}, f32[1,4608]{1,0:T(1,128)}) custom-call(s32[1]{0:T(128)} %bitcast.core_ref, bf16[128,4608]{1,0:T(8,128)(2,1)S(1)} %bitcast.16, f32[1,4608]{1,0:T(1,128)S(1)} %get-tuple-element.18.dir_ref, f32[1,4608]{1,0:T(1,128)S(1)} %get-tuple-element.19.new_ref), custom_call_target="tpu_custom_call" | custom-call | tf_op jit(solution)/shard_map/restore_own/pallas_call | solution.py:257
  77.2 1.2 %collective-permute-done.4.rows_ref = bf16[128,4608]{1,0:T(8,128)(2,1)S(1)} collective-permute-done((bf16[128,4608]{1,0:T(8,128)(2,1)S(1)}, bf16[128,4608]{1,0:T(8,128)(2,1)S(1)}, u32[]{:S(2)}, u32[]{:S(2)}) %collective-permute-start.4) | collective-permute-done | bytes 1179680 | tf_op jit(solution)/shard_map/ppermute | solution.py:81
  78.4 1.3 %restore_other.1 = bf16[128,9216]{1,0:T(8,128)(2,1)} custom-call(s32[1]{0:T(128)} %bitcast.core_ref, bf16[128,4608]{1,0:T(8,128)(2,1)S(1)} %collective-permute-done.4.rows_ref, bf16[128,9216]{1,0:T(8,128)(2,1)} %get-tuple-element.22.held_hbm), custom_call_target="tpu_custom_call", output_to_operand_aliasing={{}: (2, {})} | custom-call | tf_op jit(solution)/shard_map/restore_other/pallas_call | solution.py:274
  (1 shorter events, 0.0 us)
Async XLA Ops:
  3.2 5.9 %collective-permute-start = (bf16[128,4608]{1,0:T(8,128)(2,1)S(1)}, bf16[128,4608]{1,0:T(8,128)(2,1)S(1)}, u32[]{:S(2)}, u32[]{:S(2)}) collective-permute-start(bf16[128,4608]{1,0:T(8,128)(2,1)S(1)} %compensate.3), channel_id=1, source_target_pairs={{0,16},{1,17},{2,18},{3,19},{4,20},{5,21},{6,22},{7,23},{8,24},{9,... | collective-permute-start | bytes 3538952 | tf_op jit(solution)/shard_map/ppermute | solution.py:81
  9.4 7.5 %collective-permute-start.1 = (bf16[32,4608]{1,0:T(8,128)(2,1)S(1)}, bf16[32,4608]{1,0:T(8,128)(2,1)S(1)}, u32[]{:S(2)}, u32[]{:S(2)}) collective-permute-start(bf16[32,4608]{1,0:T(8,128)(2,1)S(1)} %get-tuple-element.14), channel_id=1, source_target_pairs={{0,2},{1,3},{2,0},{3,1},{4,6},{5,7},{6,4},{7,5},{8,10},{9,11},{10,... | collective-permute-start | bytes 884744 | tf_op jit(solution)/shard_map/ppermute | solution.py:85
  10.7 9.4 %collective-permute-start.2 = (bf16[32,4608]{1,0:T(8,128)(2,1)S(1)}, bf16[32,4608]{1,0:T(8,128)(2,1)S(1)}, u32[]{:S(2)}, u32[]{:S(2)}) collective-permute-start(bf16[32,4608]{1,0:T(8,128)(2,1)S(1)} %get-tuple-element.15), channel_id=1, source_target_pairs={{0,1},{1,2},{2,3},{3,0},{4,5},{5,6},{6,7},{7,4},{8,9},{9,10},{10,1... | collective-permute-start | bytes 884744 | tf_op jit(solution)/shard_map/ppermute | solution.py:85
  11.1 9.0 %collective-permute-start.3 = (bf16[32,4608]{1,0:T(8,128)(2,1)S(1)}, bf16[32,4608]{1,0:T(8,128)(2,1)S(1)}, u32[]{:S(2)}, u32[]{:S(2)}) collective-permute-start(bf16[32,4608]{1,0:T(8,128)(2,1)S(1)} %get-tuple-element.16), channel_id=1, source_target_pairs={{0,3},{1,0},{2,1},{3,2},{4,7},{5,4},{6,5},{7,6},{8,11},{9,8},{10,9... | collective-permute-start | bytes 884744 | tf_op jit(solution)/shard_map/ppermute | solution.py:85
  20.0 19.9 %copy-start = (f32[1,1,4608]{2,1,0:T(1,128)S(1)}, f32[1,1,4608]{2,1,0:T(1,128)}, u32[]{:S(2)}) copy-start(f32[1,1,4608]{2,1,0:T(1,128)} %param.9) | copy-start | bytes 55300
  20.0 19.9 %copy-start.1 = (f32[1,1,4608]{2,1,0:T(1,128)S(1)}, f32[1,1,4608]{2,1,0:T(1,128)}, u32[]{:S(2)}) copy-start(f32[1,1,4608]{2,1,0:T(1,128)} %param.10) | copy-start | bytes 55300
  20.1 19.9 %copy-start.2 = (f32[1,1,4608]{2,1,0:T(1,128)S(1)}, f32[1,1,4608]{2,1,0:T(1,128)}, u32[]{:S(2)}) copy-start(f32[1,1,4608]{2,1,0:T(1,128)} %param.11) | copy-start | bytes 55300
  71.5 6.9 %collective-permute-start.4 = (bf16[128,4608]{1,0:T(8,128)(2,1)S(1)}, bf16[128,4608]{1,0:T(8,128)(2,1)S(1)}, u32[]{:S(2)}, u32[]{:S(2)}) collective-permute-start(bf16[128,4608]{1,0:T(8,128)(2,1)S(1)} %bitcast.15), channel_id=1, source_target_pairs={{0,16},{1,17},{2,18},{3,19},{4,20},{5,21},{6,22},{7,23},{8,24},{9,... | collective-permute-start | bytes 3538952 | tf_op jit(solution)/shard_map/ppermute | solution.py:81

commit v6 on v5

--- a/solution.py
+++ b/solution.py
@@ -45,20 +45,6 @@
     return (((y * 2 + z // 4) * 2 + core) * 4 + z % 4) * 4 + x
 
 
-def paired(core, pair, which):
-    return (2 * pair + core + which) % 8
-
-
-def large_groups():
-    groups = [[device(x, y, paired(0, p, k), 0) for x in range(4) for k in range(2)] for y in range(4) for p in range(4)]
-    return groups + [[device(x, y, paired(1, p, k), 1) for y in range(4) for k in range(2)] for x in range(4) for p in range(4)]
-
-
-def small_groups():
-    groups = [[device(x, y, paired(0, p, k), 0) for y in range(4) for p in range(4)] for x in range(4) for k in range(2)]
-    return groups + [[device(x, y, paired(1, p, k), 1) for x in range(4) for p in range(4)] for y in range(4) for k in range(2)]
-
-
 def owner_groups():
     lines = [(zl + 4 * zh) for zl in range(4) for zh in range(2)]
     groups = [[device(x, y, z, 0) for y in range(4) for z in lines] for x in range(4)]
@@ -89,21 +75,12 @@
     return lax.all_to_all(array, AXES, 0, 0, axis_index_groups=groups, tiled=True)
 
 
-def sent_order(place, half):
-    sent = lax.broadcasted_iota(jnp.int32, (ROWS, ROWS), 0)
-    flat = lax.broadcasted_iota(jnp.int32, (ROWS, ROWS), 1)
+def order(place, half, transposed):
+    sent = lax.broadcasted_iota(jnp.int32, (ROWS, ROWS), 1 if transposed else 0)
+    flat = lax.broadcasted_iota(jnp.int32, (ROWS, ROWS), 0 if transposed else 1)
     own, a_step = jnp.where(half == 0, place % 4, place // 64), jnp.where(half == 0, 8, 2)
     a, b = (sent // 32 + own) % 4, sent // 8 % 4
     return (sent // 2 % 4 * 32 + a * a_step + b * (10 - a_step) + sent % 2 == flat).astype(F32).astype(BF16)
-
-
-def gathered_order(half):
-    sent = lax.broadcasted_iota(jnp.int32, (ROWS, ROWS), 1)
-    flat = lax.broadcasted_iota(jnp.int32, (ROWS, ROWS), 0)
-    a, k, b, p = sent // 32, sent // 16 % 2, sent // 4 % 4, sent % 4
-    z = (2 * p + k + half) % 8
-    a_step = jnp.where(half == 0, 8, 2)
-    return (z % 4 * 32 + a * a_step + b * (10 - a_step) + z // 4 == flat).astype(F32).astype(BF16)
 
 
 def compensate_kernel(other, place_ref, codes_hbm, scales_hbm, feedback_hbm, out_ref, codes, scales, feedback, turned, spread, summed, sems):
@@ -116,7 +93,7 @@
         copies.append(pltpu.make_async_copy(feedback_hbm.at[:, columns], feedback.at[i], sems.at[2 * i + 1]))
     for copy in copies:
         copy.start()
-    moved = sent_order(place_ref[0], half)
+    moved = order(place_ref[0], half, False)
     copies[0].wait()
     turned[0:SLAB_ROWS, :] = scales[pl.ds(half * SLAB_ROWS, SLAB_ROWS), :]
     scale = turned[...].T
@@ -206,7 +183,7 @@
     slab = jax.ShapeDtypeStruct((1, HALF), F32)
     return pl.pallas_call(
         adam_kernel,
-        out_shape=(slab, slab, jax.ShapeDtypeStruct((16, *SLAB), BF16)),
+        out_shape=(slab, slab, jax.ShapeDtypeStruct((32, *SLAB), BF16)),
         in_specs=[WHOLE] * 4,
         out_specs=[WHOLE] * 3,
         compiler_params=params(),
@@ -214,26 +191,11 @@
     )(arrived, master, moment, second)
 
 
-def copies_kernel(in_ref, out_ref):
-    out_ref[...] = jnp.broadcast_to(in_ref[...][None], out_ref.shape)
-
-
-def copies_of(rows):
-    return pl.pallas_call(
-        copies_kernel,
-        out_shape=jax.ShapeDtypeStruct((8, 16, HALF), BF16),
-        in_specs=[WHOLE],
-        out_specs=WHOLE,
-        compiler_params=params(),
-        name="copies_of",
-    )(rows)
-
-
-def place_half(half, rows_ref, weights_hbm, staged, sems):
-    moved = gathered_order(half)
+def place_half(place, half, blocks, weights_hbm, staged, sems):
+    moved = order(place, half, True)
     copies = []
     for i in range(CHUNKS):
-        rows = rows_ref[:, i * CHUNK : (i + 1) * CHUNK]
+        rows = jnp.concatenate([block[:, i * CHUNK : (i + 1) * CHUNK] for block in blocks], axis=0)
         staged[i] = jnp.dot(moved, rows, preferred_element_type=F32).astype(BF16)
         to = pl.ds(pl.multiple_of(half * HALF + i * CHUNK, LANES), CHUNK)
         copies.append(pltpu.make_async_copy(staged.at[i], weights_hbm.at[:, to], sems.at[i]))
@@ -241,50 +203,51 @@
     return copies
 
 
-def restore_own_kernel(core_ref, rows_ref, dir_ref, new_ref, weights_hbm, dir_hbm, new_hbm, staged, sems):
+def restore_own_kernel(place_ref, a_ref, b_ref, c_ref, d_ref, dir_ref, new_ref, weights_hbm, dir_hbm, new_hbm, staged, sems):
     copies = [
         pltpu.make_async_copy(dir_ref, dir_hbm, sems.at[CHUNKS]),
         pltpu.make_async_copy(new_ref, new_hbm, sems.at[CHUNKS + 1]),
     ]
     for copy in copies:
         copy.start()
-    for copy in copies + place_half(core_ref[0], rows_ref, weights_hbm, staged, sems):
+    half = place_ref[0] // 16 % 2
+    for copy in copies + place_half(place_ref[0], half, (a_ref, b_ref, c_ref, d_ref), weights_hbm, staged, sems):
         copy.wait()
 
 
-def restore_own(core, rows, adam_dir, new_master):
+def restore_own(place, blocks, adam_dir, new_master):
     slab = jax.ShapeDtypeStruct((1, HALF), F32)
     return pl.pallas_call(
         restore_own_kernel,
         out_shape=(jax.ShapeDtypeStruct((ROWS, WIDTH), BF16), slab, slab),
-        in_specs=[SCALAR] + [WHOLE] * 3,
+        in_specs=[SCALAR] + [WHOLE] * 6,
         out_specs=[FAR] * 3,
         scratch_shapes=[pltpu.VMEM((CHUNKS, ROWS, CHUNK), BF16), pltpu.SemaphoreType.DMA((CHUNKS + 2,))],
         compiler_params=params(),
         name="restore_own",
-    )(core, rows, adam_dir, new_master)
-
-
-def restore_other_kernel(core_ref, rows_ref, held_hbm, weights_hbm, staged, sems):
-    for copy in place_half(1 - core_ref[0], rows_ref, weights_hbm, staged, sems):
+    )(place, *blocks, adam_dir, new_master)
+
+
+def restore_other_kernel(place_ref, a_ref, b_ref, c_ref, d_ref, held_hbm, weights_hbm, staged, sems):
+    half = 1 - place_ref[0] // 16 % 2
+    for copy in place_half(place_ref[0], half, (a_ref, b_ref, c_ref, d_ref), weights_hbm, staged, sems):
         copy.wait()
 
 
-def restore_other(core, rows, weights):
+def restore_other(place, blocks, weights):
     return pl.pallas_call(
         restore_other_kernel,
         out_shape=jax.ShapeDtypeStruct((ROWS, WIDTH), BF16),
-        in_specs=[SCALAR, WHOLE, FAR],
+        in_specs=[SCALAR] + [WHOLE] * 4 + [FAR],
         out_specs=FAR,
         scratch_shapes=[pltpu.VMEM((CHUNKS, ROWS, CHUNK), BF16), pltpu.SemaphoreType.DMA((CHUNKS,))],
-        input_output_aliases={2: 0},
+        input_output_aliases={5: 0},
         compiler_params=params(),
         name="restore_other",
-    )(core, rows, weights)
+    )(place, *blocks, weights)
 
 
 def shards(grad_codes, scales, feedback, master, moment, second):
-    core = lax.axis_index("core").astype(jnp.int32).reshape(1)
     place = lax.axis_index(AXES).astype(jnp.int32).reshape(1)
     codes, feed = grad_codes[0, 0], feedback[0, 0]
     turned = jnp.swapaxes(scales[0, 0], 0, 1)
@@ -295,11 +258,12 @@
     partial = line_sum(own, [send(others[step - 1], step) for step in (2, 1, 3)])
     arrived = exchange(partial.reshape(32, *SLAB), owner_groups())
     adam_dir, new_master, copies = adam(arrived, master[0], moment[0], second[0])
-    rows = exchange(copies, small_groups()).reshape(16, HALF)
-    mine = exchange(copies_of(rows), large_groups()).reshape(ROWS, HALF)
-    theirs = swap_cores(mine)
-    weights, adam_dir, new_master = restore_own(core, mine, adam_dir, new_master)
-    weights = restore_other(core, theirs, weights)
+    joined = exchange(copies, owner_groups()).reshape(32, HALF)
+    across, after, before = [send(joined, 4 - step) for step in (2, 1, 3)]
+    mine = [joined, after, across, before]
+    theirs = [swap_cores(block) for block in mine]
+    weights, adam_dir, new_master = restore_own(place, mine, adam_dir, new_master)
+    weights = restore_other(place, theirs, weights)
     return adam_dir[None], new_master[None], weights
 
 

time: 79.9 us -> 75.5 us (0.945)
  blocking collectives: 50.7 us -> 36.8 us
  starting transfers between devices: 11.7 us -> 22.2 us
  waiting for transfers between devices: 7.84 us -> 6.91 us
    all_to_all x3 -> x2, blocking collectives: 50.7 us -> 36.8 us  [exchange(): lax.all_to_all(array, AXES, 0, 0, axis_index_groups=groups, tiled=True)]
    ppermute x2 -> x5, starting transfers between devices: 7.73 us -> 14.9 us  [swap_cores(): return lax.ppermute(array, AXES, SWAP)]
    ppermute x3 -> x6, starting transfers between devices: 3.94 us -> 7.29 us  [send(): return lax.ppermute(array, AXES, shifted(step))]
    ppermute x2 -> x5, waiting for transfers between devices: 1.16 us -> 0.22 us  [swap_cores(): return lax.ppermute(array, AXES, SWAP)]
    ppermute x3 -> x6, waiting for transfers between devices: 6.68 us -> 6.69 us  [send(): return lax.ppermute(array, AXES, shifted(step))]
  transfers between devices with their start and end apart: 5 -> 11, of which waited for: 3 -> 3; matrix products, arithmetic and copies ran while one was open for 0% -> 0% of each run, Pallas kernels for 5% -> 5%
where the time goes in v6:
time: 75.5 us; the launch traced here: 75.3 us
  blocking collectives  36.8 us (49%)
  starting transfers between devices  22.2 us (29%)
  Pallas kernels  8.54 us (11%)
  waiting for transfers between devices  6.91 us (9%)
  between operations  0.76 us (1%)
    all_to_all x2, blocking collectives, exchange(): lax.all_to_all(array, AXES, 0, 0, axis_index_groups=groups, tiled=True)  36.8 us
    ppermute x5, starting transfers between devices, swap_cores(): return lax.ppermute(array, AXES, SWAP)  14.9 us
    ppermute x6, starting transfers between devices, send(): return lax.ppermute(array, AXES, shifted(step))  7.29 us
    ppermute x6, waiting for transfers between devices, send(): return lax.ppermute(array, AXES, shifted(step))  6.69 us
    pallas_call x2, Pallas kernels, compensate(): pl.pallas_call(functools.partial(compensate_kernel, other), out_shape=jax...  5.16 us
  transfers between devices with their start and end apart: 11, of which 3 were waited for; matrix products, arithmetic and copies ran while one was open for 0% of the time, Pallas kernels for 5%

profile of v6, /device:TPU:1, one launch (start us, length us, event | category | flops | bytes accessed | tf_op | source)
XLA Modules:
  0.0 75.3 jit_solution(10978931932831641407)
XLA Ops:
  0.6 2.6 %compensate.3 = bf16[128,4608]{1,0:T(8,128)(2,1)S(1)} custom-call(s32[1]{0:T(128)} %bitcast.place_ref, s32[128,9216]{1,0:T(8,128)} %bitcast.21, f32[72,128]{1,0:T(8,128)} %bitcast.26, bf16[128,9216]{1,0:T(8,128)(2,1)} %bitcast.23), custom_call_target="tpu_custom_call" | custom-call | flops 150994944 | bytes 4718592 | tf_op jit(solution)/shard_map/compensate/pallas_call | solution.py:114
  3.2 3.3 %collective-permute-start = (bf16[128,4608]{1,0:T(8,128)(2,1)S(1)}, bf16[128,4608]{1,0:T(8,128)(2,1)S(1)}, u32[]{:S(2)}, u32[]{:S(2)}) collective-permute-start(bf16[128,4608]{1,0:T(8,128)(2,1)S(1)} %compensate.3), channel_id=1, source_target_pairs={{0,16},{1,17},{2,18},{3,19},{4,20},{5,21},{6,22},{7,23},{8,24},{9,... | collective-permute-start | bytes 3538952 | tf_op jit(solution)/shard_map/ppermute | solution.py:67
  6.6 2.6 %compensate.2.own_ref = bf16[128,4608]{1,0:T(8,128)(2,1)S(1)} custom-call(s32[1]{0:T(128)} %bitcast.place_ref, s32[128,9216]{1,0:T(8,128)} %bitcast.22, f32[72,128]{1,0:T(8,128)} %bitcast.27, bf16[128,9216]{1,0:T(8,128)(2,1)} %bitcast.24), custom_call_target="tpu_custom_call" | custom-call | flops 150994944 | bytes 4718592 | tf_op jit(solution)/shard_map/compensate/pallas_call | solution.py:114
  9.1 0.0 copy-start
  9.1 0.0 copy-start.1
  9.2 0.0 copy-start.2
  9.2 0.0 collective-permute-done.other_ref
  9.2 0.3 pair_sum.1
  9.5 1.3 %collective-permute-start.1 = (bf16[32,4608]{1,0:T(8,128)(2,1)S(1)}, bf16[32,4608]{1,0:T(8,128)(2,1)S(1)}, u32[]{:S(2)}, u32[]{:S(2)}) collective-permute-start(bf16[32,4608]{1,0:T(8,128)(2,1)S(1)} %get-tuple-element.14), channel_id=1, source_target_pairs={{0,2},{1,3},{2,0},{3,1},{4,6},{5,7},{6,4},{7,5},{8,10},{9,11},{10,... | collective-permute-start | bytes 884744 | tf_op jit(solution)/shard_map/ppermute | solution.py:71
  10.7 0.4 collective-permute-start.2
  11.1 2.3 %collective-permute-start.3 = (bf16[32,4608]{1,0:T(8,128)(2,1)S(1)}, bf16[32,4608]{1,0:T(8,128)(2,1)S(1)}, u32[]{:S(2)}, u32[]{:S(2)}) collective-permute-start(bf16[32,4608]{1,0:T(8,128)(2,1)S(1)} %get-tuple-element.16), channel_id=1, source_target_pairs={{0,3},{1,0},{2,1},{3,2},{4,7},{5,4},{6,5},{7,6},{8,11},{9,8},{10,9... | collective-permute-start | bytes 884744 | tf_op jit(solution)/shard_map/ppermute | solution.py:71
  13.4 3.6 %collective-permute-done.1.a_ref = bf16[32,4608]{1,0:T(8,128)(2,1)S(1)} collective-permute-done((bf16[32,4608]{1,0:T(8,128)(2,1)S(1)}, bf16[32,4608]{1,0:T(8,128)(2,1)S(1)}, u32[]{:S(2)}, u32[]{:S(2)}) %collective-permute-start.1) | collective-permute-done | bytes 294944 | tf_op jit(solution)/shard_map/ppermute | solution.py:71
  17.0 3.1 %collective-permute-done.2.b_ref = bf16[32,4608]{1,0:T(8,128)(2,1)S(1)} collective-permute-done((bf16[32,4608]{1,0:T(8,128)(2,1)S(1)}, bf16[32,4608]{1,0:T(8,128)(2,1)S(1)}, u32[]{:S(2)}, u32[]{:S(2)}) %collective-permute-start.2) | collective-permute-done | bytes 294944 | tf_op jit(solution)/shard_map/ppermute | solution.py:71
  20.1 0.0 collective-permute-done.3.c_ref
  20.1 0.1 line_sum.1
  20.2 0.1 reshape.16
  20.3 19.7 %all_to_all.10.arrived_ref = bf16[32,2,2304]{2,1,0:T(2,128)(2,1)S(1)} all-to-all(bf16[32,2,2304]{2,1,0:T(2,128)(2,1)S(1)} %reshape.16), channel_id=1, replica_groups={{0,32,4,36,8,40,12,44,64,96,68,100,72,104,76,108,128,160,132,164,136,16..., dimensions={0} | all-to-all | bytes 589824 | tf_op jit(solution)/shard_map/all_to_all | solution.py:75
  40.0 0.0 copy-done
  40.0 0.0 copy-done.1
  40.0 0.0 copy-done.2
  40.0 0.4 adam.1
  40.4 17.1 %all_to_all.11 = bf16[32,2,2304]{2,1,0:T(2,128)(2,1)S(1)} all-to-all(bf16[32,2,2304]{2,1,0:T(2,128)(2,1)S(1)} %get-tuple-element.17), channel_id=1, replica_groups={{0,32,4,36,8,40,12,44,64,96,68,100,72,104,76,108,128,160,132,164,136,16..., dimensions={0} | all-to-all | bytes 589824 | tf_op jit(solution)/shard_map/all_to_all | solution.py:75
  57.5 0.7 collective-permute-start.6
  58.2 2.6 %collective-permute-start.5 = (bf16[32,4608]{1,0:T(8,128)(2,1)S(1)}, bf16[32,4608]{1,0:T(8,128)(2,1)S(1)}, u32[]{:S(2)}, u32[]{:S(2)}) collective-permute-start(bf16[32,4608]{1,0:T(8,128)(2,1)S(1)} %bitcast.14), channel_id=1, source_target_pairs={{0,2},{1,3},{2,0},{3,1},{4,6},{5,7},{6,4},{7,5},{8,10},{9,11},{10,... | collective-permute-start | bytes 884744 | tf_op jit(solution)/shard_map/ppermute | solution.py:71
  60.9 0.0 collective-permute-start.4
  60.9 5.1 %collective-permute-start.7 = (bf16[32,4608]{1,0:T(8,128)(2,1)S(1)}, bf16[32,4608]{1,0:T(8,128)(2,1)S(1)}, u32[]{:S(2)}, u32[]{:S(2)}) collective-permute-start(bf16[32,4608]{1,0:T(8,128)(2,1)S(1)} %bitcast.16), channel_id=1, source_target_pairs={{0,16},{1,17},{2,18},{3,19},{4,20},{5,21},{6,22},{7,23},{8,24},{9,... | collective-permute-start | bytes 884744 | tf_op jit(solution)/shard_map/ppermute | solution.py:67
  66.0 0.0 collective-permute-done.6.d_ref
  66.0 2.5 %collective-permute-start.10 = (bf16[32,4608]{1,0:T(8,128)(2,1)S(1)}, bf16[32,4608]{1,0:T(8,128)(2,1)S(1)}, u32[]{:S(2)}, u32[]{:S(2)}) collective-permute-start(bf16[32,4608]{1,0:T(8,128)(2,1)S(1)} %collective-permute-done.6.d_ref), channel_id=1, source_target_pairs={{0,16},{1,17},{2,18},{3,19},{4,20},{5,21},{6,22},{7,23},{8,24},{9,... | collective-permute-start | bytes 884744 | tf_op jit(solution)/shard_map/ppermute | solution.py:67
  68.5 0.0 collective-permute-done.5.c_ref
  68.5 3.9 %collective-permute-start.9 = (bf16[32,4608]{1,0:T(8,128)(2,1)S(1)}, bf16[32,4608]{1,0:T(8,128)(2,1)S(1)}, u32[]{:S(2)}, u32[]{:S(2)}) collective-permute-start(bf16[32,4608]{1,0:T(8,128)(2,1)S(1)} %collective-permute-done.5.c_ref), channel_id=1, source_target_pairs={{0,16},{1,17},{2,18},{3,19},{4,20},{5,21},{6,22},{7,23},{8,24},{9,... | collective-permute-start | bytes 884744 | tf_op jit(solution)/shard_map/ppermute | solution.py:67
  72.4 0.0 collective-permute-done.4.b_ref
  72.4 0.1 collective-permute-start.8
  72.5 1.3 %restore_own.1 = (bf16[128,9216]{1,0:T(8,128)(2,1)}, f32[1,4608]{1,0:T(1,128)}, f32[1,4608]{1,0:T(1,128)}) custom-call(s32[1]{0:T(128)} %bitcast.place_ref, bf16[32,4608]{1,0:T(8,128)(2,1)S(1)} %bitcast.17, bf16[32,4608]{1,0:T(8,128)(2,1)S(1)} %collective-permute-done.4.b_ref, bf16[32,4608]{1,0:T(8,128)(2,1)S(1)} %collective-permute-done.5.c_ref, ...), custom_call_target="tpu_custom_call" | custom-call | tf_op jit(solution)/shard_map/restore_own/pallas_call | solution.py:220
  73.8 0.0 collective-permute-done.7.a_ref
  73.8 0.0 collective-permute-done.10.d_ref
  73.8 0.0 collective-permute-done.9.c_ref
  73.8 0.2 collective-permute-done.8.b_ref
  74.0 1.3 %restore_other.1 = bf16[128,9216]{1,0:T(8,128)(2,1)} custom-call(s32[1]{0:T(128)} %bitcast.place_ref, bf16[32,4608]{1,0:T(8,128)(2,1)S(1)} %collective-permute-done.7.a_ref, bf16[32,4608]{1,0:T(8,128)(2,1)S(1)} %collective-permute-done.8.b_ref, bf16[32,4608]{1,0:T(8,128)(2,1)S(1)} %collective-permute-done.9.c_ref, ...), custom_call_target="tpu_custom_call", output_to_operand_aliasing={{}: (5, {})} | custom-call | tf_op jit(solution)/shard_map/restore_other/pallas_call | solution.py:238
  (1 shorter events, 0.0 us)
Async XLA Ops:
  3.2 5.9 %collective-permute-start = (bf16[128,4608]{1,0:T(8,128)(2,1)S(1)}, bf16[128,4608]{1,0:T(8,128)(2,1)S(1)}, u32[]{:S(2)}, u32[]{:S(2)}) collective-permute-start(bf16[128,4608]{1,0:T(8,128)(2,1)S(1)} %compensate.3), channel_id=1, source_target_pairs={{0,16},{1,17},{2,18},{3,19},{4,20},{5,21},{6,22},{7,23},{8,24},{9,... | collective-permute-start | bytes 3538952 | tf_op jit(solution)/shard_map/ppermute | solution.py:67
  9.1 30.8 %copy-start = (f32[1,1,4608]{2,1,0:T(1,128)S(1)}, f32[1,1,4608]{2,1,0:T(1,128)}, u32[]{:S(2)}) copy-start(f32[1,1,4608]{2,1,0:T(1,128)} %param.9) | copy-start | bytes 55300
  9.1 30.8 %copy-start.1 = (f32[1,1,4608]{2,1,0:T(1,128)S(1)}, f32[1,1,4608]{2,1,0:T(1,128)}, u32[]{:S(2)}) copy-start(f32[1,1,4608]{2,1,0:T(1,128)} %param.10) | copy-start | bytes 55300
  9.2 30.8 %copy-start.2 = (f32[1,1,4608]{2,1,0:T(1,128)S(1)}, f32[1,1,4608]{2,1,0:T(1,128)}, u32[]{:S(2)}) copy-start(f32[1,1,4608]{2,1,0:T(1,128)} %param.11) | copy-start | bytes 55300
  9.5 7.5 %collective-permute-start.1 = (bf16[32,4608]{1,0:T(8,128)(2,1)S(1)}, bf16[32,4608]{1,0:T(8,128)(2,1)S(1)}, u32[]{:S(2)}, u32[]{:S(2)}) collective-permute-start(bf16[32,4608]{1,0:T(8,128)(2,1)S(1)} %get-tuple-element.14), channel_id=1, source_target_pairs={{0,2},{1,3},{2,0},{3,1},{4,6},{5,7},{6,4},{7,5},{8,10},{9,11},{10,... | collective-permute-start | bytes 884744 | tf_op jit(solution)/shard_map/ppermute | solution.py:71
  10.7 9.4 %collective-permute-start.2 = (bf16[32,4608]{1,0:T(8,128)(2,1)S(1)}, bf16[32,4608]{1,0:T(8,128)(2,1)S(1)}, u32[]{:S(2)}, u32[]{:S(2)}) collective-permute-start(bf16[32,4608]{1,0:T(8,128)(2,1)S(1)} %get-tuple-element.15), channel_id=1, source_target_pairs={{0,1},{1,2},{2,3},{3,0},{4,5},{5,6},{6,7},{7,4},{8,9},{9,10},{10,1... | collective-permute-start | bytes 884744 | tf_op jit(solution)/shard_map/ppermute | solution.py:71
  11.1 9.0 %collective-permute-start.3 = (bf16[32,4608]{1,0:T(8,128)(2,1)S(1)}, bf16[32,4608]{1,0:T(8,128)(2,1)S(1)}, u32[]{:S(2)}, u32[]{:S(2)}) collective-permute-start(bf16[32,4608]{1,0:T(8,128)(2,1)S(1)} %get-tuple-element.16), channel_id=1, source_target_pairs={{0,3},{1,0},{2,1},{3,2},{4,7},{5,4},{6,5},{7,6},{8,11},{9,8},{10,9... | collective-permute-start | bytes 884744 | tf_op jit(solution)/shard_map/ppermute | solution.py:71
  57.5 8.5 %collective-permute-start.6 = (bf16[32,4608]{1,0:T(8,128)(2,1)S(1)}, bf16[32,4608]{1,0:T(8,128)(2,1)S(1)}, u32[]{:S(2)}, u32[]{:S(2)}) collective-permute-start(bf16[32,4608]{1,0:T(8,128)(2,1)S(1)} %bitcast.13), channel_id=1, source_target_pairs={{0,1},{1,2},{2,3},{3,0},{4,5},{5,6},{6,7},{7,4},{8,9},{9,10},{10,1... | collective-permute-start | bytes 884744 | tf_op jit(solution)/shard_map/ppermute | solution.py:71
  58.2 10.2 %collective-permute-start.5 = (bf16[32,4608]{1,0:T(8,128)(2,1)S(1)}, bf16[32,4608]{1,0:T(8,128)(2,1)S(1)}, u32[]{:S(2)}, u32[]{:S(2)}) collective-permute-start(bf16[32,4608]{1,0:T(8,128)(2,1)S(1)} %bitcast.14), channel_id=1, source_target_pairs={{0,2},{1,3},{2,0},{3,1},{4,6},{5,7},{6,4},{7,5},{8,10},{9,11},{10,... | collective-permute-start | bytes 884744 | tf_op jit(solution)/shard_map/ppermute | solution.py:71
  60.9 11.5 %collective-permute-start.4 = (bf16[32,4608]{1,0:T(8,128)(2,1)S(1)}, bf16[32,4608]{1,0:T(8,128)(2,1)S(1)}, u32[]{:S(2)}, u32[]{:S(2)}) collective-permute-start(bf16[32,4608]{1,0:T(8,128)(2,1)S(1)} %bitcast.15), channel_id=1, source_target_pairs={{0,3},{1,0},{2,1},{3,2},{4,7},{5,4},{6,5},{7,6},{8,11},{9,8},{10,9... | collective-permute-start | bytes 884744 | tf_op jit(solution)/shard_map/ppermute | solution.py:71
  60.9 12.9 %collective-permute-start.7 = (bf16[32,4608]{1,0:T(8,128)(2,1)S(1)}, bf16[32,4608]{1,0:T(8,128)(2,1)S(1)}, u32[]{:S(2)}, u32[]{:S(2)}) collective-permute-start(bf16[32,4608]{1,0:T(8,128)(2,1)S(1)} %bitcast.16), channel_id=1, source_target_pairs={{0,16},{1,17},{2,18},{3,19},{4,20},{5,21},{6,22},{7,23},{8,24},{9,... | collective-permute-start | bytes 884744 | tf_op jit(solution)/shard_map/ppermute | solution.py:67
  66.0 7.8 %collective-permute-start.10 = (bf16[32,4608]{1,0:T(8,128)(2,1)S(1)}, bf16[32,4608]{1,0:T(8,128)(2,1)S(1)}, u32[]{:S(2)}, u32[]{:S(2)}) collective-permute-start(bf16[32,4608]{1,0:T(8,128)(2,1)S(1)} %collective-permute-done.6.d_ref), channel_id=1, source_target_pairs={{0,16},{1,17},{2,18},{3,19},{4,20},{5,21},{6,22},{7,23},{8,24},{9,... | collective-permute-start | bytes 884744 | tf_op jit(solution)/shard_map/ppermute | solution.py:67
  68.5 5.3 %collective-permute-start.9 = (bf16[32,4608]{1,0:T(8,128)(2,1)S(1)}, bf16[32,4608]{1,0:T(8,128)(2,1)S(1)}, u32[]{:S(2)}, u32[]{:S(2)}) collective-permute-start(bf16[32,4608]{1,0:T(8,128)(2,1)S(1)} %collective-permute-done.5.c_ref), channel_id=1, source_target_pairs={{0,16},{1,17},{2,18},{3,19},{4,20},{5,21},{6,22},{7,23},{8,24},{9,... | collective-permute-start | bytes 884744 | tf_op jit(solution)/shard_map/ppermute | solution.py:67
  72.4 1.6 %collective-permute-start.8 = (bf16[32,4608]{1,0:T(8,128)(2,1)S(1)}, bf16[32,4608]{1,0:T(8,128)(2,1)S(1)}, u32[]{:S(2)}, u32[]{:S(2)}) collective-permute-start(bf16[32,4608]{1,0:T(8,128)(2,1)S(1)} %collective-permute-done.4.b_ref), channel_id=1, source_target_pairs={{0,16},{1,17},{2,18},{3,19},{4,20},{5,21},{6,22},{7,23},{8,24},{9,... | collective-permute-start | bytes 884744 | tf_op jit(solution)/shard_map/ppermute | solution.py:67

commit v7 on v6

--- a/solution.py
+++ b/solution.py
@@ -165,7 +165,9 @@
 
 
 def adam_kernel(arrived_ref, master_ref, moment_ref, second_ref, dir_ref, new_ref, copies_ref):
-    total = jnp.sum(arrived_ref[...].astype(F32), axis=0)
+    total = arrived_ref[0].astype(F32)
+    for piece in range(1, 32):
+        total = total + arrived_ref[piece].astype(F32)
     grad = jnp.concatenate([total[0:1], total[1:2]], axis=1) / 256.0
     first = beta_one * moment_ref[...] + (1.0 - beta_one) * grad
     squared = beta_two * second_ref[...] + (1.0 - beta_two) * grad * grad
@@ -192,10 +194,11 @@
 
 
 def place_half(place, half, blocks, weights_hbm, staged, sems):
+    own, across, after, before = blocks
     moved = order(place, half, True)
     copies = []
     for i in range(CHUNKS):
-        rows = jnp.concatenate([block[:, i * CHUNK : (i + 1) * CHUNK] for block in blocks], axis=0)
+        rows = jnp.concatenate([block[:, i * CHUNK : (i + 1) * CHUNK] for block in (own, after, across, before)], axis=0)
         staged[i] = jnp.dot(moved, rows, preferred_element_type=F32).astype(BF16)
         to = pl.ds(pl.multiple_of(half * HALF + i * CHUNK, LANES), CHUNK)
         copies.append(pltpu.make_async_copy(staged.at[i], weights_hbm.at[:, to], sems.at[i]))
@@ -260,7 +263,7 @@
     adam_dir, new_master, copies = adam(arrived, master[0], moment[0], second[0])
     joined = exchange(copies, owner_groups()).reshape(32, HALF)
     across, after, before = [send(joined, 4 - step) for step in (2, 1, 3)]
-    mine = [joined, after, across, before]
+    mine = [joined, across, after, before]
     theirs = [swap_cores(block) for block in mine]
     weights, adam_dir, new_master = restore_own(place, mine, adam_dir, new_master)
     weights = restore_other(place, theirs, weights)

time: 75.5 us -> 75 us (level)
  transfers between devices with their start and end apart: 11 -> 11, of which waited for: 3 -> 2; matrix products, arithmetic and copies ran while one was open for 0% -> 0% of each run, Pallas kernels for 5% -> 5%
where the time goes in v7:
time: 75 us; the launch traced here: 74.8 us
  blocking collectives  36.8 us (49%)
  starting transfers between devices  22.1 us (29%)
  Pallas kernels  8.32 us (11%)
  waiting for transfers between devices  6.7 us (9%)
  between operations  0.77 us (1%)
    all_to_all x2, blocking collectives, exchange(): lax.all_to_all(array, AXES, 0, 0, axis_index_groups=groups, tiled=True)  36.8 us
    ppermute x5, starting transfers between devices, swap_cores(): return lax.ppermute(array, AXES, SWAP)  14.8 us
    ppermute x6, starting transfers between devices, send(): return lax.ppermute(array, AXES, shifted(step))  7.29 us
    ppermute x6, waiting for transfers between devices, send(): return lax.ppermute(array, AXES, shifted(step))  6.69 us
    pallas_call x2, Pallas kernels, compensate(): pl.pallas_call(functools.partial(compensate_kernel, other), out_shape=jax...  5.16 us
  transfers between devices with their start and end apart: 11, of which 2 were waited for; matrix products, arithmetic and copies ran while one was open for 0% of the time, Pallas kernels for 5%

profile of v7, /device:TPU:1, one launch (start us, length us, event | category | flops | bytes accessed | tf_op | source)
XLA Modules:
  0.0 74.8 jit_solution(4507690818018040016)
XLA Ops:
  0.6 2.6 %compensate.3 = bf16[128,4608]{1,0:T(8,128)(2,1)S(1)} custom-call(s32[1]{0:T(128)} %bitcast.place_ref, s32[128,9216]{1,0:T(8,128)} %bitcast.21, f32[72,128]{1,0:T(8,128)} %bitcast.26, bf16[128,9216]{1,0:T(8,128)(2,1)} %bitcast.23), custom_call_target="tpu_custom_call" | custom-call | flops 150994944 | bytes 4718592 | tf_op jit(solution)/shard_map/compensate/pallas_call | solution.py:114
  3.2 3.3 %collective-permute-start = (bf16[128,4608]{1,0:T(8,128)(2,1)S(1)}, bf16[128,4608]{1,0:T(8,128)(2,1)S(1)}, u32[]{:S(2)}, u32[]{:S(2)}) collective-permute-start(bf16[128,4608]{1,0:T(8,128)(2,1)S(1)} %compensate.3), channel_id=1, source_target_pairs={{0,16},{1,17},{2,18},{3,19},{4,20},{5,21},{6,22},{7,23},{8,24},{9,... | collective-permute-start | bytes 3538952 | tf_op jit(solution)/shard_map/ppermute | solution.py:67
  6.6 2.6 %compensate.2.own_ref = bf16[128,4608]{1,0:T(8,128)(2,1)S(1)} custom-call(s32[1]{0:T(128)} %bitcast.place_ref, s32[128,9216]{1,0:T(8,128)} %bitcast.22, f32[72,128]{1,0:T(8,128)} %bitcast.27, bf16[128,9216]{1,0:T(8,128)(2,1)} %bitcast.24), custom_call_target="tpu_custom_call" | custom-call | flops 150994944 | bytes 4718592 | tf_op jit(solution)/shard_map/compensate/pallas_call | solution.py:114
  9.1 0.0 copy-start
  9.1 0.0 copy-start.1
  9.2 0.0 copy-start.2
  9.2 0.0 collective-permute-done.other_ref
  9.2 0.3 pair_sum.1
  9.5 1.3 %collective-permute-start.1 = (bf16[32,4608]{1,0:T(8,128)(2,1)S(1)}, bf16[32,4608]{1,0:T(8,128)(2,1)S(1)}, u32[]{:S(2)}, u32[]{:S(2)}) collective-permute-start(bf16[32,4608]{1,0:T(8,128)(2,1)S(1)} %get-tuple-element.14), channel_id=1, source_target_pairs={{0,2},{1,3},{2,0},{3,1},{4,6},{5,7},{6,4},{7,5},{8,10},{9,11},{10,... | collective-permute-start | bytes 884744 | tf_op jit(solution)/shard_map/ppermute | solution.py:71
  10.7 0.4 collective-permute-start.2
  11.1 2.3 %collective-permute-start.3 = (bf16[32,4608]{1,0:T(8,128)(2,1)S(1)}, bf16[32,4608]{1,0:T(8,128)(2,1)S(1)}, u32[]{:S(2)}, u32[]{:S(2)}) collective-permute-start(bf16[32,4608]{1,0:T(8,128)(2,1)S(1)} %get-tuple-element.16), channel_id=1, source_target_pairs={{0,3},{1,0},{2,1},{3,2},{4,7},{5,4},{6,5},{7,6},{8,11},{9,8},{10,9... | collective-permute-start | bytes 884744 | tf_op jit(solution)/shard_map/ppermute | solution.py:71
  13.4 3.6 %collective-permute-done.1.a_ref = bf16[32,4608]{1,0:T(8,128)(2,1)S(1)} collective-permute-done((bf16[32,4608]{1,0:T(8,128)(2,1)S(1)}, bf16[32,4608]{1,0:T(8,128)(2,1)S(1)}, u32[]{:S(2)}, u32[]{:S(2)}) %collective-permute-start.1) | collective-permute-done | bytes 294944 | tf_op jit(solution)/shard_map/ppermute | solution.py:71
  17.0 3.1 %collective-permute-done.2.b_ref = bf16[32,4608]{1,0:T(8,128)(2,1)S(1)} collective-permute-done((bf16[32,4608]{1,0:T(8,128)(2,1)S(1)}, bf16[32,4608]{1,0:T(8,128)(2,1)S(1)}, u32[]{:S(2)}, u32[]{:S(2)}) %collective-permute-start.2) | collective-permute-done | bytes 294944 | tf_op jit(solution)/shard_map/ppermute | solution.py:71
  20.1 0.0 collective-permute-done.3.c_ref
  20.1 0.1 line_sum.1
  20.2 0.1 reshape.16
  20.3 19.7 %all_to_all.10.arrived_ref = bf16[32,2,2304]{2,1,0:T(2,128)(2,1)S(1)} all-to-all(bf16[32,2,2304]{2,1,0:T(2,128)(2,1)S(1)} %reshape.16), channel_id=1, replica_groups={{0,32,4,36,8,40,12,44,64,96,68,100,72,104,76,108,128,160,132,164,136,16..., dimensions={0} | all-to-all | bytes 589824 | tf_op jit(solution)/shard_map/all_to_all | solution.py:75
  40.0 0.0 copy-done
  40.0 0.0 copy-done.1
  40.0 0.0 copy-done.2
  40.0 0.1 adam.1
  40.1 17.1 %all_to_all.11 = bf16[32,2,2304]{2,1,0:T(2,128)(2,1)S(1)} all-to-all(bf16[32,2,2304]{2,1,0:T(2,128)(2,1)S(1)} %get-tuple-element.17), channel_id=1, replica_groups={{0,32,4,36,8,40,12,44,64,96,68,100,72,104,76,108,128,160,132,164,136,16..., dimensions={0} | all-to-all | bytes 589824 | tf_op jit(solution)/shard_map/all_to_all | solution.py:75
  57.3 0.7 collective-permute-start.6
  58.0 2.1 %collective-permute-start.5 = (bf16[32,4608]{1,0:T(8,128)(2,1)S(1)}, bf16[32,4608]{1,0:T(8,128)(2,1)S(1)}, u32[]{:S(2)}, u32[]{:S(2)}) collective-permute-start(bf16[32,4608]{1,0:T(8,128)(2,1)S(1)} %bitcast.14), channel_id=1, source_target_pairs={{0,3},{1,0},{2,1},{3,2},{4,7},{5,4},{6,5},{7,6},{8,11},{9,8},{10,9... | collective-permute-start | bytes 884744 | tf_op jit(solution)/shard_map/ppermute | solution.py:71
  60.1 0.6 collective-permute-start.4
  60.7 4.5 %collective-permute-start.7 = (bf16[32,4608]{1,0:T(8,128)(2,1)S(1)}, bf16[32,4608]{1,0:T(8,128)(2,1)S(1)}, u32[]{:S(2)}, u32[]{:S(2)}) collective-permute-start(bf16[32,4608]{1,0:T(8,128)(2,1)S(1)} %bitcast.16), channel_id=1, source_target_pairs={{0,16},{1,17},{2,18},{3,19},{4,20},{5,21},{6,22},{7,23},{8,24},{9,... | collective-permute-start | bytes 884744 | tf_op jit(solution)/shard_map/ppermute | solution.py:67
  65.2 0.0 collective-permute-done.6.d_ref
  65.2 3.1 %collective-permute-start.10 = (bf16[32,4608]{1,0:T(8,128)(2,1)S(1)}, bf16[32,4608]{1,0:T(8,128)(2,1)S(1)}, u32[]{:S(2)}, u32[]{:S(2)}) collective-permute-start(bf16[32,4608]{1,0:T(8,128)(2,1)S(1)} %collective-permute-done.6.d_ref), channel_id=1, source_target_pairs={{0,16},{1,17},{2,18},{3,19},{4,20},{5,21},{6,22},{7,23},{8,24},{9,... | collective-permute-start | bytes 884744 | tf_op jit(solution)/shard_map/ppermute | solution.py:67
  68.2 0.0 collective-permute-done.5.c_ref
  68.2 2.7 %collective-permute-start.9 = (bf16[32,4608]{1,0:T(8,128)(2,1)S(1)}, bf16[32,4608]{1,0:T(8,128)(2,1)S(1)}, u32[]{:S(2)}, u32[]{:S(2)}) collective-permute-start(bf16[32,4608]{1,0:T(8,128)(2,1)S(1)} %collective-permute-done.5.c_ref), channel_id=1, source_target_pairs={{0,16},{1,17},{2,18},{3,19},{4,20},{5,21},{6,22},{7,23},{8,24},{9,... | collective-permute-start | bytes 884744 | tf_op jit(solution)/shard_map/ppermute | solution.py:67
  71.0 0.0 collective-permute-done.4.b_ref
  71.0 1.2 %collective-permute-start.8 = (bf16[32,4608]{1,0:T(8,128)(2,1)S(1)}, bf16[32,4608]{1,0:T(8,128)(2,1)S(1)}, u32[]{:S(2)}, u32[]{:S(2)}) collective-permute-start(bf16[32,4608]{1,0:T(8,128)(2,1)S(1)} %collective-permute-done.4.b_ref), channel_id=1, source_target_pairs={{0,16},{1,17},{2,18},{3,19},{4,20},{5,21},{6,22},{7,23},{8,24},{9,... | collective-permute-start | bytes 884744 | tf_op jit(solution)/shard_map/ppermute | solution.py:67
  72.2 1.3 %restore_own.1 = (bf16[128,9216]{1,0:T(8,128)(2,1)}, f32[1,4608]{1,0:T(1,128)}, f32[1,4608]{1,0:T(1,128)}) custom-call(s32[1]{0:T(128)} %bitcast.place_ref, bf16[32,4608]{1,0:T(8,128)(2,1)S(1)} %bitcast.17, bf16[32,4608]{1,0:T(8,128)(2,1)S(1)} %collective-permute-done.4.b_ref, bf16[32,4608]{1,0:T(8,128)(2,1)S(1)} %collective-permute-done.5.c_ref, ...), custom_call_target="tpu_custom_call" | custom-call | tf_op jit(solution)/shard_map/restore_own/pallas_call | solution.py:223
  73.5 0.0 collective-permute-done.7.a_ref
  73.5 0.0 collective-permute-done.10.d_ref
  73.5 0.0 collective-permute-done.9.c_ref
  73.5 0.0 collective-permute-done.8.b_ref
  73.5 1.3 %restore_other.1 = bf16[128,9216]{1,0:T(8,128)(2,1)} custom-call(s32[1]{0:T(128)} %bitcast.place_ref, bf16[32,4608]{1,0:T(8,128)(2,1)S(1)} %collective-permute-done.7.a_ref, bf16[32,4608]{1,0:T(8,128)(2,1)S(1)} %collective-permute-done.8.b_ref, bf16[32,4608]{1,0:T(8,128)(2,1)S(1)} %collective-permute-done.9.c_ref, ...), custom_call_target="tpu_custom_call", output_to_operand_aliasing={{}: (5, {})} | custom-call | tf_op jit(solution)/shard_map/restore_other/pallas_call | solution.py:241
  (1 shorter events, 0.0 us)
Async XLA Ops:
  3.2 5.9 %collective-permute-start = (bf16[128,4608]{1,0:T(8,128)(2,1)S(1)}, bf16[128,4608]{1,0:T(8,128)(2,1)S(1)}, u32[]{:S(2)}, u32[]{:S(2)}) collective-permute-start(bf16[128,4608]{1,0:T(8,128)(2,1)S(1)} %compensate.3), channel_id=1, source_target_pairs={{0,16},{1,17},{2,18},{3,19},{4,20},{5,21},{6,22},{7,23},{8,24},{9,... | collective-permute-start | bytes 3538952 | tf_op jit(solution)/shard_map/ppermute | solution.py:67
  9.1 30.8 %copy-start = (f32[1,1,4608]{2,1,0:T(1,128)S(1)}, f32[1,1,4608]{2,1,0:T(1,128)}, u32[]{:S(2)}) copy-start(f32[1,1,4608]{2,1,0:T(1,128)} %param.9) | copy-start | bytes 55300
  9.1 30.8 %copy-start.1 = (f32[1,1,4608]{2,1,0:T(1,128)S(1)}, f32[1,1,4608]{2,1,0:T(1,128)}, u32[]{:S(2)}) copy-start(f32[1,1,4608]{2,1,0:T(1,128)} %param.10) | copy-start | bytes 55300
  9.2 30.8 %copy-start.2 = (f32[1,1,4608]{2,1,0:T(1,128)S(1)}, f32[1,1,4608]{2,1,0:T(1,128)}, u32[]{:S(2)}) copy-start(f32[1,1,4608]{2,1,0:T(1,128)} %param.11) | copy-start | bytes 55300
  9.5 7.5 %collective-permute-start.1 = (bf16[32,4608]{1,0:T(8,128)(2,1)S(1)}, bf16[32,4608]{1,0:T(8,128)(2,1)S(1)}, u32[]{:S(2)}, u32[]{:S(2)}) collective-permute-start(bf16[32,4608]{1,0:T(8,128)(2,1)S(1)} %get-tuple-element.14), channel_id=1, source_target_pairs={{0,2},{1,3},{2,0},{3,1},{4,6},{5,7},{6,4},{7,5},{8,10},{9,11},{10,... | collective-permute-start | bytes 884744 | tf_op jit(solution)/shard_map/ppermute | solution.py:71
  10.7 9.4 %collective-permute-start.2 = (bf16[32,4608]{1,0:T(8,128)(2,1)S(1)}, bf16[32,4608]{1,0:T(8,128)(2,1)S(1)}, u32[]{:S(2)}, u32[]{:S(2)}) collective-permute-start(bf16[32,4608]{1,0:T(8,128)(2,1)S(1)} %get-tuple-element.15), channel_id=1, source_target_pairs={{0,1},{1,2},{2,3},{3,0},{4,5},{5,6},{6,7},{7,4},{8,9},{9,10},{10,1... | collective-permute-start | bytes 884744 | tf_op jit(solution)/shard_map/ppermute | solution.py:71
  11.1 9.0 %collective-permute-start.3 = (bf16[32,4608]{1,0:T(8,128)(2,1)S(1)}, bf16[32,4608]{1,0:T(8,128)(2,1)S(1)}, u32[]{:S(2)}, u32[]{:S(2)}) collective-permute-start(bf16[32,4608]{1,0:T(8,128)(2,1)S(1)} %get-tuple-element.16), channel_id=1, source_target_pairs={{0,3},{1,0},{2,1},{3,2},{4,7},{5,4},{6,5},{7,6},{8,11},{9,8},{10,9... | collective-permute-start | bytes 884744 | tf_op jit(solution)/shard_map/ppermute | solution.py:71
  57.3 7.9 %collective-permute-start.6 = (bf16[32,4608]{1,0:T(8,128)(2,1)S(1)}, bf16[32,4608]{1,0:T(8,128)(2,1)S(1)}, u32[]{:S(2)}, u32[]{:S(2)}) collective-permute-start(bf16[32,4608]{1,0:T(8,128)(2,1)S(1)} %bitcast.13), channel_id=1, source_target_pairs={{0,1},{1,2},{2,3},{3,0},{4,5},{5,6},{6,7},{7,4},{8,9},{9,10},{10,1... | collective-permute-start | bytes 884744 | tf_op jit(solution)/shard_map/ppermute | solution.py:71
  58.0 10.2 %collective-permute-start.5 = (bf16[32,4608]{1,0:T(8,128)(2,1)S(1)}, bf16[32,4608]{1,0:T(8,128)(2,1)S(1)}, u32[]{:S(2)}, u32[]{:S(2)}) collective-permute-start(bf16[32,4608]{1,0:T(8,128)(2,1)S(1)} %bitcast.14), channel_id=1, source_target_pairs={{0,3},{1,0},{2,1},{3,2},{4,7},{5,4},{6,5},{7,6},{8,11},{9,8},{10,9... | collective-permute-start | bytes 884744 | tf_op jit(solution)/shard_map/ppermute | solution.py:71
  60.1 10.9 %collective-permute-start.4 = (bf16[32,4608]{1,0:T(8,128)(2,1)S(1)}, bf16[32,4608]{1,0:T(8,128)(2,1)S(1)}, u32[]{:S(2)}, u32[]{:S(2)}) collective-permute-start(bf16[32,4608]{1,0:T(8,128)(2,1)S(1)} %bitcast.15), channel_id=1, source_target_pairs={{0,2},{1,3},{2,0},{3,1},{4,6},{5,7},{6,4},{7,5},{8,10},{9,11},{10,... | collective-permute-start | bytes 884744 | tf_op jit(solution)/shard_map/ppermute | solution.py:71
  60.7 12.8 %collective-permute-start.7 = (bf16[32,4608]{1,0:T(8,128)(2,1)S(1)}, bf16[32,4608]{1,0:T(8,128)(2,1)S(1)}, u32[]{:S(2)}, u32[]{:S(2)}) collective-permute-start(bf16[32,4608]{1,0:T(8,128)(2,1)S(1)} %bitcast.16), channel_id=1, source_target_pairs={{0,16},{1,17},{2,18},{3,19},{4,20},{5,21},{6,22},{7,23},{8,24},{9,... | collective-permute-start | bytes 884744 | tf_op jit(solution)/shard_map/ppermute | solution.py:67
  65.2 8.3 %collective-permute-start.10 = (bf16[32,4608]{1,0:T(8,128)(2,1)S(1)}, bf16[32,4608]{1,0:T(8,128)(2,1)S(1)}, u32[]{:S(2)}, u32[]{:S(2)}) collective-permute-start(bf16[32,4608]{1,0:T(8,128)(2,1)S(1)} %collective-permute-done.6.d_ref), channel_id=1, source_target_pairs={{0,16},{1,17},{2,18},{3,19},{4,20},{5,21},{6,22},{7,23},{8,24},{9,... | collective-permute-start | bytes 884744 | tf_op jit(solution)/shard_map/ppermute | solution.py:67
  68.2 5.3 %collective-permute-start.9 = (bf16[32,4608]{1,0:T(8,128)(2,1)S(1)}, bf16[32,4608]{1,0:T(8,128)(2,1)S(1)}, u32[]{:S(2)}, u32[]{:S(2)}) collective-permute-start(bf16[32,4608]{1,0:T(8,128)(2,1)S(1)} %collective-permute-done.5.c_ref), channel_id=1, source_target_pairs={{0,16},{1,17},{2,18},{3,19},{4,20},{5,21},{6,22},{7,23},{8,24},{9,... | collective-permute-start | bytes 884744 | tf_op jit(solution)/shard_map/ppermute | solution.py:67
  71.0 2.6 %collective-permute-start.8 = (bf16[32,4608]{1,0:T(8,128)(2,1)S(1)}, bf16[32,4608]{1,0:T(8,128)(2,1)S(1)}, u32[]{:S(2)}, u32[]{:S(2)}) collective-permute-start(bf16[32,4608]{1,0:T(8,128)(2,1)S(1)} %collective-permute-done.4.b_ref), channel_id=1, source_target_pairs={{0,16},{1,17},{2,18},{3,19},{4,20},{5,21},{6,22},{7,23},{8,24},{9,... | collective-permute-start | bytes 884744 | tf_op jit(solution)/shard_map/ppermute | solution.py:67

commit v8 on v7

--- a/solution.py
+++ b/solution.py
@@ -83,66 +83,75 @@
     return (sent // 2 % 4 * 32 + a * a_step + b * (10 - a_step) + sent % 2 == flat).astype(F32).astype(BF16)
 
 
-def compensate_kernel(other, place_ref, codes_hbm, scales_hbm, feedback_hbm, out_ref, codes, scales, feedback, turned, spread, summed, sems):
+def compensate_kernel(place_ref, codes_hbm, scales_hbm, feedback_hbm, *refs):
+    *given_refs, kept_ref, codes, scales, feedback, turned, summed, sems = refs
     core = place_ref[0] // 16 % 2
-    half = 1 - core if other else core
-    copies = [pltpu.make_async_copy(scales_hbm, scales, sems.at[2 * CHUNKS])]
-    for i in range(CHUNKS):
-        columns = pl.ds(pl.multiple_of(half * HALF + i * CHUNK, LANES), CHUNK)
-        copies.append(pltpu.make_async_copy(codes_hbm.at[:, columns], codes.at[i], sems.at[2 * i]))
-        copies.append(pltpu.make_async_copy(feedback_hbm.at[:, columns], feedback.at[i], sems.at[2 * i + 1]))
+    copies = [pltpu.make_async_copy(scales_hbm, scales, sems.at[4 * CHUNKS])]
+    for turn in range(2):
+        start = (core if turn else 1 - core) * HALF
+        for i in range(CHUNKS):
+            columns = pl.ds(pl.multiple_of(start + i * CHUNK, LANES), CHUNK)
+            at = turn * CHUNKS + i
+            copies.append(pltpu.make_async_copy(codes_hbm.at[:, columns], codes.at[at], sems.at[2 * at]))
+            copies.append(pltpu.make_async_copy(feedback_hbm.at[:, columns], feedback.at[at], sems.at[2 * at + 1]))
     for copy in copies:
         copy.start()
-    moved = order(place_ref[0], half, False)
+    moved = [order(place_ref[0], 1 - core, False), order(place_ref[0], core, False)]
     copies[0].wait()
-    turned[0:SLAB_ROWS, :] = scales[pl.ds(half * SLAB_ROWS, SLAB_ROWS), :]
-    scale = turned[...].T
-    for at in range(SLAB_ROWS):
-        spread[:, at * LANES : (at + 1) * LANES] = jnp.broadcast_to(scale[:, at : at + 1], (ROWS, LANES))
-    for i in range(CHUNKS):
-        copies[1 + 2 * i].wait()
-        copies[2 + 2 * i].wait()
-        columns = slice(i * CHUNK, (i + 1) * CHUNK)
-        dequant = codes[i].astype(F32) * spread[:, columns]
-        summed[:, columns] = (dequant + feedback[i].astype(F32)).astype(BF16)
-    for i in range(CHUNKS):
-        columns = slice(i * CHUNK, (i + 1) * CHUNK)
-        out_ref[:, columns] = jnp.dot(moved, summed[:, columns], preferred_element_type=F32).astype(BF16)
-
-
-def compensate(other, place, codes, scales, feedback):
-    return pl.pallas_call(
-        functools.partial(compensate_kernel, other),
-        out_shape=jax.ShapeDtypeStruct((ROWS, HALF), BF16),
+    for turn in range(2):
+        half = core if turn else 1 - core
+        turned[turn, 0:SLAB_ROWS, :] = scales[pl.ds(half * SLAB_ROWS, SLAB_ROWS), :]
+        scale = turned[turn].T
+        for i in range(CHUNKS):
+            at = turn * CHUNKS + i
+            copies[1 + 2 * at].wait()
+            copies[2 + 2 * at].wait()
+            for block in range(PER_CHUNK):
+                columns = slice(block * LANES, (block + 1) * LANES)
+                place = i * PER_CHUNK + block
+                dequant = codes[at, :, columns].astype(F32) * scale[:, place : place + 1]
+                into = slice(place * LANES, (place + 1) * LANES)
+                summed[turn, :, into] = (dequant + feedback[at, :, columns].astype(F32)).astype(BF16)
+        for i in range(CHUNKS):
+            columns = slice(i * CHUNK, (i + 1) * CHUNK)
+            rows = jnp.dot(moved[turn], summed[turn, :, columns], preferred_element_type=F32).astype(BF16)
+            if turn:
+                kept_ref[:, columns] = rows
+            else:
+                for piece, given_ref in enumerate(given_refs):
+                    given_ref[:, columns] = rows[piece * 32 : (piece + 1) * 32]
+
+
+def compensate(place, codes, scales, feedback):
+    return pl.pallas_call(
+        compensate_kernel,
+        out_shape=[jax.ShapeDtypeStruct((32, HALF), BF16)] * 4 + [jax.ShapeDtypeStruct((ROWS, HALF), BF16)],
         in_specs=[SCALAR, FAR, FAR, FAR],
-        out_specs=WHOLE,
+        out_specs=[WHOLE] * 5,
         scratch_shapes=[
-            pltpu.VMEM((CHUNKS, ROWS, CHUNK), jnp.int32),
+            pltpu.VMEM((2 * CHUNKS, ROWS, CHUNK), jnp.int32),
             pltpu.VMEM((WIDTH // LANES, ROWS), F32),
-            pltpu.VMEM((CHUNKS, ROWS, CHUNK), BF16),
-            pltpu.VMEM((ROWS, LANES), F32),
-            pltpu.VMEM((ROWS, HALF), F32),
-            pltpu.VMEM((ROWS, HALF), BF16),
-            pltpu.SemaphoreType.DMA((2 * CHUNKS + 1,)),
+            pltpu.VMEM((2 * CHUNKS, ROWS, CHUNK), BF16),
+            pltpu.VMEM((2, ROWS, LANES), F32),
+            pltpu.VMEM((2, ROWS, HALF), BF16),
+            pltpu.SemaphoreType.DMA((4 * CHUNKS + 1,)),
         ],
         compiler_params=params(),
-        cost_estimate=pl.CostEstimate(flops=2 * ROWS * ROWS * HALF, bytes_accessed=8 * ROWS * HALF, transcendentals=0),
         name="compensate",
     )(place, in_hbm(codes), in_hbm(scales), in_hbm(feedback))
 
 
-def pair_sum_kernel(own_ref, other_ref, *out_refs):
-    for piece, out_ref in enumerate(out_refs):
-        rows = slice(piece * 32, (piece + 1) * 32)
-        out_ref[...] = (own_ref[rows, :].astype(F32) + other_ref[rows, :].astype(F32)).astype(BF16)
-
-
-def pair_sum(own, other):
-    return pl.pallas_call(
-        pair_sum_kernel,
-        out_shape=[jax.ShapeDtypeStruct((32, HALF), BF16)] * 4,
+def pair_sum_kernel(piece, own_ref, other_ref, out_ref):
+    own = own_ref[piece * 32 : (piece + 1) * 32, :].astype(F32)
+    out_ref[...] = (own + other_ref[...].astype(F32)).astype(BF16)
+
+
+def pair_sum(piece, own, other):
+    return pl.pallas_call(
+        functools.partial(pair_sum_kernel, piece),
+        out_shape=jax.ShapeDtypeStruct((32, HALF), BF16),
         in_specs=[WHOLE] * 2,
-        out_specs=[WHOLE] * 4,
+        out_specs=WHOLE,
         compiler_params=params(),
         name="pair_sum",
     )(own, other)
@@ -194,11 +203,11 @@
 
 
 def place_half(place, half, blocks, weights_hbm, staged, sems):
-    own, across, after, before = blocks
     moved = order(place, half, True)
+    ordered = [blocks[i] for i in (0, 1, 3, 2)]
     copies = []
     for i in range(CHUNKS):
-        rows = jnp.concatenate([block[:, i * CHUNK : (i + 1) * CHUNK] for block in (own, after, across, before)], axis=0)
+        rows = jnp.concatenate([block[:, i * CHUNK : (i + 1) * CHUNK] for block in ordered], axis=0)
         staged[i] = jnp.dot(moved, rows, preferred_element_type=F32).astype(BF16)
         to = pl.ds(pl.multiple_of(half * HALF + i * CHUNK, LANES), CHUNK)
         copies.append(pltpu.make_async_copy(staged.at[i], weights_hbm.at[:, to], sems.at[i]))
@@ -254,16 +263,14 @@
     place = lax.axis_index(AXES).astype(jnp.int32).reshape(1)
     codes, feed = grad_codes[0, 0], feedback[0, 0]
     turned = jnp.swapaxes(scales[0, 0], 0, 1)
-    given = compensate(True, place, codes, turned, feed)
-    taken = swap_cores(given)
-    kept = compensate(False, place, codes, turned, feed)
-    own, *others = pair_sum(kept, taken)
-    partial = line_sum(own, [send(others[step - 1], step) for step in (2, 1, 3)])
+    *given, kept = compensate(place, codes, turned, feed)
+    taken = {piece: swap_cores(given[piece]) for piece in (2, 1, 3, 0)}
+    sums = {piece: pair_sum(piece, kept, taken[piece]) for piece in (2, 1, 3, 0)}
+    partial = line_sum(sums[0], [send(sums[step], step) for step in (2, 1, 3)])
     arrived = exchange(partial.reshape(32, *SLAB), owner_groups())
     adam_dir, new_master, copies = adam(arrived, master[0], moment[0], second[0])
     joined = exchange(copies, owner_groups()).reshape(32, HALF)
-    across, after, before = [send(joined, 4 - step) for step in (2, 1, 3)]
-    mine = [joined, across, after, before]
+    mine = [joined] + [send(joined, step) for step in (3, 1, 2)]
     theirs = [swap_cores(block) for block in mine]
     weights, adam_dir, new_master = restore_own(place, mine, adam_dir, new_master)
     weights = restore_other(place, theirs, weights)

time: 75 us -> 74.3 us (level)
  Pallas kernels: 8.32 us -> 6.97 us
    pallas_call x3 -> x5, Pallas kernels: 5.43 us -> 4.09 us  [the longest x1 3.81 us: compensate(): pl.pallas_call(compensate_kernel, out_shape=[jax.ShapeDtypeStruct((32, HA...]
    ppermute x6, starting transfers between devices: 7.29 us -> 8.18 us  [send(): return lax.ppermute(array, AXES, shifted(step))]
    ppermute x5 -> x8, waiting for transfers between devices: 0.01 us -> 0.89 us  [swap_cores(): return lax.ppermute(array, AXES, SWAP)]
    ppermute x5 -> x8, starting transfers between devices: 14.8 us -> 14.7 us  [swap_cores(): return lax.ppermute(array, AXES, SWAP)]
  transfers between devices with their start and end apart: 11 -> 14, of which waited for: 2 -> 4; matrix products, arithmetic and copies ran while one was open for 0% -> 0% of each run, Pallas kernels for 5% -> 2%
where the time goes in v8:
time: 74.3 us; the launch traced here: 74.2 us
  blocking collectives  36.3 us (49%)
  starting transfers between devices  22.8 us (31%)
  waiting for transfers between devices  7.16 us (10%)
  Pallas kernels  6.97 us (9%)
  between operations  0.76 us (1%)
    all_to_all x2, blocking collectives, exchange(): lax.all_to_all(array, AXES, 0, 0, axis_index_groups=groups, tiled=True)  36.3 us
    ppermute x8, starting transfers between devices, swap_cores(): return lax.ppermute(array, AXES, SWAP)  14.7 us
    ppermute x6, starting transfers between devices, send(): return lax.ppermute(array, AXES, shifted(step))  8.18 us
    ppermute x6, waiting for transfers between devices, send(): return lax.ppermute(array, AXES, shifted(step))  6.27 us
    pallas_call x1, Pallas kernels, compensate(): pl.pallas_call(compensate_kernel, out_shape=[jax.ShapeDtypeStruct((32, HA...  3.81 us
  transfers between devices with their start and end apart: 14, of which 4 were waited for; matrix products, arithmetic and copies ran while one was open for 0% of the time, Pallas kernels for 2%

profile of v8, /device:TPU:1, one launch (start us, length us, event | category | flops | bytes accessed | tf_op | source)
XLA Modules:
  0.0 74.2 jit_solution(247833089850943417)
XLA Ops:
  0.6 3.8 %compensate.1 = (bf16[32,4608]{1,0:T(8,128)(2,1)S(1)}, bf16[32,4608]{1,0:T(8,128)(2,1)S(1)}, bf16[32,4608]{1,0:T(8,128)(2,1)S(1)}, bf16[32,4608]{1,0:T(8,128)(2,1)S(1)}, bf16[128,4608]{1,0:T(8,128)(2,1)S(1)}) custom-call(s32[1]{0:T(128)} %bitcast.place_ref, s32[128,9216]{1,0:T(8,128)} %bitcast.21, f32[72,128]{1,0:T(8,128)} %bitcast.24, ...), custom_call_target="tpu_custom_call" | custom-call | tf_op jit(solution)/shard_map/compensate/pallas_call | solution.py:126
  4.5 3.3 %collective-permute-start.1 = (bf16[32,4608]{1,0:T(8,128)(2,1)S(1)}, bf16[32,4608]{1,0:T(8,128)(2,1)S(1)}, u32[]{:S(2)}, u32[]{:S(2)}) collective-permute-start(bf16[32,4608]{1,0:T(8,128)(2,1)S(1)} %get-tuple-element.16), channel_id=1, source_target_pairs={{0,16},{1,17},{2,18},{3,19},{4,20},{5,21},{6,22},{7,23},{8,24},{9,... | collective-permute-start | bytes 884744 | tf_op jit(solution)/shard_map/ppermute | solution.py:67
  7.8 0.1 collective-permute-start.3
  7.9 0.4 collective-permute-start.5
  8.3 0.1 collective-permute-start
  8.4 0.6 collective-permute-done.1.other_ref
  9.0 0.1 pair_sum.5
  9.1 1.3 %collective-permute-start.2 = (bf16[32,4608]{1,0:T(8,128)(2,1)S(1)}, bf16[32,4608]{1,0:T(8,128)(2,1)S(1)}, u32[]{:S(2)}, u32[]{:S(2)}) collective-permute-start(bf16[32,4608]{1,0:T(8,128)(2,1)S(1)} %pair_sum.5), channel_id=1, source_target_pairs={{0,2},{1,3},{2,0},{3,1},{4,6},{5,7},{6,4},{7,5},{8,10},{9,11},{10,... | collective-permute-start | bytes 884744 | tf_op jit(solution)/shard_map/ppermute | solution.py:71
  10.3 0.0 collective-permute-done.3.other_ref
  10.3 0.1 pair_sum.6
  10.4 0.5 collective-permute-start.4
  10.9 0.0 collective-permute-done.5.other_ref
  10.9 0.1 pair_sum.7
  11.0 0.0 copy-start
  11.0 0.0 copy-start.1
  11.0 0.0 copy-start.2
  11.0 2.4 %collective-permute-start.6 = (bf16[32,4608]{1,0:T(8,128)(2,1)S(1)}, bf16[32,4608]{1,0:T(8,128)(2,1)S(1)}, u32[]{:S(2)}, u32[]{:S(2)}) collective-permute-start(bf16[32,4608]{1,0:T(8,128)(2,1)S(1)} %pair_sum.7), channel_id=1, source_target_pairs={{0,3},{1,0},{2,1},{3,2},{4,7},{5,4},{6,5},{7,6},{8,11},{9,8},{10,9... | collective-permute-start | bytes 884744 | tf_op jit(solution)/shard_map/ppermute | solution.py:71
  13.4 0.0 collective-permute-done.other_ref
  13.4 0.1 pair_sum.4.own_ref
  13.4 3.1 %collective-permute-done.2.a_ref = bf16[32,4608]{1,0:T(8,128)(2,1)S(1)} collective-permute-done((bf16[32,4608]{1,0:T(8,128)(2,1)S(1)}, bf16[32,4608]{1,0:T(8,128)(2,1)S(1)}, u32[]{:S(2)}, u32[]{:S(2)}) %collective-permute-start.2) | collective-permute-done | bytes 294944 | tf_op jit(solution)/shard_map/ppermute | solution.py:71
  16.6 3.1 %collective-permute-done.4.b_ref = bf16[32,4608]{1,0:T(8,128)(2,1)S(1)} collective-permute-done((bf16[32,4608]{1,0:T(8,128)(2,1)S(1)}, bf16[32,4608]{1,0:T(8,128)(2,1)S(1)}, u32[]{:S(2)}, u32[]{:S(2)}) %collective-permute-start.4) | collective-permute-done | bytes 294944 | tf_op jit(solution)/shard_map/ppermute | solution.py:71
  19.7 0.0 collective-permute-done.6.c_ref
  19.7 0.1 line_sum.1
  19.8 0.1 reshape.16
  19.9 19.5 %all_to_all.10.arrived_ref = bf16[32,2,2304]{2,1,0:T(2,128)(2,1)S(1)} all-to-all(bf16[32,2,2304]{2,1,0:T(2,128)(2,1)S(1)} %reshape.16), channel_id=1, replica_groups={{0,32,4,36,8,40,12,44,64,96,68,100,72,104,76,108,128,160,132,164,136,16..., dimensions={0} | all-to-all | bytes 589824 | tf_op jit(solution)/shard_map/all_to_all | solution.py:75
  39.4 0.0 copy-done
  39.4 0.0 copy-done.1
  39.4 0.0 copy-done.2
  39.4 0.1 adam.1
  39.6 16.8 %all_to_all.11 = bf16[32,2,2304]{2,1,0:T(2,128)(2,1)S(1)} all-to-all(bf16[32,2,2304]{2,1,0:T(2,128)(2,1)S(1)} %get-tuple-element.19), channel_id=1, replica_groups={{0,32,4,36,8,40,12,44,64,96,68,100,72,104,76,108,128,160,132,164,136,16..., dimensions={0} | all-to-all | bytes 589824 | tf_op jit(solution)/shard_map/all_to_all | solution.py:75
  56.4 1.4 %collective-permute-start.9 = (bf16[32,4608]{1,0:T(8,128)(2,1)S(1)}, bf16[32,4608]{1,0:T(8,128)(2,1)S(1)}, u32[]{:S(2)}, u32[]{:S(2)}) collective-permute-start(bf16[32,4608]{1,0:T(8,128)(2,1)S(1)} %bitcast.13), channel_id=1, source_target_pairs={{0,2},{1,3},{2,0},{3,1},{4,6},{5,7},{6,4},{7,5},{8,10},{9,11},{10,... | collective-permute-start | bytes 884744 | tf_op jit(solution)/shard_map/ppermute | solution.py:71
  57.8 1.1 %collective-permute-start.8 = (bf16[32,4608]{1,0:T(8,128)(2,1)S(1)}, bf16[32,4608]{1,0:T(8,128)(2,1)S(1)}, u32[]{:S(2)}, u32[]{:S(2)}) collective-permute-start(bf16[32,4608]{1,0:T(8,128)(2,1)S(1)} %bitcast.14), channel_id=1, source_target_pairs={{0,1},{1,2},{2,3},{3,0},{4,5},{5,6},{6,7},{7,4},{8,9},{9,10},{10,1... | collective-permute-start | bytes 884744 | tf_op jit(solution)/shard_map/ppermute | solution.py:71
  58.9 1.6 %collective-permute-start.7 = (bf16[32,4608]{1,0:T(8,128)(2,1)S(1)}, bf16[32,4608]{1,0:T(8,128)(2,1)S(1)}, u32[]{:S(2)}, u32[]{:S(2)}) collective-permute-start(bf16[32,4608]{1,0:T(8,128)(2,1)S(1)} %bitcast.15), channel_id=1, source_target_pairs={{0,3},{1,0},{2,1},{3,2},{4,7},{5,4},{6,5},{7,6},{8,11},{9,8},{10,9... | collective-permute-start | bytes 884744 | tf_op jit(solution)/shard_map/ppermute | solution.py:71
  60.5 5.4 %collective-permute-start.10 = (bf16[32,4608]{1,0:T(8,128)(2,1)S(1)}, bf16[32,4608]{1,0:T(8,128)(2,1)S(1)}, u32[]{:S(2)}, u32[]{:S(2)}) collective-permute-start(bf16[32,4608]{1,0:T(8,128)(2,1)S(1)} %bitcast.16), channel_id=1, source_target_pairs={{0,16},{1,17},{2,18},{3,19},{4,20},{5,21},{6,22},{7,23},{8,24},{9,... | collective-permute-start | bytes 884744 | tf_op jit(solution)/shard_map/ppermute | solution.py:67
  65.9 0.0 collective-permute-done.9.d_ref
  65.9 2.2 %collective-permute-start.13 = (bf16[32,4608]{1,0:T(8,128)(2,1)S(1)}, bf16[32,4608]{1,0:T(8,128)(2,1)S(1)}, u32[]{:S(2)}, u32[]{:S(2)}) collective-permute-start(bf16[32,4608]{1,0:T(8,128)(2,1)S(1)} %collective-permute-done.9.d_ref), channel_id=1, source_target_pairs={{0,16},{1,17},{2,18},{3,19},{4,20},{5,21},{6,22},{7,23},{8,24},{9,... | collective-permute-start | bytes 884744 | tf_op jit(solution)/shard_map/ppermute | solution.py:67
  68.1 0.0 collective-permute-done.8.c_ref
  68.1 3.1 %collective-permute-start.12 = (bf16[32,4608]{1,0:T(8,128)(2,1)S(1)}, bf16[32,4608]{1,0:T(8,128)(2,1)S(1)}, u32[]{:S(2)}, u32[]{:S(2)}) collective-permute-start(bf16[32,4608]{1,0:T(8,128)(2,1)S(1)} %collective-permute-done.8.c_ref), channel_id=1, source_target_pairs={{0,16},{1,17},{2,18},{3,19},{4,20},{5,21},{6,22},{7,23},{8,24},{9,... | collective-permute-start | bytes 884744 | tf_op jit(solution)/shard_map/ppermute | solution.py:67
  71.2 0.0 collective-permute-done.7.b_ref
  71.2 0.0 collective-permute-start.11
  71.2 1.3 %restore_own.1 = (bf16[128,9216]{1,0:T(8,128)(2,1)}, f32[1,4608]{1,0:T(1,128)}, f32[1,4608]{1,0:T(1,128)}) custom-call(s32[1]{0:T(128)} %bitcast.place_ref, bf16[32,4608]{1,0:T(8,128)(2,1)S(1)} %bitcast.17, bf16[32,4608]{1,0:T(8,128)(2,1)S(1)} %collective-permute-done.7.b_ref, bf16[32,4608]{1,0:T(8,128)(2,1)S(1)} %collective-permute-done.8.c_ref, ...), custom_call_target="tpu_custom_call" | custom-call | tf_op jit(solution)/shard_map/restore_own/pallas_call | solution.py:232
  72.6 0.0 collective-permute-done.10.a_ref
  72.6 0.0 collective-permute-done.13.d_ref
  72.6 0.0 collective-permute-done.12.c_ref
  72.6 0.3 collective-permute-done.11.b_ref
  72.9 1.3 %restore_other.1 = bf16[128,9216]{1,0:T(8,128)(2,1)} custom-call(s32[1]{0:T(128)} %bitcast.place_ref, bf16[32,4608]{1,0:T(8,128)(2,1)S(1)} %collective-permute-done.10.a_ref, bf16[32,4608]{1,0:T(8,128)(2,1)S(1)} %collective-permute-done.11.b_ref, bf16[32,4608]{1,0:T(8,128)(2,1)S(1)} %collective-permute-done.12.c_ref, ...), custom_call_target="tpu_custom_call", output_to_operand_aliasing={{}: (5, {})} | custom-call | tf_op jit(solution)/shard_map/restore_other/pallas_call | solution.py:250
  (1 shorter events, 0.0 us)
Async XLA Ops:
  4.5 4.5 %collective-permute-start.1 = (bf16[32,4608]{1,0:T(8,128)(2,1)S(1)}, bf16[32,4608]{1,0:T(8,128)(2,1)S(1)}, u32[]{:S(2)}, u32[]{:S(2)}) collective-permute-start(bf16[32,4608]{1,0:T(8,128)(2,1)S(1)} %get-tuple-element.16), channel_id=1, source_target_pairs={{0,16},{1,17},{2,18},{3,19},{4,20},{5,21},{6,22},{7,23},{8,24},{9,... | collective-permute-start | bytes 884744 | tf_op jit(solution)/shard_map/ppermute | solution.py:67
  7.8 2.5 %collective-permute-start.3 = (bf16[32,4608]{1,0:T(8,128)(2,1)S(1)}, bf16[32,4608]{1,0:T(8,128)(2,1)S(1)}, u32[]{:S(2)}, u32[]{:S(2)}) collective-permute-start(bf16[32,4608]{1,0:T(8,128)(2,1)S(1)} %get-tuple-element.17), channel_id=1, source_target_pairs={{0,16},{1,17},{2,18},{3,19},{4,20},{5,21},{6,22},{7,23},{8,24},{9,... | collective-permute-start | bytes 884744 | tf_op jit(solution)/shard_map/ppermute | solution.py:67
  7.9 3.0 %collective-permute-start.5 = (bf16[32,4608]{1,0:T(8,128)(2,1)S(1)}, bf16[32,4608]{1,0:T(8,128)(2,1)S(1)}, u32[]{:S(2)}, u32[]{:S(2)}) collective-permute-start(bf16[32,4608]{1,0:T(8,128)(2,1)S(1)} %get-tuple-element.18), channel_id=1, source_target_pairs={{0,16},{1,17},{2,18},{3,19},{4,20},{5,21},{6,22},{7,23},{8,24},{9,... | collective-permute-start | bytes 884744 | tf_op jit(solution)/shard_map/ppermute | solution.py:67
  8.3 5.1 %collective-permute-start = (bf16[32,4608]{1,0:T(8,128)(2,1)S(1)}, bf16[32,4608]{1,0:T(8,128)(2,1)S(1)}, u32[]{:S(2)}, u32[]{:S(2)}) collective-permute-start(bf16[32,4608]{1,0:T(8,128)(2,1)S(1)} %get-tuple-element.15), channel_id=1, source_target_pairs={{0,16},{1,17},{2,18},{3,19},{4,20},{5,21},{6,22},{7,23},{8,24},{9,... | collective-permute-start | bytes 884744 | tf_op jit(solution)/shard_map/ppermute | solution.py:67
  9.1 7.5 %collective-permute-start.2 = (bf16[32,4608]{1,0:T(8,128)(2,1)S(1)}, bf16[32,4608]{1,0:T(8,128)(2,1)S(1)}, u32[]{:S(2)}, u32[]{:S(2)}) collective-permute-start(bf16[32,4608]{1,0:T(8,128)(2,1)S(1)} %pair_sum.5), channel_id=1, source_target_pairs={{0,2},{1,3},{2,0},{3,1},{4,6},{5,7},{6,4},{7,5},{8,10},{9,11},{10,... | collective-permute-start | bytes 884744 | tf_op jit(solution)/shard_map/ppermute | solution.py:71
  10.4 9.3 %collective-permute-start.4 = (bf16[32,4608]{1,0:T(8,128)(2,1)S(1)}, bf16[32,4608]{1,0:T(8,128)(2,1)S(1)}, u32[]{:S(2)}, u32[]{:S(2)}) collective-permute-start(bf16[32,4608]{1,0:T(8,128)(2,1)S(1)} %pair_sum.6), channel_id=1, source_target_pairs={{0,1},{1,2},{2,3},{3,0},{4,5},{5,6},{6,7},{7,4},{8,9},{9,10},{10,1... | collective-permute-start | bytes 884744 | tf_op jit(solution)/shard_map/ppermute | solution.py:71
  11.0 28.5 %copy-start = (f32[1,1,4608]{2,1,0:T(1,128)S(1)}, f32[1,1,4608]{2,1,0:T(1,128)}, u32[]{:S(2)}) copy-start(f32[1,1,4608]{2,1,0:T(1,128)} %param.9) | copy-start | bytes 55300
  11.0 28.4 %copy-start.1 = (f32[1,1,4608]{2,1,0:T(1,128)S(1)}, f32[1,1,4608]{2,1,0:T(1,128)}, u32[]{:S(2)}) copy-start(f32[1,1,4608]{2,1,0:T(1,128)} %param.10) | copy-start | bytes 55300
  11.0 28.4 %copy-start.2 = (f32[1,1,4608]{2,1,0:T(1,128)S(1)}, f32[1,1,4608]{2,1,0:T(1,128)}, u32[]{:S(2)}) copy-start(f32[1,1,4608]{2,1,0:T(1,128)} %param.11) | copy-start | bytes 55300
  11.0 8.7 %collective-permute-start.6 = (bf16[32,4608]{1,0:T(8,128)(2,1)S(1)}, bf16[32,4608]{1,0:T(8,128)(2,1)S(1)}, u32[]{:S(2)}, u32[]{:S(2)}) collective-permute-start(bf16[32,4608]{1,0:T(8,128)(2,1)S(1)} %pair_sum.7), channel_id=1, source_target_pairs={{0,3},{1,0},{2,1},{3,2},{4,7},{5,4},{6,5},{7,6},{8,11},{9,8},{10,9... | collective-permute-start | bytes 884744 | tf_op jit(solution)/shard_map/ppermute | solution.py:71
  56.4 9.5 %collective-permute-start.9 = (bf16[32,4608]{1,0:T(8,128)(2,1)S(1)}, bf16[32,4608]{1,0:T(8,128)(2,1)S(1)}, u32[]{:S(2)}, u32[]{:S(2)}) collective-permute-start(bf16[32,4608]{1,0:T(8,128)(2,1)S(1)} %bitcast.13), channel_id=1, source_target_pairs={{0,2},{1,3},{2,0},{3,1},{4,6},{5,7},{6,4},{7,5},{8,10},{9,11},{10,... | collective-permute-start | bytes 884744 | tf_op jit(solution)/shard_map/ppermute | solution.py:71
  57.8 10.3 %collective-permute-start.8 = (bf16[32,4608]{1,0:T(8,128)(2,1)S(1)}, bf16[32,4608]{1,0:T(8,128)(2,1)S(1)}, u32[]{:S(2)}, u32[]{:S(2)}) collective-permute-start(bf16[32,4608]{1,0:T(8,128)(2,1)S(1)} %bitcast.14), channel_id=1, source_target_pairs={{0,1},{1,2},{2,3},{3,0},{4,5},{5,6},{6,7},{7,4},{8,9},{9,10},{10,1... | collective-permute-start | bytes 884744 | tf_op jit(solution)/shard_map/ppermute | solution.py:71
  58.9 12.3 %collective-permute-start.7 = (bf16[32,4608]{1,0:T(8,128)(2,1)S(1)}, bf16[32,4608]{1,0:T(8,128)(2,1)S(1)}, u32[]{:S(2)}, u32[]{:S(2)}) collective-permute-start(bf16[32,4608]{1,0:T(8,128)(2,1)S(1)} %bitcast.15), channel_id=1, source_target_pairs={{0,3},{1,0},{2,1},{3,2},{4,7},{5,4},{6,5},{7,6},{8,11},{9,8},{10,9... | collective-permute-start | bytes 884744 | tf_op jit(solution)/shard_map/ppermute | solution.py:71
  60.5 12.1 %collective-permute-start.10 = (bf16[32,4608]{1,0:T(8,128)(2,1)S(1)}, bf16[32,4608]{1,0:T(8,128)(2,1)S(1)}, u32[]{:S(2)}, u32[]{:S(2)}) collective-permute-start(bf16[32,4608]{1,0:T(8,128)(2,1)S(1)} %bitcast.16), channel_id=1, source_target_pairs={{0,16},{1,17},{2,18},{3,19},{4,20},{5,21},{6,22},{7,23},{8,24},{9,... | collective-permute-start | bytes 884744 | tf_op jit(solution)/shard_map/ppermute | solution.py:67
  65.9 6.6 %collective-permute-start.13 = (bf16[32,4608]{1,0:T(8,128)(2,1)S(1)}, bf16[32,4608]{1,0:T(8,128)(2,1)S(1)}, u32[]{:S(2)}, u32[]{:S(2)}) collective-permute-start(bf16[32,4608]{1,0:T(8,128)(2,1)S(1)} %collective-permute-done.9.d_ref), channel_id=1, source_target_pairs={{0,16},{1,17},{2,18},{3,19},{4,20},{5,21},{6,22},{7,23},{8,24},{9,... | collective-permute-start | bytes 884744 | tf_op jit(solution)/shard_map/ppermute | solution.py:67
  68.1 4.4 %collective-permute-start.12 = (bf16[32,4608]{1,0:T(8,128)(2,1)S(1)}, bf16[32,4608]{1,0:T(8,128)(2,1)S(1)}, u32[]{:S(2)}, u32[]{:S(2)}) collective-permute-start(bf16[32,4608]{1,0:T(8,128)(2,1)S(1)} %collective-permute-done.8.c_ref), channel_id=1, source_target_pairs={{0,16},{1,17},{2,18},{3,19},{4,20},{5,21},{6,22},{7,23},{8,24},{9,... | collective-permute-start | bytes 884744 | tf_op jit(solution)/shard_map/ppermute | solution.py:67
  71.2 1.6 %collective-permute-start.11 = (bf16[32,4608]{1,0:T(8,128)(2,1)S(1)}, bf16[32,4608]{1,0:T(8,128)(2,1)S(1)}, u32[]{:S(2)}, u32[]{:S(2)}) collective-permute-start(bf16[32,4608]{1,0:T(8,128)(2,1)S(1)} %collective-permute-done.7.b_ref), channel_id=1, source_target_pairs={{0,16},{1,17},{2,18},{3,19},{4,20},{5,21},{6,22},{7,23},{8,24},{9,... | collective-permute-start | bytes 884744 | tf_op jit(solution)/shard_map/ppermute | solution.py:67

commit v9 on v8

--- a/solution.py
+++ b/solution.py
@@ -96,7 +96,7 @@
             copies.append(pltpu.make_async_copy(feedback_hbm.at[:, columns], feedback.at[at], sems.at[2 * at + 1]))
     for copy in copies:
         copy.start()
-    moved = [order(place_ref[0], 1 - core, False), order(place_ref[0], core, False)]
+    moved = order(place_ref[0], 1 - core, False)
     copies[0].wait()
     for turn in range(2):
         half = core if turn else 1 - core
@@ -111,13 +111,12 @@
                 place = i * PER_CHUNK + block
                 dequant = codes[at, :, columns].astype(F32) * scale[:, place : place + 1]
                 into = slice(place * LANES, (place + 1) * LANES)
-                summed[turn, :, into] = (dequant + feedback[at, :, columns].astype(F32)).astype(BF16)
-        for i in range(CHUNKS):
-            columns = slice(i * CHUNK, (i + 1) * CHUNK)
-            rows = jnp.dot(moved[turn], summed[turn, :, columns], preferred_element_type=F32).astype(BF16)
-            if turn:
-                kept_ref[:, columns] = rows
-            else:
+                held = kept_ref if turn else summed
+                held[:, into] = (dequant + feedback[at, :, columns].astype(F32)).astype(BF16)
+        if turn == 0:
+            for i in range(CHUNKS):
+                columns = slice(i * CHUNK, (i + 1) * CHUNK)
+                rows = jnp.dot(moved, summed[:, columns], preferred_element_type=F32).astype(BF16)
                 for piece, given_ref in enumerate(given_refs):
                     given_ref[:, columns] = rows[piece * 32 : (piece + 1) * 32]
 
@@ -133,12 +132,30 @@
             pltpu.VMEM((WIDTH // LANES, ROWS), F32),
             pltpu.VMEM((2 * CHUNKS, ROWS, CHUNK), BF16),
             pltpu.VMEM((2, ROWS, LANES), F32),
-            pltpu.VMEM((2, ROWS, HALF), BF16),
+            pltpu.VMEM((ROWS, HALF), BF16),
             pltpu.SemaphoreType.DMA((4 * CHUNKS + 1,)),
         ],
         compiler_params=params(),
         name="compensate",
     )(place, in_hbm(codes), in_hbm(scales), in_hbm(feedback))
+
+
+def put_in_order_kernel(place_ref, in_ref, out_ref):
+    moved = order(place_ref[0], place_ref[0] // 16 % 2, False)
+    for i in range(CHUNKS):
+        columns = slice(i * CHUNK, (i + 1) * CHUNK)
+        out_ref[:, columns] = jnp.dot(moved, in_ref[:, columns], preferred_element_type=F32).astype(BF16)
+
+
+def put_in_order(place, rows):
+    return pl.pallas_call(
+        put_in_order_kernel,
+        out_shape=jax.ShapeDtypeStruct((ROWS, HALF), BF16),
+        in_specs=[SCALAR, WHOLE],
+        out_specs=WHOLE,
+        compiler_params=params(),
+        name="put_in_order",
+    )(place, rows)
 
 
 def pair_sum_kernel(piece, own_ref, other_ref, out_ref):
@@ -265,6 +282,7 @@
     turned = jnp.swapaxes(scales[0, 0], 0, 1)
     *given, kept = compensate(place, codes, turned, feed)
     taken = {piece: swap_cores(given[piece]) for piece in (2, 1, 3, 0)}
+    kept = put_in_order(place, kept)
     sums = {piece: pair_sum(piece, kept, taken[piece]) for piece in (2, 1, 3, 0)}
     partial = line_sum(sums[0], [send(sums[step], step) for step in (2, 1, 3)])
     arrived = exchange(partial.reshape(32, *SLAB), owner_groups())

time: 74.3 us -> 74 us (level)
  transfers between devices with their start and end apart: 14 -> 14, of which waited for: 4 -> 4; matrix products, arithmetic and copies ran while one was open for 0% -> 0% of each run, Pallas kernels for 2% -> 3%
where the time goes in v9:
time: 74 us; the launch traced here: 73.9 us
  blocking collectives  36.3 us (49%)
  starting transfers between devices  22.8 us (31%)
  Pallas kernels  7.16 us (10%)
  waiting for transfers between devices  6.67 us (9%)
  between operations  0.76 us (1%)
    all_to_all x2, blocking collectives, exchange(): lax.all_to_all(array, AXES, 0, 0, axis_index_groups=groups, tiled=True)  36.3 us
    ppermute x8, starting transfers between devices, swap_cores(): return lax.ppermute(array, AXES, SWAP)  14.7 us
    ppermute x6, starting transfers between devices, send(): return lax.ppermute(array, AXES, shifted(step))  8.17 us
    ppermute x6, waiting for transfers between devices, send(): return lax.ppermute(array, AXES, shifted(step))  6.27 us
    pallas_call x1, Pallas kernels, compensate(): pl.pallas_call(compensate_kernel, out_shape=[jax.ShapeDtypeStruct((32, HA...  3.52 us
  transfers between devices with their start and end apart: 14, of which 4 were waited for; matrix products, arithmetic and copies ran while one was open for 0% of the time, Pallas kernels for 3%

profile of v9, /device:TPU:1, one launch (start us, length us, event | category | flops | bytes accessed | tf_op | source)
XLA Modules:
  0.0 73.9 jit_solution(17978515377159584954)
XLA Ops:
  0.6 3.5 %compensate.1 = (bf16[32,4608]{1,0:T(8,128)(2,1)S(1)}, bf16[32,4608]{1,0:T(8,128)(2,1)S(1)}, bf16[32,4608]{1,0:T(8,128)(2,1)S(1)}, bf16[32,4608]{1,0:T(8,128)(2,1)S(1)}, bf16[128,4608]{1,0:T(8,128)(2,1)S(1)}) custom-call(s32[1]{0:T(128)} %bitcast.place_ref, s32[128,9216]{1,0:T(8,128)} %bitcast.21, f32[72,128]{1,0:T(8,128)} %bitcast.24, ...), custom_call_target="tpu_custom_call" | custom-call | tf_op jit(solution)/shard_map/compensate/pallas_call | solution.py:125
  4.2 3.3 %collective-permute-start.1 = (bf16[32,4608]{1,0:T(8,128)(2,1)S(1)}, bf16[32,4608]{1,0:T(8,128)(2,1)S(1)}, u32[]{:S(2)}, u32[]{:S(2)}) collective-permute-start(bf16[32,4608]{1,0:T(8,128)(2,1)S(1)} %get-tuple-element.16), channel_id=1, source_target_pairs={{0,16},{1,17},{2,18},{3,19},{4,20},{5,21},{6,22},{7,23},{8,24},{9,... | collective-permute-start | bytes 884744 | tf_op jit(solution)/shard_map/ppermute | solution.py:67
  7.5 0.1 collective-permute-start.3
  7.6 0.4 collective-permute-start.5
  8.0 0.1 collective-permute-start
  8.1 0.5 put_in_order.1.own_ref
  8.6 0.1 collective-permute-done.1.other_ref
  8.7 0.1 pair_sum.5
  8.8 1.3 %collective-permute-start.2 = (bf16[32,4608]{1,0:T(8,128)(2,1)S(1)}, bf16[32,4608]{1,0:T(8,128)(2,1)S(1)}, u32[]{:S(2)}, u32[]{:S(2)}) collective-permute-start(bf16[32,4608]{1,0:T(8,128)(2,1)S(1)} %pair_sum.5), channel_id=1, source_target_pairs={{0,2},{1,3},{2,0},{3,1},{4,6},{5,7},{6,4},{7,5},{8,10},{9,11},{10,... | collective-permute-start | bytes 884744 | tf_op jit(solution)/shard_map/ppermute | solution.py:71
  10.0 0.0 collective-permute-done.3.other_ref
  10.0 0.1 pair_sum.6
  10.1 0.5 collective-permute-start.4
  10.6 0.0 collective-permute-done.5.other_ref
  10.6 0.1 pair_sum.7
  10.7 0.0 copy-start
  10.7 0.0 copy-start.1
  10.7 0.0 copy-start.2
  10.7 2.4 %collective-permute-start.6 = (bf16[32,4608]{1,0:T(8,128)(2,1)S(1)}, bf16[32,4608]{1,0:T(8,128)(2,1)S(1)}, u32[]{:S(2)}, u32[]{:S(2)}) collective-permute-start(bf16[32,4608]{1,0:T(8,128)(2,1)S(1)} %pair_sum.7), channel_id=1, source_target_pairs={{0,3},{1,0},{2,1},{3,2},{4,7},{5,4},{6,5},{7,6},{8,11},{9,8},{10,9... | collective-permute-start | bytes 884744 | tf_op jit(solution)/shard_map/ppermute | solution.py:71
  13.1 0.0 collective-permute-done.other_ref
  13.1 0.1 pair_sum.4.own_ref
  13.1 3.1 %collective-permute-done.2.a_ref = bf16[32,4608]{1,0:T(8,128)(2,1)S(1)} collective-permute-done((bf16[32,4608]{1,0:T(8,128)(2,1)S(1)}, bf16[32,4608]{1,0:T(8,128)(2,1)S(1)}, u32[]{:S(2)}, u32[]{:S(2)}) %collective-permute-start.2) | collective-permute-done | bytes 294944 | tf_op jit(solution)/shard_map/ppermute | solution.py:71
  16.3 3.1 %collective-permute-done.4.b_ref = bf16[32,4608]{1,0:T(8,128)(2,1)S(1)} collective-permute-done((bf16[32,4608]{1,0:T(8,128)(2,1)S(1)}, bf16[32,4608]{1,0:T(8,128)(2,1)S(1)}, u32[]{:S(2)}, u32[]{:S(2)}) %collective-permute-start.4) | collective-permute-done | bytes 294944 | tf_op jit(solution)/shard_map/ppermute | solution.py:71
  19.4 0.0 collective-permute-done.6.c_ref
  19.4 0.1 line_sum.1
  19.6 0.1 reshape.16
  19.6 19.5 %all_to_all.10.arrived_ref = bf16[32,2,2304]{2,1,0:T(2,128)(2,1)S(1)} all-to-all(bf16[32,2,2304]{2,1,0:T(2,128)(2,1)S(1)} %reshape.16), channel_id=1, replica_groups={{0,32,4,36,8,40,12,44,64,96,68,100,72,104,76,108,128,160,132,164,136,16..., dimensions={0} | all-to-all | bytes 589824 | tf_op jit(solution)/shard_map/all_to_all | solution.py:75
  39.1 0.0 copy-done
  39.1 0.0 copy-done.1
  39.1 0.0 copy-done.2
  39.1 0.1 adam.1
  39.3 16.8 %all_to_all.11 = bf16[32,2,2304]{2,1,0:T(2,128)(2,1)S(1)} all-to-all(bf16[32,2,2304]{2,1,0:T(2,128)(2,1)S(1)} %get-tuple-element.19), channel_id=1, replica_groups={{0,32,4,36,8,40,12,44,64,96,68,100,72,104,76,108,128,160,132,164,136,16..., dimensions={0} | all-to-all | bytes 589824 | tf_op jit(solution)/shard_map/all_to_all | solution.py:75
  56.1 1.4 %collective-permute-start.9 = (bf16[32,4608]{1,0:T(8,128)(2,1)S(1)}, bf16[32,4608]{1,0:T(8,128)(2,1)S(1)}, u32[]{:S(2)}, u32[]{:S(2)}) collective-permute-start(bf16[32,4608]{1,0:T(8,128)(2,1)S(1)} %bitcast.13), channel_id=1, source_target_pairs={{0,2},{1,3},{2,0},{3,1},{4,6},{5,7},{6,4},{7,5},{8,10},{9,11},{10,... | collective-permute-start | bytes 884744 | tf_op jit(solution)/shard_map/ppermute | solution.py:71
  57.5 1.1 %collective-permute-start.8 = (bf16[32,4608]{1,0:T(8,128)(2,1)S(1)}, bf16[32,4608]{1,0:T(8,128)(2,1)S(1)}, u32[]{:S(2)}, u32[]{:S(2)}) collective-permute-start(bf16[32,4608]{1,0:T(8,128)(2,1)S(1)} %bitcast.14), channel_id=1, source_target_pairs={{0,1},{1,2},{2,3},{3,0},{4,5},{5,6},{6,7},{7,4},{8,9},{9,10},{10,1... | collective-permute-start | bytes 884744 | tf_op jit(solution)/shard_map/ppermute | solution.py:71
  58.6 1.6 %collective-permute-start.7 = (bf16[32,4608]{1,0:T(8,128)(2,1)S(1)}, bf16[32,4608]{1,0:T(8,128)(2,1)S(1)}, u32[]{:S(2)}, u32[]{:S(2)}) collective-permute-start(bf16[32,4608]{1,0:T(8,128)(2,1)S(1)} %bitcast.15), channel_id=1, source_target_pairs={{0,3},{1,0},{2,1},{3,2},{4,7},{5,4},{6,5},{7,6},{8,11},{9,8},{10,9... | collective-permute-start | bytes 884744 | tf_op jit(solution)/shard_map/ppermute | solution.py:71
  60.2 5.4 %collective-permute-start.10 = (bf16[32,4608]{1,0:T(8,128)(2,1)S(1)}, bf16[32,4608]{1,0:T(8,128)(2,1)S(1)}, u32[]{:S(2)}, u32[]{:S(2)}) collective-permute-start(bf16[32,4608]{1,0:T(8,128)(2,1)S(1)} %bitcast.16), channel_id=1, source_target_pairs={{0,16},{1,17},{2,18},{3,19},{4,20},{5,21},{6,22},{7,23},{8,24},{9,... | collective-permute-start | bytes 884744 | tf_op jit(solution)/shard_map/ppermute | solution.py:67
  65.6 0.0 collective-permute-done.9.d_ref
  65.6 2.2 %collective-permute-start.13 = (bf16[32,4608]{1,0:T(8,128)(2,1)S(1)}, bf16[32,4608]{1,0:T(8,128)(2,1)S(1)}, u32[]{:S(2)}, u32[]{:S(2)}) collective-permute-start(bf16[32,4608]{1,0:T(8,128)(2,1)S(1)} %collective-permute-done.9.d_ref), channel_id=1, source_target_pairs={{0,16},{1,17},{2,18},{3,19},{4,20},{5,21},{6,22},{7,23},{8,24},{9,... | collective-permute-start | bytes 884744 | tf_op jit(solution)/shard_map/ppermute | solution.py:67
  67.8 0.0 collective-permute-done.8.c_ref
  67.8 3.1 %collective-permute-start.12 = (bf16[32,4608]{1,0:T(8,128)(2,1)S(1)}, bf16[32,4608]{1,0:T(8,128)(2,1)S(1)}, u32[]{:S(2)}, u32[]{:S(2)}) collective-permute-start(bf16[32,4608]{1,0:T(8,128)(2,1)S(1)} %collective-permute-done.8.c_ref), channel_id=1, source_target_pairs={{0,16},{1,17},{2,18},{3,19},{4,20},{5,21},{6,22},{7,23},{8,24},{9,... | collective-permute-start | bytes 884744 | tf_op jit(solution)/shard_map/ppermute | solution.py:67
  70.9 0.0 collective-permute-done.7.b_ref
  70.9 0.0 collective-permute-start.11
  70.9 1.3 %restore_own.1 = (bf16[128,9216]{1,0:T(8,128)(2,1)}, f32[1,4608]{1,0:T(1,128)}, f32[1,4608]{1,0:T(1,128)}) custom-call(s32[1]{0:T(128)} %bitcast.place_ref, bf16[32,4608]{1,0:T(8,128)(2,1)S(1)} %bitcast.17, bf16[32,4608]{1,0:T(8,128)(2,1)S(1)} %collective-permute-done.7.b_ref, bf16[32,4608]{1,0:T(8,128)(2,1)S(1)} %collective-permute-done.8.c_ref, ...), custom_call_target="tpu_custom_call" | custom-call | tf_op jit(solution)/shard_map/restore_own/pallas_call | solution.py:249
  72.3 0.0 collective-permute-done.10.a_ref
  72.3 0.0 collective-permute-done.13.d_ref
  72.3 0.0 collective-permute-done.12.c_ref
  72.3 0.3 collective-permute-done.11.b_ref
  72.6 1.3 %restore_other.1 = bf16[128,9216]{1,0:T(8,128)(2,1)} custom-call(s32[1]{0:T(128)} %bitcast.place_ref, bf16[32,4608]{1,0:T(8,128)(2,1)S(1)} %collective-permute-done.10.a_ref, bf16[32,4608]{1,0:T(8,128)(2,1)S(1)} %collective-permute-done.11.b_ref, bf16[32,4608]{1,0:T(8,128)(2,1)S(1)} %collective-permute-done.12.c_ref, ...), custom_call_target="tpu_custom_call", output_to_operand_aliasing={{}: (5, {})} | custom-call | tf_op jit(solution)/shard_map/restore_other/pallas_call | solution.py:267
  (1 shorter events, 0.0 us)
Async XLA Ops:
  4.2 4.5 %collective-permute-start.1 = (bf16[32,4608]{1,0:T(8,128)(2,1)S(1)}, bf16[32,4608]{1,0:T(8,128)(2,1)S(1)}, u32[]{:S(2)}, u32[]{:S(2)}) collective-permute-start(bf16[32,4608]{1,0:T(8,128)(2,1)S(1)} %get-tuple-element.16), channel_id=1, source_target_pairs={{0,16},{1,17},{2,18},{3,19},{4,20},{5,21},{6,22},{7,23},{8,24},{9,... | collective-permute-start | bytes 884744 | tf_op jit(solution)/shard_map/ppermute | solution.py:67
  7.5 2.5 %collective-permute-start.3 = (bf16[32,4608]{1,0:T(8,128)(2,1)S(1)}, bf16[32,4608]{1,0:T(8,128)(2,1)S(1)}, u32[]{:S(2)}, u32[]{:S(2)}) collective-permute-start(bf16[32,4608]{1,0:T(8,128)(2,1)S(1)} %get-tuple-element.17), channel_id=1, source_target_pairs={{0,16},{1,17},{2,18},{3,19},{4,20},{5,21},{6,22},{7,23},{8,24},{9,... | collective-permute-start | bytes 884744 | tf_op jit(solution)/shard_map/ppermute | solution.py:67
  7.6 3.0 %collective-permute-start.5 = (bf16[32,4608]{1,0:T(8,128)(2,1)S(1)}, bf16[32,4608]{1,0:T(8,128)(2,1)S(1)}, u32[]{:S(2)}, u32[]{:S(2)}) collective-permute-start(bf16[32,4608]{1,0:T(8,128)(2,1)S(1)} %get-tuple-element.18), channel_id=1, source_target_pairs={{0,16},{1,17},{2,18},{3,19},{4,20},{5,21},{6,22},{7,23},{8,24},{9,... | collective-permute-start | bytes 884744 | tf_op jit(solution)/shard_map/ppermute | solution.py:67
  8.0 5.1 %collective-permute-start = (bf16[32,4608]{1,0:T(8,128)(2,1)S(1)}, bf16[32,4608]{1,0:T(8,128)(2,1)S(1)}, u32[]{:S(2)}, u32[]{:S(2)}) collective-permute-start(bf16[32,4608]{1,0:T(8,128)(2,1)S(1)} %get-tuple-element.15), channel_id=1, source_target_pairs={{0,16},{1,17},{2,18},{3,19},{4,20},{5,21},{6,22},{7,23},{8,24},{9,... | collective-permute-start | bytes 884744 | tf_op jit(solution)/shard_map/ppermute | solution.py:67
  8.8 7.5 %collective-permute-start.2 = (bf16[32,4608]{1,0:T(8,128)(2,1)S(1)}, bf16[32,4608]{1,0:T(8,128)(2,1)S(1)}, u32[]{:S(2)}, u32[]{:S(2)}) collective-permute-start(bf16[32,4608]{1,0:T(8,128)(2,1)S(1)} %pair_sum.5), channel_id=1, source_target_pairs={{0,2},{1,3},{2,0},{3,1},{4,6},{5,7},{6,4},{7,5},{8,10},{9,11},{10,... | collective-permute-start | bytes 884744 | tf_op jit(solution)/shard_map/ppermute | solution.py:71
  10.1 9.3 %collective-permute-start.4 = (bf16[32,4608]{1,0:T(8,128)(2,1)S(1)}, bf16[32,4608]{1,0:T(8,128)(2,1)S(1)}, u32[]{:S(2)}, u32[]{:S(2)}) collective-permute-start(bf16[32,4608]{1,0:T(8,128)(2,1)S(1)} %pair_sum.6), channel_id=1, source_target_pairs={{0,1},{1,2},{2,3},{3,0},{4,5},{5,6},{6,7},{7,4},{8,9},{9,10},{10,1... | collective-permute-start | bytes 884744 | tf_op jit(solution)/shard_map/ppermute | solution.py:71
  10.7 28.4 %copy-start = (f32[1,1,4608]{2,1,0:T(1,128)S(1)}, f32[1,1,4608]{2,1,0:T(1,128)}, u32[]{:S(2)}) copy-start(f32[1,1,4608]{2,1,0:T(1,128)} %param.9) | copy-start | bytes 55300
  10.7 28.4 %copy-start.1 = (f32[1,1,4608]{2,1,0:T(1,128)S(1)}, f32[1,1,4608]{2,1,0:T(1,128)}, u32[]{:S(2)}) copy-start(f32[1,1,4608]{2,1,0:T(1,128)} %param.10) | copy-start | bytes 55300
  10.7 28.4 %copy-start.2 = (f32[1,1,4608]{2,1,0:T(1,128)S(1)}, f32[1,1,4608]{2,1,0:T(1,128)}, u32[]{:S(2)}) copy-start(f32[1,1,4608]{2,1,0:T(1,128)} %param.11) | copy-start | bytes 55300
  10.7 8.7 %collective-permute-start.6 = (bf16[32,4608]{1,0:T(8,128)(2,1)S(1)}, bf16[32,4608]{1,0:T(8,128)(2,1)S(1)}, u32[]{:S(2)}, u32[]{:S(2)}) collective-permute-start(bf16[32,4608]{1,0:T(8,128)(2,1)S(1)} %pair_sum.7), channel_id=1, source_target_pairs={{0,3},{1,0},{2,1},{3,2},{4,7},{5,4},{6,5},{7,6},{8,11},{9,8},{10,9... | collective-permute-start | bytes 884744 | tf_op jit(solution)/shard_map/ppermute | solution.py:71
  56.1 9.5 %collective-permute-start.9 = (bf16[32,4608]{1,0:T(8,128)(2,1)S(1)}, bf16[32,4608]{1,0:T(8,128)(2,1)S(1)}, u32[]{:S(2)}, u32[]{:S(2)}) collective-permute-start(bf16[32,4608]{1,0:T(8,128)(2,1)S(1)} %bitcast.13), channel_id=1, source_target_pairs={{0,2},{1,3},{2,0},{3,1},{4,6},{5,7},{6,4},{7,5},{8,10},{9,11},{10,... | collective-permute-start | bytes 884744 | tf_op jit(solution)/shard_map/ppermute | solution.py:71
  57.5 10.3 %collective-permute-start.8 = (bf16[32,4608]{1,0:T(8,128)(2,1)S(1)}, bf16[32,4608]{1,0:T(8,128)(2,1)S(1)}, u32[]{:S(2)}, u32[]{:S(2)}) collective-permute-start(bf16[32,4608]{1,0:T(8,128)(2,1)S(1)} %bitcast.14), channel_id=1, source_target_pairs={{0,1},{1,2},{2,3},{3,0},{4,5},{5,6},{6,7},{7,4},{8,9},{9,10},{10,1... | collective-permute-start | bytes 884744 | tf_op jit(solution)/shard_map/ppermute | solution.py:71
  58.6 12.3 %collective-permute-start.7 = (bf16[32,4608]{1,0:T(8,128)(2,1)S(1)}, bf16[32,4608]{1,0:T(8,128)(2,1)S(1)}, u32[]{:S(2)}, u32[]{:S(2)}) collective-permute-start(bf16[32,4608]{1,0:T(8,128)(2,1)S(1)} %bitcast.15), channel_id=1, source_target_pairs={{0,3},{1,0},{2,1},{3,2},{4,7},{5,4},{6,5},{7,6},{8,11},{9,8},{10,9... | collective-permute-start | bytes 884744 | tf_op jit(solution)/shard_map/ppermute | solution.py:71
  60.2 12.1 %collective-permute-start.10 = (bf16[32,4608]{1,0:T(8,128)(2,1)S(1)}, bf16[32,4608]{1,0:T(8,128)(2,1)S(1)}, u32[]{:S(2)}, u32[]{:S(2)}) collective-permute-start(bf16[32,4608]{1,0:T(8,128)(2,1)S(1)} %bitcast.16), channel_id=1, source_target_pairs={{0,16},{1,17},{2,18},{3,19},{4,20},{5,21},{6,22},{7,23},{8,24},{9,... | collective-permute-start | bytes 884744 | tf_op jit(solution)/shard_map/ppermute | solution.py:67
  65.6 6.6 %collective-permute-start.13 = (bf16[32,4608]{1,0:T(8,128)(2,1)S(1)}, bf16[32,4608]{1,0:T(8,128)(2,1)S(1)}, u32[]{:S(2)}, u32[]{:S(2)}) collective-permute-start(bf16[32,4608]{1,0:T(8,128)(2,1)S(1)} %collective-permute-done.9.d_ref), channel_id=1, source_target_pairs={{0,16},{1,17},{2,18},{3,19},{4,20},{5,21},{6,22},{7,23},{8,24},{9,... | collective-permute-start | bytes 884744 | tf_op jit(solution)/shard_map/ppermute | solution.py:67
  67.8 4.4 %collective-permute-start.12 = (bf16[32,4608]{1,0:T(8,128)(2,1)S(1)}, bf16[32,4608]{1,0:T(8,128)(2,1)S(1)}, u32[]{:S(2)}, u32[]{:S(2)}) collective-permute-start(bf16[32,4608]{1,0:T(8,128)(2,1)S(1)} %collective-permute-done.8.c_ref), channel_id=1, source_target_pairs={{0,16},{1,17},{2,18},{3,19},{4,20},{5,21},{6,22},{7,23},{8,24},{9,... | collective-permute-start | bytes 884744 | tf_op jit(solution)/shard_map/ppermute | solution.py:67
  70.9 1.6 %collective-permute-start.11 = (bf16[32,4608]{1,0:T(8,128)(2,1)S(1)}, bf16[32,4608]{1,0:T(8,128)(2,1)S(1)}, u32[]{:S(2)}, u32[]{:S(2)}) collective-permute-start(bf16[32,4608]{1,0:T(8,128)(2,1)S(1)} %collective-permute-done.7.b_ref), channel_id=1, source_target_pairs={{0,16},{1,17},{2,18},{3,19},{4,20},{5,21},{6,22},{7,23},{8,24},{9,... | collective-permute-start | bytes 884744 | tf_op jit(solution)/shard_map/ppermute | solution.py:67

commit v10 on v9

--- a/solution.py
+++ b/solution.py
@@ -117,16 +117,18 @@
             for i in range(CHUNKS):
                 columns = slice(i * CHUNK, (i + 1) * CHUNK)
                 rows = jnp.dot(moved, summed[:, columns], preferred_element_type=F32).astype(BF16)
-                for piece, given_ref in enumerate(given_refs):
-                    given_ref[:, columns] = rows[piece * 32 : (piece + 1) * 32]
+                far_ref, near_ref = given_refs
+                far_ref[:, columns] = rows[64:96]
+                near_ref[0:64, columns] = rows[0:64]
+                near_ref[64:96, columns] = rows[96:128]
 
 
 def compensate(place, codes, scales, feedback):
     return pl.pallas_call(
         compensate_kernel,
-        out_shape=[jax.ShapeDtypeStruct((32, HALF), BF16)] * 4 + [jax.ShapeDtypeStruct((ROWS, HALF), BF16)],
+        out_shape=[jax.ShapeDtypeStruct((rows, HALF), BF16) for rows in (32, 96, ROWS)],
         in_specs=[SCALAR, FAR, FAR, FAR],
-        out_specs=[WHOLE] * 5,
+        out_specs=[WHOLE] * 3,
         scratch_shapes=[
             pltpu.VMEM((2 * CHUNKS, ROWS, CHUNK), jnp.int32),
             pltpu.VMEM((WIDTH // LANES, ROWS), F32),
@@ -160,7 +162,8 @@
 
 def pair_sum_kernel(piece, own_ref, other_ref, out_ref):
     own = own_ref[piece * 32 : (piece + 1) * 32, :].astype(F32)
-    out_ref[...] = (own + other_ref[...].astype(F32)).astype(BF16)
+    low = (0, 32, 0, 64)[piece]
+    out_ref[...] = (own + other_ref[low : low + 32, :].astype(F32)).astype(BF16)
 
 
 def pair_sum(piece, own, other):
@@ -280,8 +283,9 @@
     place = lax.axis_index(AXES).astype(jnp.int32).reshape(1)
     codes, feed = grad_codes[0, 0], feedback[0, 0]
     turned = jnp.swapaxes(scales[0, 0], 0, 1)
-    *given, kept = compensate(place, codes, turned, feed)
-    taken = {piece: swap_cores(given[piece]) for piece in (2, 1, 3, 0)}
+    far, near, kept = compensate(place, codes, turned, feed)
+    far, near = swap_cores(far), swap_cores(near)
+    taken = (near, near, far, near)
     kept = put_in_order(place, kept)
     sums = {piece: pair_sum(piece, kept, taken[piece]) for piece in (2, 1, 3, 0)}
     partial = line_sum(sums[0], [send(sums[step], step) for step in (2, 1, 3)])

time: 74 us -> 75.3 us (1.018)
  waiting for transfers between devices: 6.67 us -> 8.44 us
    ppermute x8 -> x6, waiting for transfers between devices: 0.41 us -> 2.17 us  [swap_cores(): return lax.ppermute(array, AXES, SWAP)]
    ppermute x8 -> x6, starting transfers between devices: 14.7 us -> 14.2 us  [swap_cores(): return lax.ppermute(array, AXES, SWAP)]
  transfers between devices with their start and end apart: 14 -> 12, of which waited for: 4 -> 4; matrix products, arithmetic and copies ran while one was open for 0% -> 0% of each run, Pallas kernels for 3% -> 3%
where the time goes in v10:
time: 75.3 us; the launch traced here: 75.1 us
  blocking collectives  36.3 us (48%)
  starting transfers between devices  22.3 us (30%)
  waiting for transfers between devices  8.44 us (11%)
  Pallas kernels  7.18 us (10%)
  between operations  0.76 us (1%)
    all_to_all x2, blocking collectives, exchange(): lax.all_to_all(array, AXES, 0, 0, axis_index_groups=groups, tiled=True)  36.3 us
    ppermute x6, starting transfers between devices, swap_cores(): return lax.ppermute(array, AXES, SWAP)  14.2 us
    ppermute x6, starting transfers between devices, send(): return lax.ppermute(array, AXES, shifted(step))  8.17 us
    ppermute x6, waiting for transfers between devices, send(): return lax.ppermute(array, AXES, shifted(step))  6.28 us
    pallas_call x1, Pallas kernels, compensate(): pl.pallas_call(compensate_kernel, out_shape=[jax.ShapeDtypeStruct((rows,...  3.52 us
    ppermute x6, waiting for transfers between devices, swap_cores(): return lax.ppermute(array, AXES, SWAP)  2.17 us
  transfers between devices with their start and end apart: 12, of which 4 were waited for; matrix products, arithmetic and copies ran while one was open for 0% of the time, Pallas kernels for 3%

profile of v10, /device:TPU:1, one launch (start us, length us, event | category | flops | bytes accessed | tf_op | source)
XLA Modules:
  0.0 75.1 jit_solution(13633865371968375852)
XLA Ops:
  0.6 3.5 %compensate.1 = (bf16[32,4608]{1,0:T(8,128)(2,1)S(1)}, bf16[96,4608]{1,0:T(8,128)(2,1)S(1)}, bf16[128,4608]{1,0:T(8,128)(2,1)S(1)}) custom-call(s32[1]{0:T(128)} %bitcast.place_ref, s32[128,9216]{1,0:T(8,128)} %bitcast.21, f32[72,128]{1,0:T(8,128)} %bitcast.24, bf16[128,9216]{1,0:T(8,128)(2,1)} %bitcast.22), custom_call_target="tpu_custom_call" | custom-call | tf_op jit(solution)/shard_map/compensate/pallas_call | solution.py:127
  4.2 3.3 %collective-permute-start = (bf16[96,4608]{1,0:T(8,128)(2,1)S(1)}, bf16[96,4608]{1,0:T(8,128)(2,1)S(1)}, u32[]{:S(2)}, u32[]{:S(2)}) collective-permute-start(bf16[96,4608]{1,0:T(8,128)(2,1)S(1)} %get-tuple-element.13), channel_id=1, source_target_pairs={{0,16},{1,17},{2,18},{3,19},{4,20},{5,21},{6,22},{7,23},{8,24},{9,... | collective-permute-start | bytes 2654216 | tf_op jit(solution)/shard_map/ppermute | solution.py:67
  7.5 0.1 collective-permute-start.1
  7.6 0.5 put_in_order.1.own_ref
  8.1 1.9 %collective-permute-done.1.other_ref = bf16[32,4608]{1,0:T(8,128)(2,1)S(1)} collective-permute-done((bf16[32,4608]{1,0:T(8,128)(2,1)S(1)}, bf16[32,4608]{1,0:T(8,128)(2,1)S(1)}, u32[]{:S(2)}, u32[]{:S(2)}) %collective-permute-start.1) | collective-permute-done | bytes 294944 | tf_op jit(solution)/shard_map/ppermute | solution.py:67
  10.0 0.1 pair_sum.5
  10.1 1.3 %collective-permute-start.2 = (bf16[32,4608]{1,0:T(8,128)(2,1)S(1)}, bf16[32,4608]{1,0:T(8,128)(2,1)S(1)}, u32[]{:S(2)}, u32[]{:S(2)}) collective-permute-start(bf16[32,4608]{1,0:T(8,128)(2,1)S(1)} %pair_sum.5), channel_id=1, source_target_pairs={{0,2},{1,3},{2,0},{3,1},{4,6},{5,7},{6,4},{7,5},{8,10},{9,11},{10,... | collective-permute-start | bytes 884744 | tf_op jit(solution)/shard_map/ppermute | solution.py:71
  11.3 0.0 collective-permute-done.other_ref
  11.3 0.1 pair_sum.6
  11.4 0.5 collective-permute-start.3
  11.9 0.1 pair_sum.7
  11.9 0.0 copy-start
  12.0 0.0 copy-start.1
  12.0 0.0 copy-start.2
  12.0 2.4 %collective-permute-start.4 = (bf16[32,4608]{1,0:T(8,128)(2,1)S(1)}, bf16[32,4608]{1,0:T(8,128)(2,1)S(1)}, u32[]{:S(2)}, u32[]{:S(2)}) collective-permute-start(bf16[32,4608]{1,0:T(8,128)(2,1)S(1)} %pair_sum.7), channel_id=1, source_target_pairs={{0,3},{1,0},{2,1},{3,2},{4,7},{5,4},{6,5},{7,6},{8,11},{9,8},{10,9... | collective-permute-start | bytes 884744 | tf_op jit(solution)/shard_map/ppermute | solution.py:71
  14.3 0.1 pair_sum.4.own_ref
  14.4 3.2 %collective-permute-done.2.a_ref = bf16[32,4608]{1,0:T(8,128)(2,1)S(1)} collective-permute-done((bf16[32,4608]{1,0:T(8,128)(2,1)S(1)}, bf16[32,4608]{1,0:T(8,128)(2,1)S(1)}, u32[]{:S(2)}, u32[]{:S(2)}) %collective-permute-start.2) | collective-permute-done | bytes 294944 | tf_op jit(solution)/shard_map/ppermute | solution.py:71
  17.6 3.1 %collective-permute-done.3.b_ref = bf16[32,4608]{1,0:T(8,128)(2,1)S(1)} collective-permute-done((bf16[32,4608]{1,0:T(8,128)(2,1)S(1)}, bf16[32,4608]{1,0:T(8,128)(2,1)S(1)}, u32[]{:S(2)}, u32[]{:S(2)}) %collective-permute-start.3) | collective-permute-done | bytes 294944 | tf_op jit(solution)/shard_map/ppermute | solution.py:71
  20.7 0.0 collective-permute-done.4.c_ref
  20.7 0.1 line_sum.1
  20.8 0.1 reshape.16
  20.9 19.5 %all_to_all.10.arrived_ref = bf16[32,2,2304]{2,1,0:T(2,128)(2,1)S(1)} all-to-all(bf16[32,2,2304]{2,1,0:T(2,128)(2,1)S(1)} %reshape.16), channel_id=1, replica_groups={{0,32,4,36,8,40,12,44,64,96,68,100,72,104,76,108,128,160,132,164,136,16..., dimensions={0} | all-to-all | bytes 589824 | tf_op jit(solution)/shard_map/all_to_all | solution.py:75
  40.4 0.0 copy-done
  40.4 0.0 copy-done.1
  40.4 0.0 copy-done.2
  40.4 0.1 adam.1
  40.6 16.8 %all_to_all.11 = bf16[32,2,2304]{2,1,0:T(2,128)(2,1)S(1)} all-to-all(bf16[32,2,2304]{2,1,0:T(2,128)(2,1)S(1)} %get-tuple-element.15), channel_id=1, replica_groups={{0,32,4,36,8,40,12,44,64,96,68,100,72,104,76,108,128,160,132,164,136,16..., dimensions={0} | all-to-all | bytes 589824 | tf_op jit(solution)/shard_map/all_to_all | solution.py:75
  57.4 1.4 %collective-permute-start.7 = (bf16[32,4608]{1,0:T(8,128)(2,1)S(1)}, bf16[32,4608]{1,0:T(8,128)(2,1)S(1)}, u32[]{:S(2)}, u32[]{:S(2)}) collective-permute-start(bf16[32,4608]{1,0:T(8,128)(2,1)S(1)} %bitcast.13), channel_id=1, source_target_pairs={{0,2},{1,3},{2,0},{3,1},{4,6},{5,7},{6,4},{7,5},{8,10},{9,11},{10,... | collective-permute-start | bytes 884744 | tf_op jit(solution)/shard_map/ppermute | solution.py:71
  58.8 1.1 %collective-permute-start.6 = (bf16[32,4608]{1,0:T(8,128)(2,1)S(1)}, bf16[32,4608]{1,0:T(8,128)(2,1)S(1)}, u32[]{:S(2)}, u32[]{:S(2)}) collective-permute-start(bf16[32,4608]{1,0:T(8,128)(2,1)S(1)} %bitcast.14), channel_id=1, source_target_pairs={{0,1},{1,2},{2,3},{3,0},{4,5},{5,6},{6,7},{7,4},{8,9},{9,10},{10,1... | collective-permute-start | bytes 884744 | tf_op jit(solution)/shard_map/ppermute | solution.py:71
  59.9 1.6 %collective-permute-start.5 = (bf16[32,4608]{1,0:T(8,128)(2,1)S(1)}, bf16[32,4608]{1,0:T(8,128)(2,1)S(1)}, u32[]{:S(2)}, u32[]{:S(2)}) collective-permute-start(bf16[32,4608]{1,0:T(8,128)(2,1)S(1)} %bitcast.15), channel_id=1, source_target_pairs={{0,3},{1,0},{2,1},{3,2},{4,7},{5,4},{6,5},{7,6},{8,11},{9,8},{10,9... | collective-permute-start | bytes 884744 | tf_op jit(solution)/shard_map/ppermute | solution.py:71
  61.5 5.4 %collective-permute-start.8 = (bf16[32,4608]{1,0:T(8,128)(2,1)S(1)}, bf16[32,4608]{1,0:T(8,128)(2,1)S(1)}, u32[]{:S(2)}, u32[]{:S(2)}) collective-permute-start(bf16[32,4608]{1,0:T(8,128)(2,1)S(1)} %bitcast.16), channel_id=1, source_target_pairs={{0,16},{1,17},{2,18},{3,19},{4,20},{5,21},{6,22},{7,23},{8,24},{9,... | collective-permute-start | bytes 884744 | tf_op jit(solution)/shard_map/ppermute | solution.py:67
  66.9 0.0 collective-permute-done.7.d_ref
  66.9 2.2 %collective-permute-start.11 = (bf16[32,4608]{1,0:T(8,128)(2,1)S(1)}, bf16[32,4608]{1,0:T(8,128)(2,1)S(1)}, u32[]{:S(2)}, u32[]{:S(2)}) collective-permute-start(bf16[32,4608]{1,0:T(8,128)(2,1)S(1)} %collective-permute-done.7.d_ref), channel_id=1, source_target_pairs={{0,16},{1,17},{2,18},{3,19},{4,20},{5,21},{6,22},{7,23},{8,24},{9,... | collective-permute-start | bytes 884744 | tf_op jit(solution)/shard_map/ppermute | solution.py:67
  69.1 0.0 collective-permute-done.6.c_ref
  69.1 3.1 %collective-permute-start.10 = (bf16[32,4608]{1,0:T(8,128)(2,1)S(1)}, bf16[32,4608]{1,0:T(8,128)(2,1)S(1)}, u32[]{:S(2)}, u32[]{:S(2)}) collective-permute-start(bf16[32,4608]{1,0:T(8,128)(2,1)S(1)} %collective-permute-done.6.c_ref), channel_id=1, source_target_pairs={{0,16},{1,17},{2,18},{3,19},{4,20},{5,21},{6,22},{7,23},{8,24},{9,... | collective-permute-start | bytes 884744 | tf_op jit(solution)/shard_map/ppermute | solution.py:67
  72.2 0.0 collective-permute-done.5.b_ref
  72.2 0.0 collective-permute-start.9
  72.2 1.3 %restore_own.1 = (bf16[128,9216]{1,0:T(8,128)(2,1)}, f32[1,4608]{1,0:T(1,128)}, f32[1,4608]{1,0:T(1,128)}) custom-call(s32[1]{0:T(128)} %bitcast.place_ref, bf16[32,4608]{1,0:T(8,128)(2,1)S(1)} %bitcast.17, bf16[32,4608]{1,0:T(8,128)(2,1)S(1)} %collective-permute-done.5.b_ref, bf16[32,4608]{1,0:T(8,128)(2,1)S(1)} %collective-permute-done.6.c_ref, ...), custom_call_target="tpu_custom_call" | custom-call | tf_op jit(solution)/shard_map/restore_own/pallas_call | solution.py:252
  73.5 0.0 collective-permute-done.8.a_ref
  73.5 0.0 collective-permute-done.11.d_ref
  73.5 0.0 collective-permute-done.10.c_ref
  73.6 0.3 collective-permute-done.9.b_ref
  73.8 1.3 %restore_other.1 = bf16[128,9216]{1,0:T(8,128)(2,1)} custom-call(s32[1]{0:T(128)} %bitcast.place_ref, bf16[32,4608]{1,0:T(8,128)(2,1)S(1)} %collective-permute-done.8.a_ref, bf16[32,4608]{1,0:T(8,128)(2,1)S(1)} %collective-permute-done.9.b_ref, bf16[32,4608]{1,0:T(8,128)(2,1)S(1)} %collective-permute-done.10.c_ref, ...), custom_call_target="tpu_custom_call", output_to_operand_aliasing={{}: (5, {})} | custom-call | tf_op jit(solution)/shard_map/restore_other/pallas_call | solution.py:270
  (1 shorter events, 0.0 us)
Async XLA Ops:
  4.2 7.2 %collective-permute-start = (bf16[96,4608]{1,0:T(8,128)(2,1)S(1)}, bf16[96,4608]{1,0:T(8,128)(2,1)S(1)}, u32[]{:S(2)}, u32[]{:S(2)}) collective-permute-start(bf16[96,4608]{1,0:T(8,128)(2,1)S(1)} %get-tuple-element.13), channel_id=1, source_target_pairs={{0,16},{1,17},{2,18},{3,19},{4,20},{5,21},{6,22},{7,23},{8,24},{9,... | collective-permute-start | bytes 2654216 | tf_op jit(solution)/shard_map/ppermute | solution.py:67
  7.5 2.5 %collective-permute-start.1 = (bf16[32,4608]{1,0:T(8,128)(2,1)S(1)}, bf16[32,4608]{1,0:T(8,128)(2,1)S(1)}, u32[]{:S(2)}, u32[]{:S(2)}) collective-permute-start(bf16[32,4608]{1,0:T(8,128)(2,1)S(1)} %get-tuple-element.14), channel_id=1, source_target_pairs={{0,16},{1,17},{2,18},{3,19},{4,20},{5,21},{6,22},{7,23},{8,24},{9,... | collective-permute-start | bytes 884744 | tf_op jit(solution)/shard_map/ppermute | solution.py:67
  10.1 7.5 %collective-permute-start.2 = (bf16[32,4608]{1,0:T(8,128)(2,1)S(1)}, bf16[32,4608]{1,0:T(8,128)(2,1)S(1)}, u32[]{:S(2)}, u32[]{:S(2)}) collective-permute-start(bf16[32,4608]{1,0:T(8,128)(2,1)S(1)} %pair_sum.5), channel_id=1, source_target_pairs={{0,2},{1,3},{2,0},{3,1},{4,6},{5,7},{6,4},{7,5},{8,10},{9,11},{10,... | collective-permute-start | bytes 884744 | tf_op jit(solution)/shard_map/ppermute | solution.py:71
  11.4 9.3 %collective-permute-start.3 = (bf16[32,4608]{1,0:T(8,128)(2,1)S(1)}, bf16[32,4608]{1,0:T(8,128)(2,1)S(1)}, u32[]{:S(2)}, u32[]{:S(2)}) collective-permute-start(bf16[32,4608]{1,0:T(8,128)(2,1)S(1)} %pair_sum.6), channel_id=1, source_target_pairs={{0,1},{1,2},{2,3},{3,0},{4,5},{5,6},{6,7},{7,4},{8,9},{9,10},{10,1... | collective-permute-start | bytes 884744 | tf_op jit(solution)/shard_map/ppermute | solution.py:71
  11.9 28.5 %copy-start = (f32[1,1,4608]{2,1,0:T(1,128)S(1)}, f32[1,1,4608]{2,1,0:T(1,128)}, u32[]{:S(2)}) copy-start(f32[1,1,4608]{2,1,0:T(1,128)} %param.9) | copy-start | bytes 55300
  12.0 28.4 %copy-start.1 = (f32[1,1,4608]{2,1,0:T(1,128)S(1)}, f32[1,1,4608]{2,1,0:T(1,128)}, u32[]{:S(2)}) copy-start(f32[1,1,4608]{2,1,0:T(1,128)} %param.10) | copy-start | bytes 55300
  12.0 28.4 %copy-start.2 = (f32[1,1,4608]{2,1,0:T(1,128)S(1)}, f32[1,1,4608]{2,1,0:T(1,128)}, u32[]{:S(2)}) copy-start(f32[1,1,4608]{2,1,0:T(1,128)} %param.11) | copy-start | bytes 55300
  12.0 8.7 %collective-permute-start.4 = (bf16[32,4608]{1,0:T(8,128)(2,1)S(1)}, bf16[32,4608]{1,0:T(8,128)(2,1)S(1)}, u32[]{:S(2)}, u32[]{:S(2)}) collective-permute-start(bf16[32,4608]{1,0:T(8,128)(2,1)S(1)} %pair_sum.7), channel_id=1, source_target_pairs={{0,3},{1,0},{2,1},{3,2},{4,7},{5,4},{6,5},{7,6},{8,11},{9,8},{10,9... | collective-permute-start | bytes 884744 | tf_op jit(solution)/shard_map/ppermute | solution.py:71
  57.4 9.5 %collective-permute-start.7 = (bf16[32,4608]{1,0:T(8,128)(2,1)S(1)}, bf16[32,4608]{1,0:T(8,128)(2,1)S(1)}, u32[]{:S(2)}, u32[]{:S(2)}) collective-permute-start(bf16[32,4608]{1,0:T(8,128)(2,1)S(1)} %bitcast.13), channel_id=1, source_target_pairs={{0,2},{1,3},{2,0},{3,1},{4,6},{5,7},{6,4},{7,5},{8,10},{9,11},{10,... | collective-permute-start | bytes 884744 | tf_op jit(solution)/shard_map/ppermute | solution.py:71
  58.8 10.3 %collective-permute-start.6 = (bf16[32,4608]{1,0:T(8,128)(2,1)S(1)}, bf16[32,4608]{1,0:T(8,128)(2,1)S(1)}, u32[]{:S(2)}, u32[]{:S(2)}) collective-permute-start(bf16[32,4608]{1,0:T(8,128)(2,1)S(1)} %bitcast.14), channel_id=1, source_target_pairs={{0,1},{1,2},{2,3},{3,0},{4,5},{5,6},{6,7},{7,4},{8,9},{9,10},{10,1... | collective-permute-start | bytes 884744 | tf_op jit(solution)/shard_map/ppermute | solution.py:71
  59.9 12.3 %collective-permute-start.5 = (bf16[32,4608]{1,0:T(8,128)(2,1)S(1)}, bf16[32,4608]{1,0:T(8,128)(2,1)S(1)}, u32[]{:S(2)}, u32[]{:S(2)}) collective-permute-start(bf16[32,4608]{1,0:T(8,128)(2,1)S(1)} %bitcast.15), channel_id=1, source_target_pairs={{0,3},{1,0},{2,1},{3,2},{4,7},{5,4},{6,5},{7,6},{8,11},{9,8},{10,9... | collective-permute-start | bytes 884744 | tf_op jit(solution)/shard_map/ppermute | solution.py:71
  61.5 12.1 %collective-permute-start.8 = (bf16[32,4608]{1,0:T(8,128)(2,1)S(1)}, bf16[32,4608]{1,0:T(8,128)(2,1)S(1)}, u32[]{:S(2)}, u32[]{:S(2)}) collective-permute-start(bf16[32,4608]{1,0:T(8,128)(2,1)S(1)} %bitcast.16), channel_id=1, source_target_pairs={{0,16},{1,17},{2,18},{3,19},{4,20},{5,21},{6,22},{7,23},{8,24},{9,... | collective-permute-start | bytes 884744 | tf_op jit(solution)/shard_map/ppermute | solution.py:67
  66.9 6.6 %collective-permute-start.11 = (bf16[32,4608]{1,0:T(8,128)(2,1)S(1)}, bf16[32,4608]{1,0:T(8,128)(2,1)S(1)}, u32[]{:S(2)}, u32[]{:S(2)}) collective-permute-start(bf16[32,4608]{1,0:T(8,128)(2,1)S(1)} %collective-permute-done.7.d_ref), channel_id=1, source_target_pairs={{0,16},{1,17},{2,18},{3,19},{4,20},{5,21},{6,22},{7,23},{8,24},{9,... | collective-permute-start | bytes 884744 | tf_op jit(solution)/shard_map/ppermute | solution.py:67
  69.1 4.4 %collective-permute-start.10 = (bf16[32,4608]{1,0:T(8,128)(2,1)S(1)}, bf16[32,4608]{1,0:T(8,128)(2,1)S(1)}, u32[]{:S(2)}, u32[]{:S(2)}) collective-permute-start(bf16[32,4608]{1,0:T(8,128)(2,1)S(1)} %collective-permute-done.6.c_ref), channel_id=1, source_target_pairs={{0,16},{1,17},{2,18},{3,19},{4,20},{5,21},{6,22},{7,23},{8,24},{9,... | collective-permute-start | bytes 884744 | tf_op jit(solution)/shard_map/ppermute | solution.py:67
  72.2 1.6 %collective-permute-start.9 = (bf16[32,4608]{1,0:T(8,128)(2,1)S(1)}, bf16[32,4608]{1,0:T(8,128)(2,1)S(1)}, u32[]{:S(2)}, u32[]{:S(2)}) collective-permute-start(bf16[32,4608]{1,0:T(8,128)(2,1)S(1)} %collective-permute-done.5.b_ref), channel_id=1, source_target_pairs={{0,16},{1,17},{2,18},{3,19},{4,20},{5,21},{6,22},{7,23},{8,24},{9,... | collective-permute-start | bytes 884744 | tf_op jit(solution)/shard_map/ppermute | solution.py:67
